TPU v7x, 256 devices: a whole 4x4x8 slice. The times are simulated.
256 devices in a mesh: dp: 16 (over z_hi, x, core), mp: 16 (over z_lo, y).
Axes of the slice: x: 4, y: 4, z: 8 (z_hi: 2, z_lo: 4; z = z_hi * 4 + z_lo), core: 2. Of those that a mesh axis runs over, the one named last changes fastest.
Arguments:
- acts: bfloat16 [2048, 8192], P('dp', 'mp'), may hold values from -6 to 6
- grad_out: bfloat16 [2048, 14336], P('dp', 'mp'), may hold values from -6 to 6
- values: bfloat16 [112, 20, 128, 128], P('mp', None, 'dp'), may hold values from -0.125 to 0.125
- block_rows: int32 [112, 20], P('mp'), may hold values from 0 to 63, as said below
- block_count: int32 [112], P('mp'), may hold values from 12 to 20, as said below
Outputs:
- hidden_out: bfloat16 [2048, 14336], P('dp', 'mp')
- grad_acts: bfloat16 [2048, 8192], P('dp', 'mp')
- grad_values: float32 [112, 20, 128, 128], P('mp', None, 'dp')
Inputs may be any that keep to these rules, and one draw needn't show every extreme that they name: `block_rows`: the live slots of a block column name distinct block rows; the first ones follow a butterfly pattern around block row c % 64. Slots at or after block_count are ignored. `block_count`: some block column has all 20 slots live.
All inputs are finite; a program needn't handle non-finite values.
Results may differ from a plain program's by a relative error of at most 0.02.
Values may be sent and summed in bfloat16 or wider, within the bound.
No kernel may reach another device: no remote copies, remote signals or barrier semaphores. Data moves between devices by JAX's collectives and lax.ppermute only.
A program may use at most 128 MiB of HBM per device.

v0:
```python
import jax
import jax.numpy as jnp
from jax import lax
from jax.sharding import PartitionSpec as P


def shards(acts, grad_out, values, block_rows, block_count):
    tok_rows = acts.shape[0]
    col_blocks = values.shape[0]
    slot_count = values.shape[1]
    block_size = values.shape[3]
    whole = lax.all_gather(acts, "mp", axis=1, tiled=True)
    row_blocks = whole.shape[1] // block_size
    blocked = whole.reshape(tok_rows, row_blocks, block_size)
    weights_all = lax.all_gather(values, "dp", axis=2, tiled=True)
    slot_live = jnp.arange(slot_count, dtype=jnp.int32)[None, :] < block_count[:, None]
    masked = jnp.where(slot_live[:, :, None, None], weights_all, jnp.zeros((), jnp.bfloat16))
    grad_blocks = grad_out.reshape(tok_rows, col_blocks, block_size)
    outputs = []
    local_grads = []
    partial_value = jnp.zeros((tok_rows, row_blocks, block_size), jnp.float32)
    for column in range(col_blocks):
        picked = jnp.take(blocked, block_rows[column], axis=1)
        upstream = grad_blocks[:, column]
        outputs.append(
            jnp.einsum("tki,kij->tj", picked, masked[column], preferred_element_type=jnp.float32)
        )
        contrib = jnp.einsum(
            "tj,kij->tki", upstream, masked[column], preferred_element_type=jnp.float32
        )
        partial_value = partial_value.at[:, block_rows[column]].add(contrib)
        local_grads.append(
            jnp.einsum("tki,tj->kij", picked, upstream, preferred_element_type=jnp.float32)
        )
    hidden_out = jnp.concatenate(outputs, axis=1).astype(jnp.bfloat16)
    rounded_partial = partial_value.reshape(tok_rows, row_blocks * block_size).astype(jnp.bfloat16)
    grad_acts = (
        lax.psum_scatter(rounded_partial, "mp", scatter_dimension=1, tiled=True)
        .astype(jnp.float32)
        .astype(jnp.bfloat16)
    )
    stacked = jnp.stack(local_grads)
    stacked = jnp.where(slot_live[:, :, None, None], stacked, jnp.zeros((), jnp.float32))
    grad_values = lax.psum_scatter(
        stacked.astype(jnp.bfloat16), "dp", scatter_dimension=2, tiled=True
    ).astype(jnp.float32)
    return (hidden_out, grad_acts, grad_values)


def solution(mesh):
    placed = (P("dp", "mp"), P("dp", "mp"), P("mp", None, "dp", None), P("mp", None), P("mp"))
    return jax.shard_map(
        shards,
        mesh=mesh,
        in_specs=placed,
        out_specs=(P("dp", "mp"), P("dp", "mp"), P("mp", None, "dp", None)),
        check_vma=False,
    )
```

profile of v0, /device:TPU:24, one launch (start us, length us, event | category | flops | bytes accessed | tf_op | source)
XLA Modules:
  0.0 478.1 jit_solution(14113657356584369845)
XLA Ops:
  7.2 1.7 copy.129
  13.5 78.1 %all-gather.3.cloned.1.call-done = bf16[128,8192]{0,1:T(8,128)(2,1)} async-done(((bf16[128,512]{0,1:T(8,128)(2,1)}), bf16[128,8192]{0,1:T(8,128)(2,1)}) %all-gather.3.cloned.1.call-update) | async-done | bytes 2097168 | tf_op jit(solution)/shard_map/all_gather | solution.py:12
  91.6 3.2 copy.130
  94.8 1.5 gather_fusion
  96.3 1.5 gather_fusion.1
  97.8 1.5 gather_fusion.2
  99.4 1.5 gather_fusion.3
  100.9 1.5 gather_fusion.4
  102.4 1.5 gather_fusion.5
  104.6 2.5 fusion.6
  107.1 2.4 fusion.5
  109.5 2.4 fusion.4
  111.9 2.4 fusion.3
  118.0 59.6 %all-gather.5.cloned.1.call-done = bf16[7,20,128,128]{3,2,1,0:T(8,128)(2,1)} async-done(((bf16[7,20,8,128]{3,2,1,0:T(8,128)(2,1)}), bf16[7,20,128,128]{3,2,1,0:T(8,128)(2,1)}) %all-gather.5.cloned.1.call-update) | async-done | bytes 4587536 | tf_op jit(solution)/shard_map/all_gather | solution.py:15
  177.7 7.2 %copy.131 = bf16[7,20,128,128]{2,3,1,0:T(8,128)(2,1)} copy(bf16[7,20,128,128]{3,2,1,0:T(8,128)(2,1)} %all-gather.5.cloned.1.call-done) | data formatting | bytes 9175040 | tf_op jit(solution)/shard_map/all_gather | solution.py:15
  184.9 6.9 %select_convert_fusion = (bf16[7,20,128,128]{2,3,1,0:T(8,128)(2,1)}, bf16[7,20,128,128]{2,3,1,0:T(8,128)(2,1)S(1)}) fusion(bf16[7,20,128,128]{2,3,1,0:T(8,128)(2,1)} %fusion, pred[7,20]{1,0:T(8,128)(4,1)S(1)} %iota_compare_fusion, bf16[7,20,128,128]{2,3,1,0:T(8,128)(2,1)} %copy.131), kind=kLoop, calls=%fused_computation.14 | loop fusion | flops 4587520 | bytes 18350220 | tf_op jit(solution)/shard_map/convert_element_type | solution.py:45
  191.8 1.7 convolution_bitcast_fusion.13
  193.5 1.4 convolution_bitcast_fusion.12
  196.4 1.4 convolution_bitcast_fusion.10
  198.6 1.4 convolution_bitcast_fusion.7
  200.0 2.8 copy.141
  202.8 2.8 copy.144
  205.6 2.8 copy.147
  208.4 2.8 copy.150
  211.2 1.5 copy.153
  213.1 1.7 copy.159
  214.8 2.4 broadcast_in_dim.47
  217.3 7.3 %scatter_fusion = f32[128,64,128]{2,0,1:T(8,128)} fusion(f32[128,64,128]{2,0,1:T(8,128)} %broadcast_in_dim.47, s32[20]{0:T(128)S(1)} %get-tuple-element.31, f32[20,128,128]{2,1,0:T(8,128)} %copy.141), kind=kCustom, calls=%fused_computation.7 | custom fusion | flops 327680 | bytes 3932240 | tf_op jit(solution)/shard_map/scatter-add | solution.py:31
  224.6 7.2 %scatter_fusion.1 = f32[128,64,128]{2,0,1:T(8,128)} fusion(f32[128,64,128]{2,0,1:T(8,128)} %scatter_fusion, s32[20]{0:T(128)S(1)} %get-tuple-element.32, f32[20,128,128]{2,1,0:T(8,128)} %copy.144), kind=kCustom, calls=%fused_computation.8 | custom fusion | flops 327680 | bytes 3932240 | tf_op jit(solution)/shard_map/scatter-add | solution.py:31
  231.8 7.4 %scatter_fusion.2 = f32[128,64,128]{2,0,1:T(8,128)} fusion(f32[128,64,128]{2,0,1:T(8,128)} %scatter_fusion.1, s32[20]{0:T(128)S(1)} %get-tuple-element.33, f32[20,128,128]{2,1,0:T(8,128)} %copy.147), kind=kCustom, calls=%fused_computation.9 | custom fusion | flops 327680 | bytes 3932240 | tf_op jit(solution)/shard_map/scatter-add | solution.py:31
  239.2 7.3 %scatter_fusion.3 = f32[128,64,128]{2,0,1:T(8,128)} fusion(f32[128,64,128]{2,0,1:T(8,128)} %scatter_fusion.2, s32[20]{0:T(128)S(1)} %get-tuple-element.34, f32[20,128,128]{2,1,0:T(8,128)} %copy.150), kind=kCustom, calls=%fused_computation.10 | custom fusion | flops 327680 | bytes 3932240 | tf_op jit(solution)/shard_map/scatter-add | solution.py:31
  246.5 7.2 %scatter_fusion.4 = f32[128,64,128]{2,0,1:T(8,128)} fusion(f32[128,64,128]{2,0,1:T(8,128)} %scatter_fusion.3, s32[20]{0:T(128)S(1)} %get-tuple-element.35, f32[20,128,128]{2,1,0:T(8,128)} %copy.153), kind=kCustom, calls=%fused_computation.11 | custom fusion | flops 327680 | bytes 3932240 | tf_op jit(solution)/shard_map/scatter-add | solution.py:31
  253.7 6.8 %scatter_fusion.5 = f32[128,64,128]{2,0,1:T(8,128)} fusion(f32[128,64,128]{2,0,1:T(8,128)} %scatter_fusion.4, s32[20]{0:T(128)S(1)} %get-tuple-element.36, f32[20,128,128]{2,1,0:T(8,128)S(1)} %copy.156), kind=kCustom, calls=%fused_computation.12 | custom fusion | flops 327680 | bytes 3932240 | tf_op jit(solution)/shard_map/scatter-add | solution.py:31
  260.5 6.7 %scatter_fusion.6 = f32[128,64,128]{2,0,1:T(8,128)} fusion(f32[128,64,128]{2,0,1:T(8,128)} %scatter_fusion.5, s32[20]{0:T(128)S(1)} %get-tuple-element.30, f32[20,128,128]{2,1,0:T(8,128)S(1)} %copy.159), kind=kCustom, calls=%fused_computation.13 | custom fusion | flops 327680 | bytes 3932240 | tf_op jit(solution)/shard_map/scatter-add | solution.py:31
  267.2 2.6 convert_element_type.15
  269.7 2.9 copy.160
  272.7 8.0 %copy.175 = bf16[7,20,128,128]{3,0,1,2:T(8,128)(2,1)} copy(bf16[7,20,128,128]{2,3,1,0:T(8,128)(2,1)} %get-tuple-element.49) | data formatting | bytes 9175040 | tf_op jit(solution)/shard_map/convert_element_type | solution.py:45
  281.8 1.6 fusion.8
  283.5 1.6 fusion.10
  285.1 1.5 fusion.12
  286.6 1.5 fusion.14
  288.1 1.5 fusion.16
  289.7 1.5 fusion.18
  291.2 1.5 fusion.20
  293.6 54.6 %reduce-scatter.3.cloned.1.call-done = bf16[128,512]{0,1:T(8,128)(2,1)} async-done(((bf16[128,8192]{0,1:T(8,128)(2,1)}), bf16[128,512]{0,1:T(8,128)(2,1)}) %reduce-scatter.3.cloned.1.call-update) | async-done | bytes 131088 | tf_op jit(solution)/shard_map/reduce_scatter | solution.py:38
  348.2 1.7 copy.177
  349.8 119.9 %reduce-scatter.5.cloned.1.call-done = bf16[7,20,8,128]{3,0,1,2:T(8,128)(2,1)} async-done(((bf16[7,20,128,128]{3,0,1,2:T(8,128)(2,1)}), bf16[7,20,8,128]{3,0,1,2:T(8,128)(2,1)}) %reduce-scatter.5.cloned.1.call-update) | async-done | bytes 286736 | tf_op jit(solution)/shard_map/reduce_scatter | solution.py:44
  469.7 1.9 copy.178
  (51 shorter events, 13.6 us)
Async XLA Ops:
  7.2 84.4 %all-gather.3.cloned.1.call-start = ((), (), s32[]{:S(2)}) async-start(), calls=%async_computation.2 | async-start | bytes 2228224 | tf_op jit(solution)/shard_map/all_gather | solution.py:12
  8.9 168.8 %all-gather.5.cloned.1.call-start = ((), (), s32[]{:S(2)}) async-start(), calls=%async_computation.3 | async-start | bytes 4874240 | tf_op jit(solution)/shard_map/all_gather | solution.py:15
  9.7 338.5 %reduce-scatter.3.cloned.1.call-start = ((), (), s32[]{:S(2)}) async-start(), calls=%async_computation.4 | async-start | bytes 2228224 | tf_op jit(solution)/shard_map/reduce_scatter | solution.py:38
  11.8 92.8 %copy-start.11 = (pred[20]{0:T(512)(128)(4,1)}, pred[20]{0:T(512)(128)(4,1)S(1)}, u32[]{:S(2)}) copy-start(pred[20]{0:T(512)(128)(4,1)S(1)} %get-tuple-element.45) | copy-start | bytes 64
  11.8 95.3 %copy-start.9 = (pred[20]{0:T(512)(128)(4,1)}, pred[20]{0:T(512)(128)(4,1)S(1)}, u32[]{:S(2)}) copy-start(pred[20]{0:T(512)(128)(4,1)S(1)} %get-tuple-element.43) | copy-start | bytes 64
  104.6 9.7 %copy-start.3 = (bf16[20,128,128]{2,1,0:T(8,128)(2,1)S(1)}, bf16[20,128,128]{2,1,0:T(8,128)(2,1)}, u32[]{:S(2)}) copy-start(bf16[20,128,128]{2,1,0:T(8,128)(2,1)} %gather_fusion.4) | copy-start | bytes 1966084
  107.1 8.5 %copy-start.1 = (bf16[20,128,128]{2,1,0:T(8,128)(2,1)S(1)}, bf16[20,128,128]{2,1,0:T(8,128)(2,1)}, u32[]{:S(2)}) copy-start(bf16[20,128,128]{2,1,0:T(8,128)(2,1)} %gather_fusion.5) | copy-start | bytes 1966084
  191.8 6.8 %copy-start = (bf16[7,20,128,128]{2,3,1,0:T(8,128)(2,1)}, bf16[7,20,128,128]{2,3,1,0:T(8,128)(2,1)S(1)}, u32[]{:S(2)}) copy-start(bf16[7,20,128,128]{2,3,1,0:T(8,128)(2,1)S(1)} %get-tuple-element.50) | copy-start | bytes 13762564
  272.7 197.0 %reduce-scatter.5.cloned.1.call-start = ((), (), s32[]{:S(2)}) async-start(), calls=%async_computation.5 | async-start | bytes 5570560 | tf_op jit(solution)/shard_map/reduce_scatter | solution.py:44
  280.7 1.1 copy-start.8
  280.7 1.1 copy-start.12
  280.7 2.7 copy-start.7
  280.7 2.7 copy-start.10
  280.7 4.3 copy-start.6
  281.8 4.8 copy-start.5
  281.8 6.3 %copy-start.4 = (bf16[20,128,128]{2,1,0:T(8,128)(2,1)S(1)}, bf16[20,128,128]{2,1,0:T(8,128)(2,1)}, u32[]{:S(2)}) copy-start(bf16[20,128,128]{2,1,0:T(8,128)(2,1)} %gather_fusion.4) | copy-start | bytes 1966084
  283.5 6.2 %copy-start.2 = (bf16[20,128,128]{2,1,0:T(8,128)(2,1)S(1)}, bf16[20,128,128]{2,1,0:T(8,128)(2,1)}, u32[]{:S(2)}) copy-start(bf16[20,128,128]{2,1,0:T(8,128)(2,1)} %gather_fusion.5) | copy-start | bytes 1966084
Sparse Core Ops, SparseCore 0:
  10.4 81.1 all-gather.2
  94.2 83.4 all-gather.4
  272.8 75.3 reduce-scatter.2
  352.4 117.2 reduce-scatter.4
where the time goes:
time: 480 us; the launch traced here: 478 us
  waiting for transfers between devices  313 us (65%)
  other arithmetic  62 us (13%)
  local copies, waits for them, and re-layouts  56.6 us (12%)
  matrix products  32.4 us (7%)
  between operations  14 us (3%)
    reduce_scatter x1, waiting for transfers between devices, shards(): lax.psum_scatter(stacked.astype(jnp.bfloat16), 'dp', scatter_dimension=2,...  120 us
    all_gather x1, waiting for transfers between devices, shards(): whole = lax.all_gather(acts, 'mp', axis=1, tiled=True)  78.1 us
    all_gather x1, waiting for transfers between devices, shards(): weights_all = lax.all_gather(values, 'dp', axis=2, tiled=True)  59.6 us
    reduce_scatter x1, waiting for transfers between devices, shards(): lax.psum_scatter(rounded_partial, 'mp', scatter_dimension=1, tiled=True)  54.6 us
    scatter-add x7, other arithmetic, shards(): partial_value = partial_value.at[:, block_rows[column]].add(contrib)  49.9 us
    dot_general x7, local copies, waits for them, and re-layouts, shards(): jnp.einsum('tj,kij->tki', upstream, masked[column], preferred_element_typ...  14.8 us
    dot_general x7, matrix products, shards(): jnp.einsum('tki,tj->kij', picked, upstream, preferred_element_type=jnp.fl...  13.4 us
    dot_general x7, matrix products, shards(): jnp.einsum('tki,kij->tj', picked, masked[column], preferred_element_type=...  10.8 us
  transfers between devices with their start and end apart: 4, of which 4 were waited for; matrix products, arithmetic and copies ran while one was open for 11% of the time, Pallas kernels for 0%

commit v1 on v0

v1 whole, which is shorter than its diff:
```python
import functools

import jax
import jax.numpy as jnp
from jax import lax
from jax.experimental import pallas as pl
from jax.experimental.pallas import tpu as pltpu
from jax.sharding import PartitionSpec as P

NZ = 4
NY = 4
NX = 4
BLK = 128
VMEM_LIMIT = 40 * 1024 * 1024


def y_pairs(shift):
    return [(z * NY + y, z * NY + (y + shift) % NY) for z in range(NZ) for y in range(NY)]


def z_pairs(shift):
    return [(z * NY + y, (z + shift) % NZ * NY + y) for z in range(NZ) for y in range(NY)]


def x_pairs(shift):
    return [
        ((h * NX + x) * 2 + c, (h * NX + (x + shift) % NX) * 2 + c)
        for h in range(2)
        for x in range(NX)
        for c in range(2)
    ]


CORE_PAIRS = [(i, i ^ 1) for i in range(16)]
HALF_PAIRS = [(i, i ^ 8) for i in range(16)]


def block_grads(cols, half, pos_ref, chip_ref, acts_ref, up_ref, *outs):
    def column(c, carry):
        up = up_ref[:, pl.ds(pl.multiple_of(c * BLK, BLK), BLK)]
        for h, out in enumerate(outs):
            for k in range(half):
                slot = c * half + k
                block = acts_ref[pos_ref[h * cols * half + slot]]
                grad = lax.dot_general(
                    block, up, (((0,), (0,)), ((), ())), preferred_element_type=jnp.float32
                ).astype(jnp.bfloat16)
                for chip in range(8):
                    out[chip_ref[chip], slot] = grad[chip * 16 : (chip + 1) * 16]
        return carry

    lax.fori_loop(0, cols, column, 0)


def project(cols, half, pos_ref, chip_ref, acts_ref, up_ref, w0_ref, w1_ref, hidden_ref, *rest):
    parts, total = rest[:-1], rest[-1]
    total[...] = jnp.zeros_like(total)

    def column(c, carry):
        lanes = pl.ds(pl.multiple_of(c * BLK, BLK), BLK)
        up = up_ref[:, lanes]
        hidden = jnp.zeros((up.shape[0], BLK), jnp.float32)
        for h, w_ref in enumerate((w0_ref, w1_ref)):
            for k in range(0, half, 2):
                rows = []
                blocks = []
                weights = []
                for j in range(2):
                    slot = c * half + k + j
                    rows.append(pos_ref[h * cols * half + slot])
                    blocks.append(acts_ref[rows[-1]])
                    weights += [w_ref[chip_ref[chip], slot] for chip in range(8)]
                weight = jnp.concatenate(weights, axis=0)
                hidden += jnp.dot(
                    jnp.concatenate(blocks, axis=1), weight, preferred_element_type=jnp.float32
                )
                back = lax.dot_general(
                    up, weight, (((1,), (1,)), ((), ())), preferred_element_type=jnp.float32
                )
                for j in range(2):
                    total[rows[j]] += back[:, j * BLK : (j + 1) * BLK]
        hidden_ref[:, lanes] = hidden.astype(jnp.bfloat16)
        return carry

    lax.fori_loop(0, cols, column, 0)
    step = total.shape[0] // len(parts)
    for p, part in enumerate(parts):
        part[...] = total[p * step : (p + 1) * step].astype(jnp.bfloat16)


def kernel_call(body, outs, scratch, flops, ins):
    specs = [pl.BlockSpec(memory_space=pltpu.SMEM)] * 2
    specs += [pl.BlockSpec(memory_space=pltpu.VMEM)] * (len(ins) - 2)
    moved = sum(a.size * a.dtype.itemsize for a in list(ins) + list(outs))
    return pl.pallas_call(
        body,
        out_shape=outs,
        in_specs=specs,
        out_specs=[pl.BlockSpec(memory_space=pltpu.VMEM)] * len(outs),
        scratch_shapes=scratch,
        compiler_params=pltpu.CompilerParams(vmem_limit_bytes=VMEM_LIMIT),
        cost_estimate=pl.CostEstimate(flops=flops, bytes_accessed=moved, transcendentals=0),
    )(*ins)


def f32(a):
    return a.astype(jnp.float32)


def shards(acts, grad_out, values, block_rows, block_count):
    tokens = acts.shape[0]
    cols, slots = block_rows.shape
    half = slots // 2
    own_blocks = acts.shape[1] // BLK
    bf = jnp.bfloat16
    dp, mp = lax.axis_index("dp"), lax.axis_index("mp")
    core, x, zh = dp % 2, dp // 2 % NX, dp // (2 * NX)
    z, y = mp // NY, mp % NY
    first = core == 0

    def halves(a):
        return (
            jnp.where(first, a[:, :half], a[:, half:]),
            jnp.where(first, a[:, half:], a[:, :half]),
        )

    def ordered(mine, other, axis):
        return jnp.where(
            first,
            jnp.concatenate([mine, other], axis=axis),
            jnp.concatenate([other, mine], axis=axis),
        )

    live = jnp.arange(slots, dtype=jnp.int32)[None, :] < block_count[:, None]
    block = jnp.clip(block_rows, 0, NZ * NY * own_blocks - 1)
    owner = block // own_blocks
    place = ((y - owner % NY) % NY * NZ + (z - owner // NY) % NZ) * own_blocks + block % own_blocks
    pos = jnp.concatenate([a.reshape(-1) for a in halves(place)])
    chips = jnp.arange(8, dtype=jnp.int32)
    chip = (x - chips % NX) % NX * 2 + (zh + chips // NX) % 2

    masked = jnp.where(live[:, :, None, None], values, jnp.zeros((), bf))
    mine, other = halves(masked)
    came = lax.ppermute(other, "dp", CORE_PAIRS)
    rows16 = ordered(mine, came, 2).reshape(cols * half, 16, BLK)

    own = acts.reshape(tokens, own_blocks, BLK).transpose(1, 0, 2)
    along_z = jnp.concatenate([own] + [lax.ppermute(own, "mp", z_pairs(q)) for q in range(1, NZ)])

    w2 = jnp.stack([rows16, lax.ppermute(rows16, "dp", HALF_PAIRS)])
    whole = jnp.concatenate(
        [along_z] + [lax.ppermute(along_z, "mp", y_pairs(p)) for p in range(1, NY)]
    )
    w8 = jnp.concatenate([w2] + [lax.ppermute(w2, "dp", x_pairs(s)) for s in range(1, NX)])
    w8_other = lax.ppermute(w8, "dp", CORE_PAIRS)

    flops = 2 * tokens * BLK * BLK * cols * slots
    shape = jax.ShapeDtypeStruct((8, cols * half, 16, BLK), bf)
    mine, other = kernel_call(
        functools.partial(block_grads, cols, half),
        [shape, shape],
        [],
        flops,
        (pos, chip, whole, grad_out),
    )
    came = lax.ppermute(other, "dp", CORE_PAIRS)
    sums = [(f32(mine[s * 2 : s * 2 + 2]) + f32(came[s * 2 : s * 2 + 2])).astype(bf) for s in range(NX)]
    came = [lax.ppermute(sums[s], "dp", x_pairs(-s)) for s in range(1, NX)]
    total = f32(sums[0]) + f32(came[0]) + f32(came[1]) + f32(came[2])
    came = lax.ppermute(total[1].astype(bf), "dp", HALF_PAIRS)
    total = (total[0] + f32(came)).reshape(cols, half, 16, BLK)
    keep = jnp.where(first, total[:, :, :8], total[:, :, 8:])
    send = jnp.where(first, total[:, :, 8:], total[:, :, :8])
    grad_values = ordered(keep, lax.ppermute(send, "dp", CORE_PAIRS), 1)
    grad_values = jnp.where(live[:, :, None, None], grad_values, jnp.zeros((), jnp.float32))

    part = jax.ShapeDtypeStruct((NZ * own_blocks, tokens, BLK), bf)
    hidden_out, *parts = kernel_call(
        functools.partial(project, cols, half),
        [jax.ShapeDtypeStruct(grad_out.shape, bf)] + [part] * NY,
        [pltpu.VMEM((NZ * NY * own_blocks, tokens, BLK), jnp.float32)],
        2 * flops,
        (pos, chip, whole, grad_out, w8, w8_other),
    )
    came = [lax.ppermute(parts[p], "mp", y_pairs(-p)) for p in range(1, NY)]

    def summed(q):
        at = slice(q * own_blocks, (q + 1) * own_blocks)
        return f32(parts[0][at]) + f32(came[0][at]) + f32(came[1][at]) + f32(came[2][at])

    total = summed(0)
    for q in range(1, NZ):
        total += f32(lax.ppermute(summed(q).astype(bf), "mp", z_pairs(-q)))
    grad_acts = total.transpose(1, 0, 2).reshape(tokens, own_blocks * BLK).astype(bf)
    return hidden_out, grad_acts, grad_values


def solution(mesh):
    placed = (P("dp", "mp"), P("dp", "mp"), P("mp", None, "dp", None), P("mp", None), P("mp"))
    return jax.shard_map(
        shards,
        mesh=mesh,
        in_specs=placed,
        out_specs=(P("dp", "mp"), P("dp", "mp"), P("mp", None, "dp", None)),
        check_vma=False,
    )
```

time: 480 us -> 184 us (0.38)
  waiting for transfers between devices: 313 us -> 117 us
  other arithmetic: 62 us -> 5.36 us
  local copies, waits for them, and re-layouts: 56.6 us -> 2.99 us
  starting transfers between devices: 0.16 us -> 45.5 us
  matrix products: 32.4 us -> 0 us
  between operations: 14 us -> 0.93 us
  Pallas kernels: 0 us -> 8.24 us
    reduce_scatter x2 -> x0, waiting for transfers between devices: 174 us -> none  [the longest x1 120 us: shards(): lax.psum_scatter(stacked.astype(jnp.bfloat16), 'dp', scatter_dimension=2,...]
    all_gather x2 -> x0, waiting for transfers between devices: 138 us -> none  [the longest x1 78.1 us: shards(): whole = lax.all_gather(acts, 'mp', axis=1, tiled=True)]
    ppermute x0 -> x24, waiting for transfers between devices: none -> 117 us  [the longest x3 26.2 us: shards(): came = [lax.ppermute(sums[s], 'dp', x_pairs(-s)) for s in range(1, NX)]]
    scatter-add x7 -> x0, other arithmetic: 49.9 us -> none  [shards(): partial_value = partial_value.at[:, block_rows[column]].add(contrib)]
    ppermute x0 -> x24, starting transfers between devices: none -> 45.5 us  [the longest x3 10.7 us: shards(): total += f32(lax.ppermute(summed(q).astype(bf), 'mp', z_pairs(-q)))]
    dot_general x21 -> x0, matrix products: 32.4 us -> none  [the longest x7 13.4 us: shards(): jnp.einsum('tki,tj->kij', picked, upstream, preferred_element_type=jnp.fl...]
    dot_general x7 -> x0, local copies, waits for them, and re-layouts: 14.8 us -> none  [shards(): jnp.einsum('tj,kij->tki', upstream, masked[column], preferred_element_typ...]
    convert_element_type x2, local copies, waits for them, and re-layouts: 10.9 us -> 0.17 us  [the longest x1 0.13 us: shards(): total.transpose(1, 0, 2).reshape(tokens, own_blocks * BLK).astype(bf)]
  transfers between devices with their start and end apart: 4 -> 24, of which waited for: 4 -> 15; matrix products, arithmetic and copies ran while one was open for 11% -> 3% of each run, Pallas kernels for 0% -> 5%
where the time goes in v1:
time: 184 us; the launch traced here: 180 us
  waiting for transfers between devices  117 us (64%)
  starting transfers between devices  45.5 us (25%)
  Pallas kernels  8.24 us (4%)
  other arithmetic  5.36 us (3%)
  local copies, waits for them, and re-layouts  2.99 us (2%)
    ppermute x3, waiting for transfers between devices, shards(): came = [lax.ppermute(sums[s], 'dp', x_pairs(-s)) for s in range(1, NX)]  26.2 us
    ppermute x3, waiting for transfers between devices, shards(): lax.ppermute(w2, 'dp', x_pairs(s))  23.2 us
    ppermute x3, waiting for transfers between devices, shards(): lax.ppermute(along_z, 'mp', y_pairs(p))  22.8 us
    ppermute x3, waiting for transfers between devices, shards(): came = [lax.ppermute(parts[p], 'mp', y_pairs(-p)) for p in range(1, NY)]  20.7 us
    ppermute x3, starting transfers between devices, shards(): total += f32(lax.ppermute(summed(q).astype(bf), 'mp', z_pairs(-q)))  10.7 us
    ppermute x3, waiting for transfers between devices, shards(): total += f32(lax.ppermute(summed(q).astype(bf), 'mp', z_pairs(-q)))  8.93 us
    pallas_call x2, Pallas kernels, kernel_call(): pl.pallas_call(body, out_shape=outs, in_specs=specs, out_specs=[pl.BlockS...  8.24 us
    ppermute x1, waiting for transfers between devices, shards(): w2 = jnp.stack([rows16, lax.ppermute(rows16, 'dp', HALF_PAIRS)])  7.7 us
  transfers between devices with their start and end apart: 24, of which 15 were waited for; matrix products, arithmetic and copies ran while one was open for 3% of the time, Pallas kernels for 5%

profile of v1, /device:TPU:24, one launch (start us, length us, event | category | flops | bytes accessed | tf_op | source)
XLA Modules:
  0.0 180.0 jit_solution(9548264715227621426)
XLA Ops:
  0.6 1.0 copy.8
  1.7 0.1 copy.9
  1.8 4.7 %collective-permute-start.2 = (bf16[4,128,128]{2,1,0:T(8,128)(2,1)S(1)}, bf16[4,128,128]{2,1,0:T(8,128)(2,1)S(1)}, u32[]{:S(2)}, u32[]{:S(2)}) collective-permute-start(bf16[4,128,128]{2,1,0:T(8,128)(2,1)S(1)} %bitcast.22), channel_id=1, source_target_pairs={{0,12},{1,13},{2,14},{3,15},{4,0},{5,1},{6,2},{7,3},{8,4},{9,5},{1... | collective-permute-start | bytes 393224 | tf_op jit(solution)/shard_map/ppermute | solution.py:148
  6.5 0.7 collective-permute-start
  7.2 0.7 iota_compare_fusion
  7.9 1.2 broadcast_select_fusion
  9.3 0.7 fusion.9
  10.2 0.2 collective-permute-done.2
  10.4 7.3 %collective-permute-done.1 = bf16[4,128,128]{2,1,0:T(8,128)(2,1)S(1)} collective-permute-done((bf16[4,128,128]{2,1,0:T(8,128)(2,1)S(1)}, bf16[4,128,128]{2,1,0:T(8,128)(2,1)S(1)}, u32[]{:S(2)}, u32[]{:S(2)}) %collective-permute-start.1) | collective-permute-done | bytes 131104 | tf_op jit(solution)/shard_map/ppermute | solution.py:148
  17.8 0.3 collective-permute-start.3
  18.2 2.6 %collective-permute-start.4 = (bf16[16,128,128]{2,1,0:T(8,128)(2,1)S(1)}, bf16[16,128,128]{2,1,0:T(8,128)(2,1)S(1)}, u32[]{:S(2)}, u32[]{:S(2)}) collective-permute-start(bf16[16,128,128]{2,1,0:T(8,128)(2,1)S(1)} %pad_maximum_fusion.1), channel_id=1, source_target_pairs={{0,2},{1,3},{2,0},{3,1},{4,6},{5,7},{6,4},{7,5},{8,10},{9,11},{10,... | collective-permute-start | bytes 1572872 | tf_op jit(solution)/shard_map/ppermute | solution.py:152
  21.0 11.8 %collective-permute-done.3 = bf16[16,128,128]{2,1,0:T(8,128)(2,1)S(1)} collective-permute-done((bf16[16,128,128]{2,1,0:T(8,128)(2,1)S(1)}, bf16[16,128,128]{2,1,0:T(8,128)(2,1)S(1)}, u32[]{:S(2)}, u32[]{:S(2)}) %collective-permute-start.3) | collective-permute-done | bytes 524320 | tf_op jit(solution)/shard_map/ppermute | solution.py:152
  32.8 1.8 collective-permute-done.4
  34.7 9.2 %collective-permute-done.5 = bf16[16,128,128]{2,1,0:T(8,128)(2,1)S(1)} collective-permute-done((bf16[16,128,128]{2,1,0:T(8,128)(2,1)S(1)}, bf16[16,128,128]{2,1,0:T(8,128)(2,1)S(1)}, u32[]{:S(2)}, u32[]{:S(2)}) %collective-permute-start.5) | collective-permute-done | bytes 524320 | tf_op jit(solution)/shard_map/ppermute | solution.py:152
  44.0 3.2 %shard_map.77 = (bf16[8,70,16,128]{3,2,1,0:T(8,128)(2,1)S(1)}, bf16[8,70,16,128]{3,2,1,0:T(8,128)(2,1)S(1)}) custom-call(s32[140]{0:T(256)S(1)} %pad_add_fusion.pos_ref, s32[8]{0:T(128)S(1)} %fusion.15.chip_ref, bf16[64,128,128]{2,1,0:T(8,128)(2,1)S(1)} %constant_dynamic-update-slice_fusion.acts_ref, bf16[128,896]{1,0:T(8,128)(2,1)S(1)} %copy-done), custom_call_target="tpu_custom_call" | custom-call | flops 587202560 | bytes 6914640 | tf_op jit(solution)/shard_map/pallas_call | solution.py:95
  47.4 5.6 %collective-permute-start.7 = (bf16[70,16,128]{2,1,0:T(8,128)(2,1)S(1)}, bf16[70,16,128]{2,1,0:T(8,128)(2,1)S(1)}, u32[]{:S(2)}, u32[]{:S(2)}) collective-permute-start(bf16[70,16,128]{2,1,0:T(8,128)(2,1)S(1)} %maximum_select_fusion.2), channel_id=1, source_target_pairs={{0,128},{16,144},{32,160},{48,176},{64,192},{80,208},{96,224},{112... | collective-permute-start | bytes 860168 | tf_op jit(solution)/shard_map/ppermute | solution.py:150
  53.1 7.7 %collective-permute-done.7 = bf16[70,16,128]{2,1,0:T(8,128)(2,1)S(1)} collective-permute-done((bf16[70,16,128]{2,1,0:T(8,128)(2,1)S(1)}, bf16[70,16,128]{2,1,0:T(8,128)(2,1)S(1)}, u32[]{:S(2)}, u32[]{:S(2)}) %collective-permute-start.7) | collective-permute-done | bytes 286752 | tf_op jit(solution)/shard_map/ppermute | solution.py:150
  60.8 1.6 collective-permute-start.8
  62.4 2.7 %collective-permute-start.9 = (bf16[2,70,16,128]{3,2,1,0:T(8,128)(2,1)S(1)}, bf16[2,70,16,128]{3,2,1,0:T(8,128)(2,1)S(1)}, u32[]{:S(2)}, u32[]{:S(2)}) collective-permute-start(bf16[2,70,16,128]{3,2,1,0:T(8,128)(2,1)S(1)} %pad_maximum_fusion), channel_id=1, source_target_pairs={{0,64},{16,80},{32,96},{48,112},{64,0},{80,16},{96,32},{112,48},{1... | collective-permute-start | bytes 1720328 | tf_op jit(solution)/shard_map/ppermute | solution.py:154
  65.1 1.4 collective-permute-start.10
  66.6 10.4 %collective-permute-done.8 = bf16[2,70,16,128]{3,2,1,0:T(8,128)(2,1)S(1)} collective-permute-done((bf16[2,70,16,128]{3,2,1,0:T(8,128)(2,1)S(1)}, bf16[2,70,16,128]{3,2,1,0:T(8,128)(2,1)S(1)}, u32[]{:S(2)}, u32[]{:S(2)}) %collective-permute-start.8) | collective-permute-done | bytes 573472 | tf_op jit(solution)/shard_map/ppermute | solution.py:154
  77.0 0.1 constant_dynamic-update-slice_fusion.9
  77.1 12.8 %collective-permute-done.9 = bf16[2,70,16,128]{3,2,1,0:T(8,128)(2,1)S(1)} collective-permute-done((bf16[2,70,16,128]{3,2,1,0:T(8,128)(2,1)S(1)}, bf16[2,70,16,128]{3,2,1,0:T(8,128)(2,1)S(1)}, u32[]{:S(2)}, u32[]{:S(2)}) %collective-permute-start.9) | collective-permute-done | bytes 573472 | tf_op jit(solution)/shard_map/ppermute | solution.py:154
  89.9 0.1 constant_dynamic-update-slice_fusion.8
  90.1 0.1 constant_dynamic-update-slice_fusion.7.w0_ref
  90.3 0.4 add_convert_fusion.2
  90.8 2.2 %collective-permute-start.19 = (bf16[2,70,16,128]{3,2,1,0:T(8,128)(2,1)S(1)}, bf16[2,70,16,128]{3,2,1,0:T(8,128)(2,1)S(1)}, u32[]{:S(2)}, u32[]{:S(2)}) collective-permute-start(bf16[2,70,16,128]{3,2,1,0:T(8,128)(2,1)S(1)} %get-tuple-element.22), channel_id=1, source_target_pairs={{0,96},{16,112},{32,0},{48,16},{64,32},{80,48},{96,64},{112,80},{1... | collective-permute-start | bytes 1720328 | tf_op jit(solution)/shard_map/ppermute | solution.py:168
  93.0 2.4 %collective-permute-start.20 = (bf16[2,70,16,128]{3,2,1,0:T(8,128)(2,1)S(1)}, bf16[2,70,16,128]{3,2,1,0:T(8,128)(2,1)S(1)}, u32[]{:S(2)}, u32[]{:S(2)}) collective-permute-start(bf16[2,70,16,128]{3,2,1,0:T(8,128)(2,1)S(1)} %get-tuple-element.24), channel_id=1, source_target_pairs={{0,64},{16,80},{32,96},{48,112},{64,0},{80,16},{96,32},{112,48},{1... | collective-permute-start | bytes 1720328 | tf_op jit(solution)/shard_map/ppermute | solution.py:168
  95.4 22.8 %collective-permute-done.19 = bf16[2,70,16,128]{3,2,1,0:T(8,128)(2,1)S(1)} collective-permute-done((bf16[2,70,16,128]{3,2,1,0:T(8,128)(2,1)S(1)}, bf16[2,70,16,128]{3,2,1,0:T(8,128)(2,1)S(1)}, u32[]{:S(2)}, u32[]{:S(2)}) %collective-permute-start.19) | collective-permute-done | bytes 573472 | tf_op jit(solution)/shard_map/ppermute | solution.py:168
  118.2 3.4 %collective-permute-done.21 = bf16[2,70,16,128]{3,2,1,0:T(8,128)(2,1)S(1)} collective-permute-done((bf16[2,70,16,128]{3,2,1,0:T(8,128)(2,1)S(1)}, bf16[2,70,16,128]{3,2,1,0:T(8,128)(2,1)S(1)}, u32[]{:S(2)}, u32[]{:S(2)}) %collective-permute-start.21) | collective-permute-done | bytes 573472 | tf_op jit(solution)/shard_map/ppermute | solution.py:168
  121.6 0.3 convert_add_fusion
  122.0 5.7 %collective-permute-start.22 = (bf16[70,16,128]{2,1,0:T(8,128)(2,1)S(1)}, bf16[70,16,128]{2,1,0:T(8,128)(2,1)S(1)}, u32[]{:S(2)}, u32[]{:S(2)}) collective-permute-start(bf16[70,16,128]{2,1,0:T(8,128)(2,1)S(1)} %fusion.2), channel_id=1, source_target_pairs={{0,128},{16,144},{32,160},{48,176},{64,192},{80,208},{96,224},{112... | collective-permute-start | bytes 860168 | tf_op jit(solution)/shard_map/ppermute | solution.py:170
  127.6 5.1 %shard_map.76 = (bf16[128,896]{1,0:T(8,128)(2,1)}, bf16[16,128,128]{2,1,0:T(8,128)(2,1)S(1)}, bf16[16,128,128]{2,1,0:T(8,128)(2,1)S(1)}, bf16[16,128,128]{2,1,0:T(8,128)(2,1)S(1)}, bf16[16,128,128]{2,1,0:T(8,128)(2,1)S(1)}) custom-call(s32[140]{0:T(256)S(1)} %pad_add_fusion.pos_ref, s32[8]{0:T(128)S(1)} %fusion.15.chip_ref, ...), custom_call_target="tpu_custom_call" | custom-call | flops 1174405120 | bytes 9241168 | tf_op jit(solution)/shard_map/pallas_call | solution.py:95
  132.7 1.0 collective-permute-start.12
  133.7 1.6 collective-permute-start.13
  135.3 1.9 %collective-permute-start.14 = (bf16[16,128,128]{2,1,0:T(8,128)(2,1)S(1)}, bf16[16,128,128]{2,1,0:T(8,128)(2,1)S(1)}, u32[]{:S(2)}, u32[]{:S(2)}) collective-permute-start(bf16[16,128,128]{2,1,0:T(8,128)(2,1)S(1)} %get-tuple-element.14), channel_id=1, source_target_pairs={{0,1},{1,2},{2,3},{3,0},{4,5},{5,6},{6,7},{7,4},{8,9},{9,10},{10,1... | collective-permute-start | bytes 1572872 | tf_op jit(solution)/shard_map/ppermute | solution.py:185
  137.2 20.1 %collective-permute-done.12 = bf16[16,128,128]{2,1,0:T(8,128)(2,1)S(1)} collective-permute-done((bf16[16,128,128]{2,1,0:T(8,128)(2,1)S(1)}, bf16[16,128,128]{2,1,0:T(8,128)(2,1)S(1)}, u32[]{:S(2)}, u32[]{:S(2)}) %collective-permute-start.12) | collective-permute-done | bytes 524320 | tf_op jit(solution)/shard_map/ppermute | solution.py:185
  157.4 0.6 collective-permute-done.14
  158.0 0.2 add_convert_fusion.7
  158.2 0.8 collective-permute-start.15
  159.0 7.0 %collective-permute-start.17 = (bf16[4,128,128]{2,1,0:T(8,128)(2,1)S(1)}, bf16[4,128,128]{2,1,0:T(8,128)(2,1)S(1)}, u32[]{:S(2)}, u32[]{:S(2)}) collective-permute-start(bf16[4,128,128]{2,1,0:T(8,128)(2,1)S(1)} %get-tuple-element.26), channel_id=1, source_target_pairs={{0,4},{1,5},{2,6},{3,7},{4,8},{5,9},{6,10},{7,11},{8,12},{9,13},{1... | collective-permute-start | bytes 393224 | tf_op jit(solution)/shard_map/ppermute | solution.py:193
  166.0 2.9 %collective-permute-start.16 = (bf16[4,128,128]{2,1,0:T(8,128)(2,1)S(1)}, bf16[4,128,128]{2,1,0:T(8,128)(2,1)S(1)}, u32[]{:S(2)}, u32[]{:S(2)}) collective-permute-start(bf16[4,128,128]{2,1,0:T(8,128)(2,1)S(1)} %get-tuple-element.27), channel_id=1, source_target_pairs={{0,8},{1,9},{2,10},{3,11},{4,12},{5,13},{6,14},{7,15},{8,0},{9,1},... | collective-permute-start | bytes 393224 | tf_op jit(solution)/shard_map/ppermute | solution.py:193
  169.0 2.6 %collective-permute-done.15 = bf16[4,128,128]{2,1,0:T(8,128)(2,1)S(1)} collective-permute-done((bf16[4,128,128]{2,1,0:T(8,128)(2,1)S(1)}, bf16[4,128,128]{2,1,0:T(8,128)(2,1)S(1)}, u32[]{:S(2)}, u32[]{:S(2)}) %collective-permute-start.15) | collective-permute-done | bytes 131104 | tf_op jit(solution)/shard_map/ppermute | solution.py:193
  171.6 3.3 %collective-permute-done.17 = bf16[4,128,128]{2,1,0:T(8,128)(2,1)S(1)} collective-permute-done((bf16[4,128,128]{2,1,0:T(8,128)(2,1)S(1)}, bf16[4,128,128]{2,1,0:T(8,128)(2,1)S(1)}, u32[]{:S(2)}, u32[]{:S(2)}) %collective-permute-start.17) | collective-permute-done | bytes 131104 | tf_op jit(solution)/shard_map/ppermute | solution.py:193
  174.9 3.0 %collective-permute-done.16 = bf16[4,128,128]{2,1,0:T(8,128)(2,1)S(1)} collective-permute-done((bf16[4,128,128]{2,1,0:T(8,128)(2,1)S(1)}, bf16[4,128,128]{2,1,0:T(8,128)(2,1)S(1)}, u32[]{:S(2)}, u32[]{:S(2)}) %collective-permute-start.16) | collective-permute-done | bytes 131104 | tf_op jit(solution)/shard_map/ppermute | solution.py:193
  178.1 0.1 copy.10
  178.2 0.8 copy.11
  179.0 1.0 fusion.1
  (40 shorter events, 1.7 us)
Async XLA Ops:
  1.8 8.6 %collective-permute-start.2 = (bf16[4,128,128]{2,1,0:T(8,128)(2,1)S(1)}, bf16[4,128,128]{2,1,0:T(8,128)(2,1)S(1)}, u32[]{:S(2)}, u32[]{:S(2)}) collective-permute-start(bf16[4,128,128]{2,1,0:T(8,128)(2,1)S(1)} %bitcast.22), channel_id=1, source_target_pairs={{0,12},{1,13},{2,14},{3,15},{4,0},{5,1},{6,2},{7,3},{8,4},{9,5},{1... | collective-permute-start | bytes 393224 | tf_op jit(solution)/shard_map/ppermute | solution.py:148
  6.5 11.2 %collective-permute-start.1 = (bf16[4,128,128]{2,1,0:T(8,128)(2,1)S(1)}, bf16[4,128,128]{2,1,0:T(8,128)(2,1)S(1)}, u32[]{:S(2)}, u32[]{:S(2)}) collective-permute-start(bf16[4,128,128]{2,1,0:T(8,128)(2,1)S(1)} %bitcast.23), channel_id=1, source_target_pairs={{0,8},{1,9},{2,10},{3,11},{4,12},{5,13},{6,14},{7,15},{8,0},{9,1},... | collective-permute-start | bytes 393224 | tf_op jit(solution)/shard_map/ppermute | solution.py:148
  6.5 11.2 %collective-permute-start = (bf16[4,128,128]{2,1,0:T(8,128)(2,1)S(1)}, bf16[4,128,128]{2,1,0:T(8,128)(2,1)S(1)}, u32[]{:S(2)}, u32[]{:S(2)}) collective-permute-start(bf16[4,128,128]{2,1,0:T(8,128)(2,1)S(1)} %bitcast.24), channel_id=1, source_target_pairs={{0,4},{1,5},{2,6},{3,7},{4,8},{5,9},{6,10},{7,11},{8,12},{9,13},{1... | collective-permute-start | bytes 393224 | tf_op jit(solution)/shard_map/ppermute | solution.py:148
  9.1 38.2 %collective-permute-start.6 = (bf16[7,10,8,128]{3,2,1,0:T(8,128)(2,1)S(1)}, bf16[7,10,8,128]{3,2,1,0:T(8,128)(2,1)S(1)}, u32[]{:S(2)}, u32[]{:S(2)}) collective-permute-start(bf16[7,10,8,128]{3,2,1,0:T(8,128)(2,1)S(1)} %get-tuple-element.30), channel_id=1, source_target_pairs={{0,16},{16,0},{32,48},{48,32},{64,80},{80,64},{96,112},{112,96},{1... | collective-permute-start | bytes 430088 | tf_op jit(solution)/shard_map/ppermute | solution.py:144
  17.8 26.2 %copy-start = (bf16[128,896]{1,0:T(8,128)(2,1)S(1)}, bf16[128,896]{1,0:T(8,128)(2,1)}, u32[]{:S(2)}) copy-start(bf16[128,896]{1,0:T(8,128)(2,1)} %up_ref.3) | copy-start | bytes 688132
  17.8 14.9 %collective-permute-start.3 = (bf16[16,128,128]{2,1,0:T(8,128)(2,1)S(1)}, bf16[16,128,128]{2,1,0:T(8,128)(2,1)S(1)}, u32[]{:S(2)}, u32[]{:S(2)}) collective-permute-start(bf16[16,128,128]{2,1,0:T(8,128)(2,1)S(1)} %pad_maximum_fusion.1), channel_id=1, source_target_pairs={{0,1},{1,2},{2,3},{3,0},{4,5},{5,6},{6,7},{7,4},{8,9},{9,10},{10,1... | collective-permute-start | bytes 1572872 | tf_op jit(solution)/shard_map/ppermute | solution.py:152
  18.2 16.4 %collective-permute-start.4 = (bf16[16,128,128]{2,1,0:T(8,128)(2,1)S(1)}, bf16[16,128,128]{2,1,0:T(8,128)(2,1)S(1)}, u32[]{:S(2)}, u32[]{:S(2)}) collective-permute-start(bf16[16,128,128]{2,1,0:T(8,128)(2,1)S(1)} %pad_maximum_fusion.1), channel_id=1, source_target_pairs={{0,2},{1,3},{2,0},{3,1},{4,6},{5,7},{6,4},{7,5},{8,10},{9,11},{10,... | collective-permute-start | bytes 1572872 | tf_op jit(solution)/shard_map/ppermute | solution.py:152
  20.8 23.1 %collective-permute-start.5 = (bf16[16,128,128]{2,1,0:T(8,128)(2,1)S(1)}, bf16[16,128,128]{2,1,0:T(8,128)(2,1)S(1)}, u32[]{:S(2)}, u32[]{:S(2)}) collective-permute-start(bf16[16,128,128]{2,1,0:T(8,128)(2,1)S(1)} %pad_maximum_fusion.1), channel_id=1, source_target_pairs={{0,3},{1,0},{2,1},{3,2},{4,7},{5,4},{6,5},{7,6},{8,11},{9,8},{10,9... | collective-permute-start | bytes 1572872 | tf_op jit(solution)/shard_map/ppermute | solution.py:152
  47.2 43.2 %collective-permute-start.18 = (bf16[8,70,16,128]{3,2,1,0:T(8,128)(2,1)S(1)}, bf16[8,70,16,128]{3,2,1,0:T(8,128)(2,1)S(1)}, u32[]{:S(2)}, u32[]{:S(2)}) collective-permute-start(bf16[8,70,16,128]{3,2,1,0:T(8,128)(2,1)S(1)} %get-tuple-element.16), channel_id=1, source_target_pairs={{0,16},{16,0},{32,48},{48,32},{64,80},{80,64},{96,112},{112,96},{1... | collective-permute-start | bytes 6881288 | tf_op jit(solution)/shard_map/ppermute | solution.py:166
  47.4 13.4 %collective-permute-start.7 = (bf16[70,16,128]{2,1,0:T(8,128)(2,1)S(1)}, bf16[70,16,128]{2,1,0:T(8,128)(2,1)S(1)}, u32[]{:S(2)}, u32[]{:S(2)}) collective-permute-start(bf16[70,16,128]{2,1,0:T(8,128)(2,1)S(1)} %maximum_select_fusion.2), channel_id=1, source_target_pairs={{0,128},{16,144},{32,160},{48,176},{64,192},{80,208},{96,224},{112... | collective-permute-start | bytes 860168 | tf_op jit(solution)/shard_map/ppermute | solution.py:150
  60.8 16.2 %collective-permute-start.8 = (bf16[2,70,16,128]{3,2,1,0:T(8,128)(2,1)S(1)}, bf16[2,70,16,128]{3,2,1,0:T(8,128)(2,1)S(1)}, u32[]{:S(2)}, u32[]{:S(2)}) collective-permute-start(bf16[2,70,16,128]{3,2,1,0:T(8,128)(2,1)S(1)} %pad_maximum_fusion), channel_id=1, source_target_pairs={{0,32},{16,48},{32,64},{48,80},{64,96},{80,112},{96,0},{112,16},{1... | collective-permute-start | bytes 1720328 | tf_op jit(solution)/shard_map/ppermute | solution.py:154
  62.4 27.6 %collective-permute-start.9 = (bf16[2,70,16,128]{3,2,1,0:T(8,128)(2,1)S(1)}, bf16[2,70,16,128]{3,2,1,0:T(8,128)(2,1)S(1)}, u32[]{:S(2)}, u32[]{:S(2)}) collective-permute-start(bf16[2,70,16,128]{3,2,1,0:T(8,128)(2,1)S(1)} %pad_maximum_fusion), channel_id=1, source_target_pairs={{0,64},{16,80},{32,96},{48,112},{64,0},{80,16},{96,32},{112,48},{1... | collective-permute-start | bytes 1720328 | tf_op jit(solution)/shard_map/ppermute | solution.py:154
  65.1 25.0 %collective-permute-start.10 = (bf16[2,70,16,128]{3,2,1,0:T(8,128)(2,1)S(1)}, bf16[2,70,16,128]{3,2,1,0:T(8,128)(2,1)S(1)}, u32[]{:S(2)}, u32[]{:S(2)}) collective-permute-start(bf16[2,70,16,128]{3,2,1,0:T(8,128)(2,1)S(1)} %pad_maximum_fusion), channel_id=1, source_target_pairs={{0,96},{16,112},{32,0},{48,16},{64,32},{80,48},{96,64},{112,80},{1... | collective-permute-start | bytes 1720328 | tf_op jit(solution)/shard_map/ppermute | solution.py:154
  90.2 37.4 %collective-permute-start.11 = (bf16[8,70,16,128]{3,2,1,0:T(8,128)(2,1)S(1)}, bf16[8,70,16,128]{3,2,1,0:T(8,128)(2,1)S(1)}, u32[]{:S(2)}, u32[]{:S(2)}) collective-permute-start(bf16[8,70,16,128]{3,2,1,0:T(8,128)(2,1)S(1)} %constant_dynamic-update-slice_fusion.7.w0_ref), channel_id=1, source_target_pairs={{0,16},{16,0},{32,48},{48,32},{64,80},{80,64},{96,112},{112,96},{1... | collective-permute-start | bytes 6881288 | tf_op jit(solution)/shard_map/ppermute | solution.py:155
  90.8 27.4 %collective-permute-start.19 = (bf16[2,70,16,128]{3,2,1,0:T(8,128)(2,1)S(1)}, bf16[2,70,16,128]{3,2,1,0:T(8,128)(2,1)S(1)}, u32[]{:S(2)}, u32[]{:S(2)}) collective-permute-start(bf16[2,70,16,128]{3,2,1,0:T(8,128)(2,1)S(1)} %get-tuple-element.22), channel_id=1, source_target_pairs={{0,96},{16,112},{32,0},{48,16},{64,32},{80,48},{96,64},{112,80},{1... | collective-permute-start | bytes 1720328 | tf_op jit(solution)/shard_map/ppermute | solution.py:168
  93.0 28.6 %collective-permute-start.21 = (bf16[2,70,16,128]{3,2,1,0:T(8,128)(2,1)S(1)}, bf16[2,70,16,128]{3,2,1,0:T(8,128)(2,1)S(1)}, u32[]{:S(2)}, u32[]{:S(2)}) collective-permute-start(bf16[2,70,16,128]{3,2,1,0:T(8,128)(2,1)S(1)} %get-tuple-element.23), channel_id=1, source_target_pairs={{0,32},{16,48},{32,64},{48,80},{64,96},{80,112},{96,0},{112,16},{1... | collective-permute-start | bytes 1720328 | tf_op jit(solution)/shard_map/ppermute | solution.py:168
  93.0 28.6 %collective-permute-start.20 = (bf16[2,70,16,128]{3,2,1,0:T(8,128)(2,1)S(1)}, bf16[2,70,16,128]{3,2,1,0:T(8,128)(2,1)S(1)}, u32[]{:S(2)}, u32[]{:S(2)}) collective-permute-start(bf16[2,70,16,128]{3,2,1,0:T(8,128)(2,1)S(1)} %get-tuple-element.24), channel_id=1, source_target_pairs={{0,64},{16,80},{32,96},{48,112},{64,0},{80,16},{96,32},{112,48},{1... | collective-permute-start | bytes 1720328 | tf_op jit(solution)/shard_map/ppermute | solution.py:168
  122.0 15.2 %collective-permute-start.22 = (bf16[70,16,128]{2,1,0:T(8,128)(2,1)S(1)}, bf16[70,16,128]{2,1,0:T(8,128)(2,1)S(1)}, u32[]{:S(2)}, u32[]{:S(2)}) collective-permute-start(bf16[70,16,128]{2,1,0:T(8,128)(2,1)S(1)} %fusion.2), channel_id=1, source_target_pairs={{0,128},{16,144},{32,160},{48,176},{64,192},{80,208},{96,224},{112... | collective-permute-start | bytes 860168 | tf_op jit(solution)/shard_map/ppermute | solution.py:170
  132.7 24.6 %collective-permute-start.12 = (bf16[16,128,128]{2,1,0:T(8,128)(2,1)S(1)}, bf16[16,128,128]{2,1,0:T(8,128)(2,1)S(1)}, u32[]{:S(2)}, u32[]{:S(2)}) collective-permute-start(bf16[16,128,128]{2,1,0:T(8,128)(2,1)S(1)} %get-tuple-element.12), channel_id=1, source_target_pairs={{0,3},{1,0},{2,1},{3,2},{4,7},{5,4},{6,5},{7,6},{8,11},{9,8},{10,9... | collective-permute-start | bytes 1572872 | tf_op jit(solution)/shard_map/ppermute | solution.py:185
  133.7 23.6 %collective-permute-start.13 = (bf16[16,128,128]{2,1,0:T(8,128)(2,1)S(1)}, bf16[16,128,128]{2,1,0:T(8,128)(2,1)S(1)}, u32[]{:S(2)}, u32[]{:S(2)}) collective-permute-start(bf16[16,128,128]{2,1,0:T(8,128)(2,1)S(1)} %get-tuple-element.13), channel_id=1, source_target_pairs={{0,2},{1,3},{2,0},{3,1},{4,6},{5,7},{6,4},{7,5},{8,10},{9,11},{10,... | collective-permute-start | bytes 1572872 | tf_op jit(solution)/shard_map/ppermute | solution.py:185
  135.3 22.7 %collective-permute-start.14 = (bf16[16,128,128]{2,1,0:T(8,128)(2,1)S(1)}, bf16[16,128,128]{2,1,0:T(8,128)(2,1)S(1)}, u32[]{:S(2)}, u32[]{:S(2)}) collective-permute-start(bf16[16,128,128]{2,1,0:T(8,128)(2,1)S(1)} %get-tuple-element.14), channel_id=1, source_target_pairs={{0,1},{1,2},{2,3},{3,0},{4,5},{5,6},{6,7},{7,4},{8,9},{9,10},{10,1... | collective-permute-start | bytes 1572872 | tf_op jit(solution)/shard_map/ppermute | solution.py:185
  158.2 13.4 %collective-permute-start.15 = (bf16[4,128,128]{2,1,0:T(8,128)(2,1)S(1)}, bf16[4,128,128]{2,1,0:T(8,128)(2,1)S(1)}, u32[]{:S(2)}, u32[]{:S(2)}) collective-permute-start(bf16[4,128,128]{2,1,0:T(8,128)(2,1)S(1)} %get-tuple-element.25), channel_id=1, source_target_pairs={{0,12},{1,13},{2,14},{3,15},{4,0},{5,1},{6,2},{7,3},{8,4},{9,5},{1... | collective-permute-start | bytes 393224 | tf_op jit(solution)/shard_map/ppermute | solution.py:193
  159.0 15.9 %collective-permute-start.17 = (bf16[4,128,128]{2,1,0:T(8,128)(2,1)S(1)}, bf16[4,128,128]{2,1,0:T(8,128)(2,1)S(1)}, u32[]{:S(2)}, u32[]{:S(2)}) collective-permute-start(bf16[4,128,128]{2,1,0:T(8,128)(2,1)S(1)} %get-tuple-element.26), channel_id=1, source_target_pairs={{0,4},{1,5},{2,6},{3,7},{4,8},{5,9},{6,10},{7,11},{8,12},{9,13},{1... | collective-permute-start | bytes 393224 | tf_op jit(solution)/shard_map/ppermute | solution.py:193
  166.0 11.9 %collective-permute-start.16 = (bf16[4,128,128]{2,1,0:T(8,128)(2,1)S(1)}, bf16[4,128,128]{2,1,0:T(8,128)(2,1)S(1)}, u32[]{:S(2)}, u32[]{:S(2)}) collective-permute-start(bf16[4,128,128]{2,1,0:T(8,128)(2,1)S(1)} %get-tuple-element.27), channel_id=1, source_target_pairs={{0,8},{1,9},{2,10},{3,11},{4,12},{5,13},{6,14},{7,15},{8,0},{9,1},... | collective-permute-start | bytes 393224 | tf_op jit(solution)/shard_map/ppermute | solution.py:193
  168.9 10.1 %collective-permute-start.23 = (f32[7,10,8,128]{3,2,1,0:T(8,128)S(1)}, f32[7,10,8,128]{3,2,1,0:T(8,128)S(1)}, u32[]{:S(2)}, u32[]{:S(2)}) collective-permute-start(f32[7,10,8,128]{3,2,1,0:T(8,128)S(1)} %get-tuple-element.29), channel_id=1, source_target_pairs={{0,16},{16,0},{32,48},{48,32},{64,80},{80,64},{96,112},{112,96},{1... | collective-permute-start | bytes 860168 | tf_op jit(solution)/shard_map/ppermute | solution.py:174

commit v2 on v1

--- a/solution.py
+++ b/solution.py
@@ -83,9 +83,10 @@
         return carry
 
     lax.fori_loop(0, cols, column, 0)
-    step = total.shape[0] // len(parts)
-    for p, part in enumerate(parts):
-        part[...] = total[p * step : (p + 1) * step].astype(jnp.bfloat16)
+    start = 0
+    for part in parts:
+        part[...] = total[start : start + part.shape[0]].astype(jnp.bfloat16)
+        start += part.shape[0]
 
 
 def kernel_call(body, outs, scratch, flops, ins):
@@ -107,6 +108,58 @@
     return a.astype(jnp.float32)
 
 
+def z_step(a, q):
+    with jax.named_scope("z_lo"):
+        return lax.ppermute(a, "mp", z_pairs(q))
+
+
+def y_step(a, p):
+    with jax.named_scope("y"):
+        return lax.ppermute(a, "mp", y_pairs(p))
+
+
+def x_step(a, s):
+    with jax.named_scope("x"):
+        return lax.ppermute(a, "dp", x_pairs(s))
+
+
+def zh_step(a):
+    with jax.named_scope("z_hi"):
+        return lax.ppermute(a, "dp", HALF_PAIRS)
+
+
+def core_step(a):
+    with jax.named_scope("core"):
+        return lax.ppermute(a, "dp", CORE_PAIRS)
+
+
+def tie(values, *after):
+    return lax.optimization_barrier((values, after))[0]
+
+
+def gather_direct(step, a):
+    return [a] + [step(a, s) for s in range(1, 4)]
+
+
+def gather_passed(step, a):
+    n = a.shape[0] // 2
+    back, ahead = step(a, 1), step(a, -1)
+    opposite = jnp.concatenate([step(back[:n], 1), step(ahead[n:], -1)])
+    return [a, back, opposite, ahead]
+
+
+def sum_direct(step, p0, p1, p2a, p2b, p3):
+    return f32(p0) + f32(step(p1, -1)) + f32(step(jnp.concatenate([p2a, p2b]), -2)) + f32(step(p3, -3))
+
+
+def sum_passed(step, p0, p1, p2a, p2b, p3):
+    n = p2a.shape[0]
+    ahead, back = step(p2a, 1), step(p2b, -1)
+    p3 = jnp.concatenate([(f32(p3[:n]) + f32(ahead)).astype(p3.dtype), p3[n:]])
+    p1 = jnp.concatenate([p1[:n], (f32(p1[n:]) + f32(back)).astype(p1.dtype)])
+    return f32(p0) + f32(step(p3, 1)) + f32(step(p1, -1))
+
+
 def shards(acts, grad_out, values, block_rows, block_count):
     tokens = acts.shape[0]
     cols, slots = block_rows.shape
@@ -131,28 +184,28 @@
             jnp.concatenate([other, mine], axis=axis),
         )
 
+    blocks = NZ * NY * own_blocks
     live = jnp.arange(slots, dtype=jnp.int32)[None, :] < block_count[:, None]
-    block = jnp.clip(block_rows, 0, NZ * NY * own_blocks - 1)
-    owner = block // own_blocks
-    place = ((y - owner % NY) % NY * NZ + (z - owner // NY) % NZ) * own_blocks + block % own_blocks
+    owner = block_rows // own_blocks
+    place = ((y - owner % NY) % NY * NZ + (z - owner // NY) % NZ) * own_blocks + block_rows % own_blocks
+    place = jnp.where(live, place, blocks)
     pos = jnp.concatenate([a.reshape(-1) for a in halves(place)])
     chips = jnp.arange(8, dtype=jnp.int32)
-    chip = (x - chips % NX) % NX * 2 + (zh + chips // NX) % 2
-
-    masked = jnp.where(live[:, :, None, None], values, jnp.zeros((), bf))
-    mine, other = halves(masked)
-    came = lax.ppermute(other, "dp", CORE_PAIRS)
-    rows16 = ordered(mine, came, 2).reshape(cols * half, 16, BLK)
+    chip = (zh + chips // NX) % 2 * NX + (x - chips % NX) % NX
+
+    mine, other = halves(values)
+    rows16 = ordered(mine, core_step(other), 2).reshape(cols * half, 16, BLK)
 
     own = acts.reshape(tokens, own_blocks, BLK).transpose(1, 0, 2)
-    along_z = jnp.concatenate([own] + [lax.ppermute(own, "mp", z_pairs(q)) for q in range(1, NZ)])
-
-    w2 = jnp.stack([rows16, lax.ppermute(rows16, "dp", HALF_PAIRS)])
-    whole = jnp.concatenate(
-        [along_z] + [lax.ppermute(along_z, "mp", y_pairs(p)) for p in range(1, NY)]
-    )
-    w8 = jnp.concatenate([w2] + [lax.ppermute(w2, "dp", x_pairs(s)) for s in range(1, NX)])
-    w8_other = lax.ppermute(w8, "dp", CORE_PAIRS)
+    along_z = jnp.concatenate([own] + [z_step(own, q) for q in range(1, NZ)])
+    far16 = zh_step(rows16)
+    near = gather_direct(x_step, rows16)
+    along_z = tie(along_z, rows16)
+    whole = gather_passed(y_step, along_z)
+    far = gather_direct(x_step, far16)
+    whole = jnp.concatenate(whole + [jnp.zeros((1, tokens, BLK), bf)])
+    w8 = jnp.stack(near + far)
+    w8_other = core_step(w8)
 
     flops = 2 * tokens * BLK * BLK * cols * slots
     shape = jax.ShapeDtypeStruct((8, cols * half, 16, BLK), bf)
@@ -163,34 +216,37 @@
         flops,
         (pos, chip, whole, grad_out),
     )
-    came = lax.ppermute(other, "dp", CORE_PAIRS)
-    sums = [(f32(mine[s * 2 : s * 2 + 2]) + f32(came[s * 2 : s * 2 + 2])).astype(bf) for s in range(NX)]
-    came = [lax.ppermute(sums[s], "dp", x_pairs(-s)) for s in range(1, NX)]
-    total = f32(sums[0]) + f32(came[0]) + f32(came[1]) + f32(came[2])
-    came = lax.ppermute(total[1].astype(bf), "dp", HALF_PAIRS)
-    total = (total[0] + f32(came)).reshape(cols, half, 16, BLK)
-    keep = jnp.where(first, total[:, :, :8], total[:, :, 8:])
-    send = jnp.where(first, total[:, :, 8:], total[:, :, :8])
-    grad_values = ordered(keep, lax.ppermute(send, "dp", CORE_PAIRS), 1)
-    grad_values = jnp.where(live[:, :, None, None], grad_values, jnp.zeros((), jnp.float32))
+    came = core_step(other)
 
     part = jax.ShapeDtypeStruct((NZ * own_blocks, tokens, BLK), bf)
+    half_part = jax.ShapeDtypeStruct((NZ * own_blocks // 2, tokens, BLK), bf)
     hidden_out, *parts = kernel_call(
         functools.partial(project, cols, half),
-        [jax.ShapeDtypeStruct(grad_out.shape, bf)] + [part] * NY,
-        [pltpu.VMEM((NZ * NY * own_blocks, tokens, BLK), jnp.float32)],
+        [jax.ShapeDtypeStruct(grad_out.shape, bf), part, part, half_part, half_part, part],
+        [pltpu.VMEM((blocks + 1, tokens, BLK), jnp.float32)],
         2 * flops,
         (pos, chip, whole, grad_out, w8, w8_other),
     )
-    came = [lax.ppermute(parts[p], "mp", y_pairs(-p)) for p in range(1, NY)]
-
-    def summed(q):
-        at = slice(q * own_blocks, (q + 1) * own_blocks)
-        return f32(parts[0][at]) + f32(came[0][at]) + f32(came[1][at]) + f32(came[2][at])
-
-    total = summed(0)
+
+    def over_x(zr, after=None):
+        sums = [(f32(mine[zr * NX + s]) + f32(came[zr * NX + s])).astype(bf) for s in range(NX)]
+        if after is not None:
+            sums = tie(sums, after)
+        n = sums[2].shape[0] // 2
+        return sum_passed(x_step, sums[0], sums[1], sums[2][:n], sums[2][n:], sums[3])
+
+    away = over_x(1).astype(bf)
+    total = over_x(0, away)
+    away = zh_step(away)
+    total = (total + f32(away)).reshape(cols, half, 16, BLK)
+    keep = jnp.where(first, total[:, :, :8], total[:, :, 8:])
+    send = jnp.where(first, total[:, :, 8:], total[:, :, :8])
+    grad_values = ordered(keep, core_step(send), 1)
+
+    rest = sum_passed(y_step, *parts)
+    total = rest[:own_blocks]
     for q in range(1, NZ):
-        total += f32(lax.ppermute(summed(q).astype(bf), "mp", z_pairs(-q)))
+        total += f32(z_step(rest[q * own_blocks : (q + 1) * own_blocks].astype(bf), -q))
     grad_acts = total.transpose(1, 0, 2).reshape(tokens, own_blocks * BLK).astype(bf)
     return hidden_out, grad_acts, grad_values
 

time: 184 us -> 119 us (0.65); the launches traced: 180 us -> 119 us
  waiting for transfers between devices: 117 us -> 34.6 us
  starting transfers between devices: 45.5 us -> 67.4 us
    ppermute x24 -> x34, waiting for transfers between devices: 117 us -> 34.6 us  [the longest x14 19 us: x_step(): return lax.ppermute(a, 'dp', x_pairs(s))]
    ppermute x24 -> x34, starting transfers between devices: 45.5 us -> 67.4 us  [the longest x14 26.1 us: x_step(): return lax.ppermute(a, 'dp', x_pairs(s))]
  transfers between devices with their start and end apart: 24 -> 34, of which waited for: 15 -> 14; matrix products, arithmetic and copies ran while one was open for 3% -> 5% of each run, Pallas kernels for 5% -> 7%
where the time goes in v2:
time: 119 us
  starting transfers between devices  67.4 us (57%)
  waiting for transfers between devices  34.6 us (29%)
  Pallas kernels  8.25 us (7%)
  other arithmetic  4.72 us (4%)
  local copies, waits for them, and re-layouts  2.95 us (2%)
    ppermute x14, starting transfers between devices, x_step(): return lax.ppermute(a, 'dp', x_pairs(s))  26.1 us
    ppermute x14, waiting for transfers between devices, x_step(): return lax.ppermute(a, 'dp', x_pairs(s))  19 us
    ppermute x2, starting transfers between devices, zh_step(): return lax.ppermute(a, 'dp', HALF_PAIRS)  17.9 us
    ppermute x6, starting transfers between devices, z_step(): return lax.ppermute(a, 'mp', z_pairs(q))  13.6 us
    ppermute x8, starting transfers between devices, y_step(): return lax.ppermute(a, 'mp', y_pairs(p))  8.77 us
    pallas_call x2, Pallas kernels, kernel_call(): pl.pallas_call(body, out_shape=outs, in_specs=specs, out_specs=[pl.BlockS...  8.25 us
    ppermute x6, waiting for transfers between devices, z_step(): return lax.ppermute(a, 'mp', z_pairs(q))  6.46 us
    ppermute x2, waiting for transfers between devices, zh_step(): return lax.ppermute(a, 'dp', HALF_PAIRS)  5.77 us
  transfers between devices with their start and end apart: 34, of which 14 were waited for; matrix products, arithmetic and copies ran while one was open for 5% of the time, Pallas kernels for 7%

profile of v2, /device:TPU:24, one launch (start us, length us, event | category | flops | bytes accessed | tf_op | source)
XLA Modules:
  0.0 119.0 jit_solution(18034525003084405941)
XLA Ops:
  0.6 1.0 copy.8
  1.8 4.7 %collective-permute-start.2 = (bf16[4,128,128]{2,1,0:T(8,128)(2,1)S(1)}, bf16[4,128,128]{2,1,0:T(8,128)(2,1)S(1)}, u32[]{:S(2)}, u32[]{:S(2)}) collective-permute-start(bf16[4,128,128]{2,1,0:T(8,128)(2,1)S(1)} %bitcast.62), channel_id=1, source_target_pairs={{0,12},{1,13},{2,14},{3,15},{4,0},{5,1},{6,2},{7,3},{8,4},{9,5},{1... | collective-permute-start | bytes 393224 | tf_op jit(solution)/shard_map/z_lo/ppermute | solution.py:113
  6.5 0.7 collective-permute-start
  7.2 1.0 broadcast_select_fusion.1
  8.3 0.8 fusion.20
  9.4 0.2 collective-permute-done.3
  9.7 5.5 %collective-permute-start.11 = (bf16[70,16,128]{2,1,0:T(8,128)(2,1)S(1)}, bf16[70,16,128]{2,1,0:T(8,128)(2,1)S(1)}, u32[]{:S(2)}, u32[]{:S(2)}) collective-permute-start(bf16[70,16,128]{2,1,0:T(8,128)(2,1)S(1)} %maximum_select_fusion.1), channel_id=1, source_target_pairs={{0,128},{16,144},{32,160},{48,176},{64,192},{80,208},{96,224},{112... | collective-permute-start | bytes 860168 | tf_op jit(solution)/shard_map/z_hi/ppermute | solution.py:128
  15.2 1.5 %collective-permute-start.8 = (bf16[70,16,128]{2,1,0:T(8,128)(2,1)S(1)}, bf16[70,16,128]{2,1,0:T(8,128)(2,1)S(1)}, u32[]{:S(2)}, u32[]{:S(2)}) collective-permute-start(bf16[70,16,128]{2,1,0:T(8,128)(2,1)S(1)} %maximum_select_fusion.1), channel_id=1, source_target_pairs={{0,32},{16,48},{32,64},{48,80},{64,96},{80,112},{96,0},{112,16},{1... | collective-permute-start | bytes 860168 | tf_op jit(solution)/shard_map/x/ppermute | solution.py:123
  16.7 1.0 collective-permute-done.1
  17.8 2.8 %collective-permute-start.10 = (bf16[70,16,128]{2,1,0:T(8,128)(2,1)S(1)}, bf16[70,16,128]{2,1,0:T(8,128)(2,1)S(1)}, u32[]{:S(2)}, u32[]{:S(2)}) collective-permute-start(bf16[70,16,128]{2,1,0:T(8,128)(2,1)S(1)} %maximum_select_fusion.1), channel_id=1, source_target_pairs={{0,96},{16,112},{32,0},{48,16},{64,32},{80,48},{96,64},{112,80},{1... | collective-permute-start | bytes 860168 | tf_op jit(solution)/shard_map/x/ppermute | solution.py:123
  20.6 0.8 collective-permute-start.9
  21.4 0.7 collective-permute-start.6
  22.3 5.8 %collective-permute-done.11 = bf16[70,16,128]{2,1,0:T(8,128)(2,1)S(1)} collective-permute-done((bf16[70,16,128]{2,1,0:T(8,128)(2,1)S(1)}, bf16[70,16,128]{2,1,0:T(8,128)(2,1)S(1)}, u32[]{:S(2)}, u32[]{:S(2)}) %collective-permute-start.11) | collective-permute-done | bytes 286752 | tf_op jit(solution)/shard_map/z_hi/ppermute | solution.py:128
  28.3 2.8 %collective-permute-start.14 = (bf16[70,16,128]{2,1,0:T(8,128)(2,1)S(1)}, bf16[70,16,128]{2,1,0:T(8,128)(2,1)S(1)}, u32[]{:S(2)}, u32[]{:S(2)}) collective-permute-start(bf16[70,16,128]{2,1,0:T(8,128)(2,1)S(1)} %collective-permute-done.11), channel_id=1, source_target_pairs={{0,96},{16,112},{32,0},{48,16},{64,32},{80,48},{96,64},{112,80},{1... | collective-permute-start | bytes 860168 | tf_op jit(solution)/shard_map/x/ppermute | solution.py:123
  31.1 1.1 collective-permute-done.9
  32.2 0.8 collective-permute-start.13
  33.2 4.3 %collective-permute-start.12 = (bf16[70,16,128]{2,1,0:T(8,128)(2,1)S(1)}, bf16[70,16,128]{2,1,0:T(8,128)(2,1)S(1)}, u32[]{:S(2)}, u32[]{:S(2)}) collective-permute-start(bf16[70,16,128]{2,1,0:T(8,128)(2,1)S(1)} %collective-permute-done.11), channel_id=1, source_target_pairs={{0,32},{16,48},{32,64},{48,80},{64,96},{80,112},{96,0},{112,16},{1... | collective-permute-start | bytes 860168 | tf_op jit(solution)/shard_map/x/ppermute | solution.py:123
  37.6 0.6 collective-permute-start.7
  38.2 2.6 %collective-permute-done.4 = bf16[16,128,128]{2,1,0:T(8,128)(2,1)S(1)} collective-permute-done((bf16[16,128,128]{2,1,0:T(8,128)(2,1)S(1)}, bf16[16,128,128]{2,1,0:T(8,128)(2,1)S(1)}, u32[]{:S(2)}, u32[]{:S(2)}) %collective-permute-start.4) | collective-permute-done | bytes 524320 | tf_op jit(solution)/shard_map/y/ppermute | solution.py:118
  40.9 1.6 %collective-permute-start.5 = (bf16[8,128,128]{2,1,0:T(8,128)(2,1)S(1)}, bf16[8,128,128]{2,1,0:T(8,128)(2,1)S(1)}, u32[]{:S(2)}, u32[]{:S(2)}) collective-permute-start(bf16[8,128,128]{2,1,0:T(8,128)(2,1)S(1)} %slice.203), channel_id=1, source_target_pairs={{0,1},{1,2},{2,3},{3,0},{4,5},{5,6},{6,7},{7,4},{8,9},{9,10},{10,1... | collective-permute-start | bytes 786440 | tf_op jit(solution)/shard_map/y/ppermute | solution.py:118
  42.5 5.2 %collective-permute-done.12 = bf16[70,16,128]{2,1,0:T(8,128)(2,1)S(1)} collective-permute-done((bf16[70,16,128]{2,1,0:T(8,128)(2,1)S(1)}, bf16[70,16,128]{2,1,0:T(8,128)(2,1)S(1)}, u32[]{:S(2)}, u32[]{:S(2)}) %collective-permute-start.12) | collective-permute-done | bytes 286752 | tf_op jit(solution)/shard_map/x/ppermute | solution.py:123
  47.9 0.3 collective-permute-start.15
  48.4 3.2 %shard_map.77 = (bf16[8,70,16,128]{3,2,1,0:T(8,128)(2,1)S(1)}, bf16[8,70,16,128]{3,2,1,0:T(8,128)(2,1)S(1)}) custom-call(s32[140]{0:T(256)S(1)} %pad_add_fusion.pos_ref, s32[8]{0:T(128)S(1)} %fusion.27.chip_ref, bf16[65,128,128]{2,1,0:T(8,128)(2,1)S(1)} %constant_dynamic-update-slice_fusion.acts_ref, bf16[128,896]{1,0:T(8,128)(2,1)S(1)} %copy-done), custom_call_target="tpu_custom_call" | custom-call | flops 587202560 | bytes 6947408 | tf_op jit(solution)/shard_map/pallas_call | solution.py:96
  51.6 0.6 collective-permute-start.23
  52.1 0.5 collective-permute-done.15.w1_ref
  52.6 5.1 %shard_map.76 = (bf16[128,896]{1,0:T(8,128)(2,1)}, bf16[16,128,128]{2,1,0:T(8,128)(2,1)S(1)}, bf16[16,128,128]{2,1,0:T(8,128)(2,1)S(1)}, bf16[8,128,128]{2,1,0:T...) custom-call(s32[140]{0:T(256)S(1)} %pad_add_fusion.pos_ref, s32[8]{0:T(128)S(1)} %fusion.27.chip_ref, ...), custom_call_target="tpu_custom_call" | custom-call | flops 1174405120 | bytes 9273936 | tf_op jit(solution)/shard_map/pallas_call | solution.py:96
  57.7 1.0 collective-permute-start.16
  58.7 1.1 collective-permute-start.18
  59.8 0.5 fusion.5
  60.4 0.5 collective-permute-start.24
  60.9 2.8 %collective-permute-start.26 = (bf16[35,16,128]{2,1,0:T(8,128)(2,1)S(1)}, bf16[35,16,128]{2,1,0:T(8,128)(2,1)S(1)}, u32[]{:S(2)}, u32[]{:S(2)}) collective-permute-start(bf16[35,16,128]{2,1,0:T(8,128)(2,1)S(1)} %get-tuple-element.49), channel_id=1, source_target_pairs={{0,96},{16,112},{32,0},{48,16},{64,32},{80,48},{96,64},{112,80},{1... | collective-permute-start | bytes 430088 | tf_op jit(solution)/shard_map/x/ppermute | solution.py:123
  63.7 2.8 %collective-permute-done.26 = bf16[35,16,128]{2,1,0:T(8,128)(2,1)S(1)} collective-permute-done((bf16[35,16,128]{2,1,0:T(8,128)(2,1)S(1)}, bf16[35,16,128]{2,1,0:T(8,128)(2,1)S(1)}, u32[]{:S(2)}, u32[]{:S(2)}) %collective-permute-start.26) | collective-permute-done | bytes 143392 | tf_op jit(solution)/shard_map/x/ppermute | solution.py:123
  66.6 3.6 %collective-permute-start.27 = (bf16[70,16,128]{2,1,0:T(8,128)(2,1)S(1)}, bf16[70,16,128]{2,1,0:T(8,128)(2,1)S(1)}, u32[]{:S(2)}, u32[]{:S(2)}) collective-permute-start(bf16[70,16,128]{2,1,0:T(8,128)(2,1)S(1)} %pad_maximum_fusion.4), channel_id=1, source_target_pairs={{0,96},{16,112},{32,0},{48,16},{64,32},{80,48},{96,64},{112,80},{1... | collective-permute-start | bytes 860168 | tf_op jit(solution)/shard_map/x/ppermute | solution.py:123
  70.5 0.8 collective-permute-start.19
  71.3 3.5 %collective-permute-done.27 = bf16[70,16,128]{2,1,0:T(8,128)(2,1)S(1)} collective-permute-done((bf16[70,16,128]{2,1,0:T(8,128)(2,1)S(1)}, bf16[70,16,128]{2,1,0:T(8,128)(2,1)S(1)}, u32[]{:S(2)}, u32[]{:S(2)}) %collective-permute-start.27) | collective-permute-done | bytes 286752 | tf_op jit(solution)/shard_map/x/ppermute | solution.py:123
  74.9 3.6 %collective-permute-done.25 = bf16[70,16,128]{2,1,0:T(8,128)(2,1)S(1)} collective-permute-done((bf16[70,16,128]{2,1,0:T(8,128)(2,1)S(1)}, bf16[70,16,128]{2,1,0:T(8,128)(2,1)S(1)}, u32[]{:S(2)}, u32[]{:S(2)}) %collective-permute-start.25) | collective-permute-done | bytes 286752 | tf_op jit(solution)/shard_map/x/ppermute | solution.py:123
  79.0 2.7 %collective-permute-start.17 = (bf16[16,128,128]{2,1,0:T(8,128)(2,1)S(1)}, bf16[16,128,128]{2,1,0:T(8,128)(2,1)S(1)}, u32[]{:S(2)}, u32[]{:S(2)}) collective-permute-start(bf16[16,128,128]{2,1,0:T(8,128)(2,1)S(1)} %pad_maximum_fusion.1), channel_id=1, source_target_pairs={{0,1},{1,2},{2,3},{3,0},{4,5},{5,6},{6,7},{7,4},{8,9},{9,10},{10,1... | collective-permute-start | bytes 1572872 | tf_op jit(solution)/shard_map/y/ppermute | solution.py:118
  81.7 12.4 %collective-permute-start.32 = (bf16[70,16,128]{2,1,0:T(8,128)(2,1)S(1)}, bf16[70,16,128]{2,1,0:T(8,128)(2,1)S(1)}, u32[]{:S(2)}, u32[]{:S(2)}) collective-permute-start(bf16[70,16,128]{2,1,0:T(8,128)(2,1)S(1)} %fusion.1), channel_id=1, source_target_pairs={{0,128},{16,144},{32,160},{48,176},{64,192},{80,208},{96,224},{112... | collective-permute-start | bytes 860168 | tf_op jit(solution)/shard_map/z_hi/ppermute | solution.py:128
  94.1 2.0 %collective-permute-start.28 = (bf16[35,16,128]{2,1,0:T(8,128)(2,1)S(1)}, bf16[35,16,128]{2,1,0:T(8,128)(2,1)S(1)}, u32[]{:S(2)}, u32[]{:S(2)}) collective-permute-start(bf16[35,16,128]{2,1,0:T(8,128)(2,1)S(1)} %get-tuple-element.46), channel_id=1, source_target_pairs={{0,32},{16,48},{32,64},{48,80},{64,96},{80,112},{96,0},{112,16},{1... | collective-permute-start | bytes 430088 | tf_op jit(solution)/shard_map/x/ppermute | solution.py:123
  96.2 1.6 %collective-permute-start.31 = (bf16[70,16,128]{2,1,0:T(8,128)(2,1)S(1)}, bf16[70,16,128]{2,1,0:T(8,128)(2,1)S(1)}, u32[]{:S(2)}, u32[]{:S(2)}) collective-permute-start(bf16[70,16,128]{2,1,0:T(8,128)(2,1)S(1)} %pad_maximum_fusion.6), channel_id=1, source_target_pairs={{0,96},{16,112},{32,0},{48,16},{64,32},{80,48},{96,64},{112,80},{1... | collective-permute-start | bytes 860168 | tf_op jit(solution)/shard_map/x/ppermute | solution.py:123
  97.8 2.7 %collective-permute-done.28 = bf16[35,16,128]{2,1,0:T(8,128)(2,1)S(1)} collective-permute-done((bf16[35,16,128]{2,1,0:T(8,128)(2,1)S(1)}, bf16[35,16,128]{2,1,0:T(8,128)(2,1)S(1)}, u32[]{:S(2)}, u32[]{:S(2)}) %collective-permute-start.28) | collective-permute-done | bytes 143392 | tf_op jit(solution)/shard_map/x/ppermute | solution.py:123
  100.6 2.3 %collective-permute-start.29 = (bf16[70,16,128]{2,1,0:T(8,128)(2,1)S(1)}, bf16[70,16,128]{2,1,0:T(8,128)(2,1)S(1)}, u32[]{:S(2)}, u32[]{:S(2)}) collective-permute-start(bf16[70,16,128]{2,1,0:T(8,128)(2,1)S(1)} %pad_maximum_fusion.5), channel_id=1, source_target_pairs={{0,32},{16,48},{32,64},{48,80},{64,96},{80,112},{96,0},{112,16},{1... | collective-permute-start | bytes 860168 | tf_op jit(solution)/shard_map/x/ppermute | solution.py:123
  103.3 4.2 %collective-permute-start.22 = (bf16[4,128,128]{2,1,0:T(8,128)(2,1)S(1)}, bf16[4,128,128]{2,1,0:T(8,128)(2,1)S(1)}, u32[]{:S(2)}, u32[]{:S(2)}) collective-permute-start(bf16[4,128,128]{2,1,0:T(8,128)(2,1)S(1)} %get-tuple-element.44), channel_id=1, source_target_pairs={{0,4},{1,5},{2,6},{3,7},{4,8},{5,9},{6,10},{7,11},{8,12},{9,13},{1... | collective-permute-start | bytes 393224 | tf_op jit(solution)/shard_map/z_lo/ppermute | solution.py:113
  107.5 4.0 %collective-permute-start.21 = (bf16[4,128,128]{2,1,0:T(8,128)(2,1)S(1)}, bf16[4,128,128]{2,1,0:T(8,128)(2,1)S(1)}, u32[]{:S(2)}, u32[]{:S(2)}) collective-permute-start(bf16[4,128,128]{2,1,0:T(8,128)(2,1)S(1)} %get-tuple-element.45), channel_id=1, source_target_pairs={{0,8},{1,9},{2,10},{3,11},{4,12},{5,13},{6,14},{7,15},{8,0},{9,1},... | collective-permute-start | bytes 393224 | tf_op jit(solution)/shard_map/z_lo/ppermute | solution.py:113
  111.8 3.6 %collective-permute-done.22 = bf16[4,128,128]{2,1,0:T(8,128)(2,1)S(1)} collective-permute-done((bf16[4,128,128]{2,1,0:T(8,128)(2,1)S(1)}, bf16[4,128,128]{2,1,0:T(8,128)(2,1)S(1)}, u32[]{:S(2)}, u32[]{:S(2)}) %collective-permute-start.22) | collective-permute-done | bytes 131104 | tf_op jit(solution)/shard_map/z_lo/ppermute | solution.py:113
  115.3 1.9 %collective-permute-done.21 = bf16[4,128,128]{2,1,0:T(8,128)(2,1)S(1)} collective-permute-done((bf16[4,128,128]{2,1,0:T(8,128)(2,1)S(1)}, bf16[4,128,128]{2,1,0:T(8,128)(2,1)S(1)}, u32[]{:S(2)}, u32[]{:S(2)}) %collective-permute-start.21) | collective-permute-done | bytes 131104 | tf_op jit(solution)/shard_map/z_lo/ppermute | solution.py:113
  117.4 0.8 copy.11
  118.2 0.8 maximum_select_fusion
  (81 shorter events, 3.6 us)
Async XLA Ops:
  1.8 14.9 %collective-permute-start.2 = (bf16[4,128,128]{2,1,0:T(8,128)(2,1)S(1)}, bf16[4,128,128]{2,1,0:T(8,128)(2,1)S(1)}, u32[]{:S(2)}, u32[]{:S(2)}) collective-permute-start(bf16[4,128,128]{2,1,0:T(8,128)(2,1)S(1)} %bitcast.62), channel_id=1, source_target_pairs={{0,12},{1,13},{2,14},{3,15},{4,0},{5,1},{6,2},{7,3},{8,4},{9,5},{1... | collective-permute-start | bytes 393224 | tf_op jit(solution)/shard_map/z_lo/ppermute | solution.py:113
  6.5 11.2 %collective-permute-start.1 = (bf16[4,128,128]{2,1,0:T(8,128)(2,1)S(1)}, bf16[4,128,128]{2,1,0:T(8,128)(2,1)S(1)}, u32[]{:S(2)}, u32[]{:S(2)}) collective-permute-start(bf16[4,128,128]{2,1,0:T(8,128)(2,1)S(1)} %bitcast.63), channel_id=1, source_target_pairs={{0,8},{1,9},{2,10},{3,11},{4,12},{5,13},{6,14},{7,15},{8,0},{9,1},... | collective-permute-start | bytes 393224 | tf_op jit(solution)/shard_map/z_lo/ppermute | solution.py:113
  6.5 11.2 %collective-permute-start = (bf16[4,128,128]{2,1,0:T(8,128)(2,1)S(1)}, bf16[4,128,128]{2,1,0:T(8,128)(2,1)S(1)}, u32[]{:S(2)}, u32[]{:S(2)}) collective-permute-start(bf16[4,128,128]{2,1,0:T(8,128)(2,1)S(1)} %bitcast.64), channel_id=1, source_target_pairs={{0,4},{1,5},{2,6},{3,7},{4,8},{5,9},{6,10},{7,11},{8,12},{9,13},{1... | collective-permute-start | bytes 393224 | tf_op jit(solution)/shard_map/z_lo/ppermute | solution.py:113
  8.2 1.5 %collective-permute-start.3 = (bf16[7,10,8,128]{3,2,1,0:T(8,128)(2,1)S(1)}, bf16[7,10,8,128]{3,2,1,0:T(8,128)(2,1)S(1)}, u32[]{:S(2)}, u32[]{:S(2)}) collective-permute-start(bf16[7,10,8,128]{3,2,1,0:T(8,128)(2,1)S(1)} %get-tuple-element.51), channel_id=1, source_target_pairs={{0,16},{16,0},{32,48},{48,32},{64,80},{80,64},{96,112},{112,96},{1... | collective-permute-start | bytes 430088 | tf_op jit(solution)/shard_map/core/ppermute | solution.py:133
  9.7 18.4 %collective-permute-start.11 = (bf16[70,16,128]{2,1,0:T(8,128)(2,1)S(1)}, bf16[70,16,128]{2,1,0:T(8,128)(2,1)S(1)}, u32[]{:S(2)}, u32[]{:S(2)}) collective-permute-start(bf16[70,16,128]{2,1,0:T(8,128)(2,1)S(1)} %maximum_select_fusion.1), channel_id=1, source_target_pairs={{0,128},{16,144},{32,160},{48,176},{64,192},{80,208},{96,224},{112... | collective-permute-start | bytes 860168 | tf_op jit(solution)/shard_map/z_hi/ppermute | solution.py:128
  15.2 13.1 %collective-permute-start.8 = (bf16[70,16,128]{2,1,0:T(8,128)(2,1)S(1)}, bf16[70,16,128]{2,1,0:T(8,128)(2,1)S(1)}, u32[]{:S(2)}, u32[]{:S(2)}) collective-permute-start(bf16[70,16,128]{2,1,0:T(8,128)(2,1)S(1)} %maximum_select_fusion.1), channel_id=1, source_target_pairs={{0,32},{16,48},{32,64},{48,80},{64,96},{80,112},{96,0},{112,16},{1... | collective-permute-start | bytes 860168 | tf_op jit(solution)/shard_map/x/ppermute | solution.py:123
  17.8 15.4 %collective-permute-start.10 = (bf16[70,16,128]{2,1,0:T(8,128)(2,1)S(1)}, bf16[70,16,128]{2,1,0:T(8,128)(2,1)S(1)}, u32[]{:S(2)}, u32[]{:S(2)}) collective-permute-start(bf16[70,16,128]{2,1,0:T(8,128)(2,1)S(1)} %maximum_select_fusion.1), channel_id=1, source_target_pairs={{0,96},{16,112},{32,0},{48,16},{64,32},{80,48},{96,64},{112,80},{1... | collective-permute-start | bytes 860168 | tf_op jit(solution)/shard_map/x/ppermute | solution.py:123
  20.6 11.6 %collective-permute-start.9 = (bf16[70,16,128]{2,1,0:T(8,128)(2,1)S(1)}, bf16[70,16,128]{2,1,0:T(8,128)(2,1)S(1)}, u32[]{:S(2)}, u32[]{:S(2)}) collective-permute-start(bf16[70,16,128]{2,1,0:T(8,128)(2,1)S(1)} %maximum_select_fusion.1), channel_id=1, source_target_pairs={{0,64},{16,80},{32,96},{48,112},{64,0},{80,16},{96,32},{112,48},{1... | collective-permute-start | bytes 860168 | tf_op jit(solution)/shard_map/x/ppermute | solution.py:123
  21.4 16.2 %collective-permute-start.6 = (bf16[16,128,128]{2,1,0:T(8,128)(2,1)S(1)}, bf16[16,128,128]{2,1,0:T(8,128)(2,1)S(1)}, u32[]{:S(2)}, u32[]{:S(2)}) collective-permute-start(bf16[16,128,128]{2,1,0:T(8,128)(2,1)S(1)} %pad_maximum_fusion), channel_id=1, source_target_pairs={{0,3},{1,0},{2,1},{3,2},{4,7},{5,4},{6,5},{7,6},{8,11},{9,8},{10,9... | collective-permute-start | bytes 1572872 | tf_op jit(solution)/shard_map/y/ppermute | solution.py:118
  28.1 12.8 %collective-permute-start.4 = (bf16[16,128,128]{2,1,0:T(8,128)(2,1)S(1)}, bf16[16,128,128]{2,1,0:T(8,128)(2,1)S(1)}, u32[]{:S(2)}, u32[]{:S(2)}) collective-permute-start(bf16[16,128,128]{2,1,0:T(8,128)(2,1)S(1)} %pad_maximum_fusion), channel_id=1, source_target_pairs={{0,1},{1,2},{2,3},{3,0},{4,5},{5,6},{6,7},{7,4},{8,9},{9,10},{10,1... | collective-permute-start | bytes 1572872 | tf_op jit(solution)/shard_map/y/ppermute | solution.py:118
  28.3 19.5 %collective-permute-start.14 = (bf16[70,16,128]{2,1,0:T(8,128)(2,1)S(1)}, bf16[70,16,128]{2,1,0:T(8,128)(2,1)S(1)}, u32[]{:S(2)}, u32[]{:S(2)}) collective-permute-start(bf16[70,16,128]{2,1,0:T(8,128)(2,1)S(1)} %collective-permute-done.11), channel_id=1, source_target_pairs={{0,96},{16,112},{32,0},{48,16},{64,32},{80,48},{96,64},{112,80},{1... | collective-permute-start | bytes 860168 | tf_op jit(solution)/shard_map/x/ppermute | solution.py:123
  32.2 15.5 %collective-permute-start.13 = (bf16[70,16,128]{2,1,0:T(8,128)(2,1)S(1)}, bf16[70,16,128]{2,1,0:T(8,128)(2,1)S(1)}, u32[]{:S(2)}, u32[]{:S(2)}) collective-permute-start(bf16[70,16,128]{2,1,0:T(8,128)(2,1)S(1)} %collective-permute-done.11), channel_id=1, source_target_pairs={{0,64},{16,80},{32,96},{48,112},{64,0},{80,16},{96,32},{112,48},{1... | collective-permute-start | bytes 860168 | tf_op jit(solution)/shard_map/x/ppermute | solution.py:123
  33.2 14.5 %collective-permute-start.12 = (bf16[70,16,128]{2,1,0:T(8,128)(2,1)S(1)}, bf16[70,16,128]{2,1,0:T(8,128)(2,1)S(1)}, u32[]{:S(2)}, u32[]{:S(2)}) collective-permute-start(bf16[70,16,128]{2,1,0:T(8,128)(2,1)S(1)} %collective-permute-done.11), channel_id=1, source_target_pairs={{0,32},{16,48},{32,64},{48,80},{64,96},{80,112},{96,0},{112,16},{1... | collective-permute-start | bytes 860168 | tf_op jit(solution)/shard_map/x/ppermute | solution.py:123
  37.6 10.6 %collective-permute-start.7 = (bf16[8,128,128]{2,1,0:T(8,128)(2,1)S(1)}, bf16[8,128,128]{2,1,0:T(8,128)(2,1)S(1)}, u32[]{:S(2)}, u32[]{:S(2)}) collective-permute-start(bf16[8,128,128]{2,1,0:T(8,128)(2,1)S(1)} %slice.204), channel_id=1, source_target_pairs={{0,3},{1,0},{2,1},{3,2},{4,7},{5,4},{6,5},{7,6},{8,11},{9,8},{10,9... | collective-permute-start | bytes 786440 | tf_op jit(solution)/shard_map/y/ppermute | solution.py:118
  40.9 7.5 %copy-start = (bf16[128,896]{1,0:T(8,128)(2,1)S(1)}, bf16[128,896]{1,0:T(8,128)(2,1)}, u32[]{:S(2)}) copy-start(bf16[128,896]{1,0:T(8,128)(2,1)} %up_ref.3) | copy-start | bytes 688132
  40.9 7.3 %collective-permute-start.5 = (bf16[8,128,128]{2,1,0:T(8,128)(2,1)S(1)}, bf16[8,128,128]{2,1,0:T(8,128)(2,1)S(1)}, u32[]{:S(2)}, u32[]{:S(2)}) collective-permute-start(bf16[8,128,128]{2,1,0:T(8,128)(2,1)S(1)} %slice.203), channel_id=1, source_target_pairs={{0,1},{1,2},{2,3},{3,0},{4,5},{5,6},{6,7},{7,4},{8,9},{9,10},{10,1... | collective-permute-start | bytes 786440 | tf_op jit(solution)/shard_map/y/ppermute | solution.py:118
  47.9 4.7 %collective-permute-start.15 = (bf16[8,70,16,128]{3,2,1,0:T(8,128)(2,1)S(1)}, bf16[8,70,16,128]{3,2,1,0:T(8,128)(2,1)S(1)}, u32[]{:S(2)}, u32[]{:S(2)}) collective-permute-start(bf16[8,70,16,128]{3,2,1,0:T(8,128)(2,1)S(1)} %bitcast_dynamic-update-slice_fusion.w0_ref), channel_id=1, source_target_pairs={{0,16},{16,0},{32,48},{48,32},{64,80},{80,64},{96,112},{112,96},{1... | collective-permute-start | bytes 6881288 | tf_op jit(solution)/shard_map/core/ppermute | solution.py:133
  51.6 8.3 %collective-permute-start.23 = (bf16[8,70,16,128]{3,2,1,0:T(8,128)(2,1)S(1)}, bf16[8,70,16,128]{3,2,1,0:T(8,128)(2,1)S(1)}, u32[]{:S(2)}, u32[]{:S(2)}) collective-permute-start(bf16[8,70,16,128]{3,2,1,0:T(8,128)(2,1)S(1)} %get-tuple-element.24), channel_id=1, source_target_pairs={{0,16},{16,0},{32,48},{48,32},{64,80},{80,64},{96,112},{112,96},{1... | collective-permute-start | bytes 6881288 | tf_op jit(solution)/shard_map/core/ppermute | solution.py:133
  57.7 21.1 %collective-permute-start.16 = (bf16[8,128,128]{2,1,0:T(8,128)(2,1)S(1)}, bf16[8,128,128]{2,1,0:T(8,128)(2,1)S(1)}, u32[]{:S(2)}, u32[]{:S(2)}) collective-permute-start(bf16[8,128,128]{2,1,0:T(8,128)(2,1)S(1)} %get-tuple-element.20), channel_id=1, source_target_pairs={{0,1},{1,2},{2,3},{3,0},{4,5},{5,6},{6,7},{7,4},{8,9},{9,10},{10,1... | collective-permute-start | bytes 786440 | tf_op jit(solution)/shard_map/y/ppermute | solution.py:118
  58.7 11.6 %collective-permute-start.18 = (bf16[8,128,128]{2,1,0:T(8,128)(2,1)S(1)}, bf16[8,128,128]{2,1,0:T(8,128)(2,1)S(1)}, u32[]{:S(2)}, u32[]{:S(2)}) collective-permute-start(bf16[8,128,128]{2,1,0:T(8,128)(2,1)S(1)} %get-tuple-element.22), channel_id=1, source_target_pairs={{0,3},{1,0},{2,1},{3,2},{4,7},{5,4},{6,5},{7,6},{8,11},{9,8},{10,9... | collective-permute-start | bytes 786440 | tf_op jit(solution)/shard_map/y/ppermute | solution.py:118
  60.4 9.8 %collective-permute-start.24 = (bf16[35,16,128]{2,1,0:T(8,128)(2,1)S(1)}, bf16[35,16,128]{2,1,0:T(8,128)(2,1)S(1)}, u32[]{:S(2)}, u32[]{:S(2)}) collective-permute-start(bf16[35,16,128]{2,1,0:T(8,128)(2,1)S(1)} %get-tuple-element.48), channel_id=1, source_target_pairs={{0,32},{16,48},{32,64},{48,80},{64,96},{80,112},{96,0},{112,16},{1... | collective-permute-start | bytes 430088 | tf_op jit(solution)/shard_map/x/ppermute | solution.py:123
  60.9 5.6 %collective-permute-start.26 = (bf16[35,16,128]{2,1,0:T(8,128)(2,1)S(1)}, bf16[35,16,128]{2,1,0:T(8,128)(2,1)S(1)}, u32[]{:S(2)}, u32[]{:S(2)}) collective-permute-start(bf16[35,16,128]{2,1,0:T(8,128)(2,1)S(1)} %get-tuple-element.49), channel_id=1, source_target_pairs={{0,96},{16,112},{32,0},{48,16},{64,32},{80,48},{96,64},{112,80},{1... | collective-permute-start | bytes 430088 | tf_op jit(solution)/shard_map/x/ppermute | solution.py:123
  66.6 8.3 %collective-permute-start.27 = (bf16[70,16,128]{2,1,0:T(8,128)(2,1)S(1)}, bf16[70,16,128]{2,1,0:T(8,128)(2,1)S(1)}, u32[]{:S(2)}, u32[]{:S(2)}) collective-permute-start(bf16[70,16,128]{2,1,0:T(8,128)(2,1)S(1)} %pad_maximum_fusion.4), channel_id=1, source_target_pairs={{0,96},{16,112},{32,0},{48,16},{64,32},{80,48},{96,64},{112,80},{1... | collective-permute-start | bytes 860168 | tf_op jit(solution)/shard_map/x/ppermute | solution.py:123
  70.3 8.2 %collective-permute-start.25 = (bf16[70,16,128]{2,1,0:T(8,128)(2,1)S(1)}, bf16[70,16,128]{2,1,0:T(8,128)(2,1)S(1)}, u32[]{:S(2)}, u32[]{:S(2)}) collective-permute-start(bf16[70,16,128]{2,1,0:T(8,128)(2,1)S(1)} %pad_maximum_fusion.3), channel_id=1, source_target_pairs={{0,32},{16,48},{32,64},{48,80},{64,96},{80,112},{96,0},{112,16},{1... | collective-permute-start | bytes 860168 | tf_op jit(solution)/shard_map/x/ppermute | solution.py:123
  70.5 32.4 %collective-permute-start.19 = (bf16[16,128,128]{2,1,0:T(8,128)(2,1)S(1)}, bf16[16,128,128]{2,1,0:T(8,128)(2,1)S(1)}, u32[]{:S(2)}, u32[]{:S(2)}) collective-permute-start(bf16[16,128,128]{2,1,0:T(8,128)(2,1)S(1)} %pad_maximum_fusion.2), channel_id=1, source_target_pairs={{0,3},{1,0},{2,1},{3,2},{4,7},{5,4},{6,5},{7,6},{8,11},{9,8},{10,9... | collective-permute-start | bytes 1572872 | tf_op jit(solution)/shard_map/y/ppermute | solution.py:118
  78.7 17.5 %collective-permute-start.30 = (bf16[35,16,128]{2,1,0:T(8,128)(2,1)S(1)}, bf16[35,16,128]{2,1,0:T(8,128)(2,1)S(1)}, u32[]{:S(2)}, u32[]{:S(2)}) collective-permute-start(bf16[35,16,128]{2,1,0:T(8,128)(2,1)S(1)} %get-tuple-element.47), channel_id=1, source_target_pairs={{0,96},{16,112},{32,0},{48,16},{64,32},{80,48},{96,64},{112,80},{1... | collective-permute-start | bytes 430088 | tf_op jit(solution)/shard_map/x/ppermute | solution.py:123
  79.0 23.9 %collective-permute-start.17 = (bf16[16,128,128]{2,1,0:T(8,128)(2,1)S(1)}, bf16[16,128,128]{2,1,0:T(8,128)(2,1)S(1)}, u32[]{:S(2)}, u32[]{:S(2)}) collective-permute-start(bf16[16,128,128]{2,1,0:T(8,128)(2,1)S(1)} %pad_maximum_fusion.1), channel_id=1, source_target_pairs={{0,1},{1,2},{2,3},{3,0},{4,5},{5,6},{6,7},{7,4},{8,9},{9,10},{10,1... | collective-permute-start | bytes 1572872 | tf_op jit(solution)/shard_map/y/ppermute | solution.py:118
  81.7 25.7 %collective-permute-start.32 = (bf16[70,16,128]{2,1,0:T(8,128)(2,1)S(1)}, bf16[70,16,128]{2,1,0:T(8,128)(2,1)S(1)}, u32[]{:S(2)}, u32[]{:S(2)}) collective-permute-start(bf16[70,16,128]{2,1,0:T(8,128)(2,1)S(1)} %fusion.1), channel_id=1, source_target_pairs={{0,128},{16,144},{32,160},{48,176},{64,192},{80,208},{96,224},{112... | collective-permute-start | bytes 860168 | tf_op jit(solution)/shard_map/z_hi/ppermute | solution.py:128
  94.1 6.4 %collective-permute-start.28 = (bf16[35,16,128]{2,1,0:T(8,128)(2,1)S(1)}, bf16[35,16,128]{2,1,0:T(8,128)(2,1)S(1)}, u32[]{:S(2)}, u32[]{:S(2)}) collective-permute-start(bf16[35,16,128]{2,1,0:T(8,128)(2,1)S(1)} %get-tuple-element.46), channel_id=1, source_target_pairs={{0,32},{16,48},{32,64},{48,80},{64,96},{80,112},{96,0},{112,16},{1... | collective-permute-start | bytes 430088 | tf_op jit(solution)/shard_map/x/ppermute | solution.py:123
  96.2 15.2 %collective-permute-start.31 = (bf16[70,16,128]{2,1,0:T(8,128)(2,1)S(1)}, bf16[70,16,128]{2,1,0:T(8,128)(2,1)S(1)}, u32[]{:S(2)}, u32[]{:S(2)}) collective-permute-start(bf16[70,16,128]{2,1,0:T(8,128)(2,1)S(1)} %pad_maximum_fusion.6), channel_id=1, source_target_pairs={{0,96},{16,112},{32,0},{48,16},{64,32},{80,48},{96,64},{112,80},{1... | collective-permute-start | bytes 860168 | tf_op jit(solution)/shard_map/x/ppermute | solution.py:123
  100.6 10.8 %collective-permute-start.29 = (bf16[70,16,128]{2,1,0:T(8,128)(2,1)S(1)}, bf16[70,16,128]{2,1,0:T(8,128)(2,1)S(1)}, u32[]{:S(2)}, u32[]{:S(2)}) collective-permute-start(bf16[70,16,128]{2,1,0:T(8,128)(2,1)S(1)} %pad_maximum_fusion.5), channel_id=1, source_target_pairs={{0,32},{16,48},{32,64},{48,80},{64,96},{80,112},{96,0},{112,16},{1... | collective-permute-start | bytes 860168 | tf_op jit(solution)/shard_map/x/ppermute | solution.py:123
  103.2 8.5 %collective-permute-start.20 = (bf16[4,128,128]{2,1,0:T(8,128)(2,1)S(1)}, bf16[4,128,128]{2,1,0:T(8,128)(2,1)S(1)}, u32[]{:S(2)}, u32[]{:S(2)}) collective-permute-start(bf16[4,128,128]{2,1,0:T(8,128)(2,1)S(1)} %get-tuple-element.43), channel_id=1, source_target_pairs={{0,12},{1,13},{2,14},{3,15},{4,0},{5,1},{6,2},{7,3},{8,4},{9,5},{1... | collective-permute-start | bytes 393224 | tf_op jit(solution)/shard_map/z_lo/ppermute | solution.py:113
  103.3 12.0 %collective-permute-start.22 = (bf16[4,128,128]{2,1,0:T(8,128)(2,1)S(1)}, bf16[4,128,128]{2,1,0:T(8,128)(2,1)S(1)}, u32[]{:S(2)}, u32[]{:S(2)}) collective-permute-start(bf16[4,128,128]{2,1,0:T(8,128)(2,1)S(1)} %get-tuple-element.44), channel_id=1, source_target_pairs={{0,4},{1,5},{2,6},{3,7},{4,8},{5,9},{6,10},{7,11},{8,12},{9,13},{1... | collective-permute-start | bytes 393224 | tf_op jit(solution)/shard_map/z_lo/ppermute | solution.py:113
  107.5 9.7 %collective-permute-start.21 = (bf16[4,128,128]{2,1,0:T(8,128)(2,1)S(1)}, bf16[4,128,128]{2,1,0:T(8,128)(2,1)S(1)}, u32[]{:S(2)}, u32[]{:S(2)}) collective-permute-start(bf16[4,128,128]{2,1,0:T(8,128)(2,1)S(1)} %get-tuple-element.45), channel_id=1, source_target_pairs={{0,8},{1,9},{2,10},{3,11},{4,12},{5,13},{6,14},{7,15},{8,0},{9,1},... | collective-permute-start | bytes 393224 | tf_op jit(solution)/shard_map/z_lo/ppermute | solution.py:113
  111.6 6.5 %collective-permute-start.33 = (f32[7,10,8,128]{3,2,1,0:T(8,128)S(1)}, f32[7,10,8,128]{3,2,1,0:T(8,128)S(1)}, u32[]{:S(2)}, u32[]{:S(2)}) collective-permute-start(f32[7,10,8,128]{3,2,1,0:T(8,128)S(1)} %get-tuple-element.42), channel_id=1, source_target_pairs={{0,16},{16,0},{32,48},{48,32},{64,80},{80,64},{96,112},{112,96},{1... | collective-permute-start | bytes 860168 | tf_op jit(solution)/shard_map/core/ppermute | solution.py:133

commit v3 on v2

--- a/solution.py
+++ b/solution.py
@@ -11,7 +11,7 @@
 NY = 4
 NX = 4
 BLK = 128
-VMEM_LIMIT = 40 * 1024 * 1024
+VMEM_LIMIT = 16 * 1024 * 1024
 
 
 def y_pairs(shift):
@@ -199,9 +199,11 @@
     own = acts.reshape(tokens, own_blocks, BLK).transpose(1, 0, 2)
     along_z = jnp.concatenate([own] + [z_step(own, q) for q in range(1, NZ)])
     far16 = zh_step(rows16)
-    near = gather_direct(x_step, rows16)
+    near1, near3 = x_step(rows16, 1), x_step(rows16, 3)
     along_z = tie(along_z, rows16)
     whole = gather_passed(y_step, along_z)
+    n = rows16.shape[0] // 2
+    near = [rows16, near1, jnp.concatenate([x_step(near1[:n], 1), x_step(near3[n:], -1)]), near3]
     far = gather_direct(x_step, far16)
     whole = jnp.concatenate(whole + [jnp.zeros((1, tokens, BLK), bf)])
     w8 = jnp.stack(near + far)

time: 119 us -> 118 us (level)
  starting transfers between devices: 67.4 us -> 65.7 us
    ppermute x14 -> x15, waiting for transfers between devices: 19 us -> 28.4 us  [x_step(): return lax.ppermute(a, 'dp', x_pairs(s))]
    ppermute x2, waiting for transfers between devices: 5.77 us -> 0.01 us  [zh_step(): return lax.ppermute(a, 'dp', HALF_PAIRS)]
    ppermute x8, starting transfers between devices: 8.77 us -> 12.1 us  [y_step(): return lax.ppermute(a, 'mp', y_pairs(p))]
    ppermute x8, waiting for transfers between devices: 2.66 us -> 0.02 us  [y_step(): return lax.ppermute(a, 'mp', y_pairs(p))]
    ppermute x14 -> x15, starting transfers between devices: 26.1 us -> 24 us  [x_step(): return lax.ppermute(a, 'dp', x_pairs(s))]
    ppermute x2, starting transfers between devices: 17.9 us -> 15.9 us  [zh_step(): return lax.ppermute(a, 'dp', HALF_PAIRS)]
  transfers between devices with their start and end apart: 34 -> 35, of which waited for: 14 -> 11; matrix products, arithmetic and copies ran while one was open for 5% -> 5% of each run, Pallas kernels for 7% -> 7%
where the time goes in v3:
time: 118 us
  starting transfers between devices  65.7 us (56%)
  waiting for transfers between devices  34.8 us (29%)
  Pallas kernels  8.23 us (7%)
  other arithmetic  4.76 us (4%)
  local copies, waits for them, and re-layouts  2.93 us (2%)
    ppermute x15, waiting for transfers between devices, x_step(): return lax.ppermute(a, 'dp', x_pairs(s))  28.4 us
    ppermute x15, starting transfers between devices, x_step(): return lax.ppermute(a, 'dp', x_pairs(s))  24 us
    ppermute x2, starting transfers between devices, zh_step(): return lax.ppermute(a, 'dp', HALF_PAIRS)  15.9 us
    ppermute x6, starting transfers between devices, z_step(): return lax.ppermute(a, 'mp', z_pairs(q))  12.8 us
    ppermute x8, starting transfers between devices, y_step(): return lax.ppermute(a, 'mp', y_pairs(p))  12.1 us
    pallas_call x2, Pallas kernels, kernel_call(): pl.pallas_call(body, out_shape=outs, in_specs=specs, out_specs=[pl.BlockS...  8.23 us
    ppermute x6, waiting for transfers between devices, z_step(): return lax.ppermute(a, 'mp', z_pairs(q))  5.66 us
  transfers between devices with their start and end apart: 35, of which 11 were waited for; matrix products, arithmetic and copies ran while one was open for 5% of the time, Pallas kernels for 7%

profile of v3, /device:TPU:24, one launch (start us, length us, event | category | flops | bytes accessed | tf_op | source)
XLA Modules:
  0.0 117.5 jit_solution(7069389296469701588)
XLA Ops:
  0.6 1.0 copy.8
  1.7 0.1 copy.9
  1.8 4.7 %collective-permute-start.2 = (bf16[4,128,128]{2,1,0:T(8,128)(2,1)S(1)}, bf16[4,128,128]{2,1,0:T(8,128)(2,1)S(1)}, u32[]{:S(2)}, u32[]{:S(2)}) collective-permute-start(bf16[4,128,128]{2,1,0:T(8,128)(2,1)S(1)} %bitcast.64), channel_id=1, source_target_pairs={{0,12},{1,13},{2,14},{3,15},{4,0},{5,1},{6,2},{7,3},{8,4},{9,5},{1... | collective-permute-start | bytes 393224 | tf_op jit(solution)/shard_map/z_lo/ppermute | solution.py:113
  6.5 0.7 collective-permute-start
  7.2 1.0 broadcast_select_fusion.1
  8.2 0.1 collective-permute-start.3
  8.3 0.8 fusion.21
  9.4 0.2 collective-permute-done.3
  9.7 5.5 %collective-permute-start.12 = (bf16[70,16,128]{2,1,0:T(8,128)(2,1)S(1)}, bf16[70,16,128]{2,1,0:T(8,128)(2,1)S(1)}, u32[]{:S(2)}, u32[]{:S(2)}) collective-permute-start(bf16[70,16,128]{2,1,0:T(8,128)(2,1)S(1)} %maximum_select_fusion.1), channel_id=1, source_target_pairs={{0,128},{16,144},{32,160},{48,176},{64,192},{80,208},{96,224},{112... | collective-permute-start | bytes 860168 | tf_op jit(solution)/shard_map/z_hi/ppermute | solution.py:128
  15.2 2.8 %collective-permute-start.10 = (bf16[70,16,128]{2,1,0:T(8,128)(2,1)S(1)}, bf16[70,16,128]{2,1,0:T(8,128)(2,1)S(1)}, u32[]{:S(2)}, u32[]{:S(2)}) collective-permute-start(bf16[70,16,128]{2,1,0:T(8,128)(2,1)S(1)} %maximum_select_fusion.1), channel_id=1, source_target_pairs={{0,96},{16,112},{32,0},{48,16},{64,32},{80,48},{96,64},{112,80},{1... | collective-permute-start | bytes 860168 | tf_op jit(solution)/shard_map/x/ppermute | solution.py:123
  18.1 0.8 collective-permute-start.6
  18.9 2.5 %collective-permute-start.4 = (bf16[16,128,128]{2,1,0:T(8,128)(2,1)S(1)}, bf16[16,128,128]{2,1,0:T(8,128)(2,1)S(1)}, u32[]{:S(2)}, u32[]{:S(2)}) collective-permute-start(bf16[16,128,128]{2,1,0:T(8,128)(2,1)S(1)} %pad_maximum_fusion), channel_id=1, source_target_pairs={{0,1},{1,2},{2,3},{3,0},{4,5},{5,6},{6,7},{7,4},{8,9},{9,10},{10,1... | collective-permute-start | bytes 1572872 | tf_op jit(solution)/shard_map/y/ppermute | solution.py:118
  21.5 2.7 %collective-permute-done.10 = bf16[70,16,128]{2,1,0:T(8,128)(2,1)S(1)} collective-permute-done((bf16[70,16,128]{2,1,0:T(8,128)(2,1)S(1)}, bf16[70,16,128]{2,1,0:T(8,128)(2,1)S(1)}, u32[]{:S(2)}, u32[]{:S(2)}) %collective-permute-start.10) | collective-permute-done | bytes 286752 | tf_op jit(solution)/shard_map/x/ppermute | solution.py:123
  24.2 3.8 %collective-permute-start.11 = (bf16[35,16,128]{2,1,0:T(8,128)(2,1)S(1)}, bf16[35,16,128]{2,1,0:T(8,128)(2,1)S(1)}, u32[]{:S(2)}, u32[]{:S(2)}) collective-permute-start(bf16[35,16,128]{2,1,0:T(8,128)(2,1)S(1)} %slice.214), channel_id=1, source_target_pairs={{0,96},{16,112},{32,0},{48,16},{64,32},{80,48},{96,64},{112,80},{1... | collective-permute-start | bytes 430088 | tf_op jit(solution)/shard_map/x/ppermute | solution.py:123
  28.1 3.2 %collective-permute-start.15 = (bf16[70,16,128]{2,1,0:T(8,128)(2,1)S(1)}, bf16[70,16,128]{2,1,0:T(8,128)(2,1)S(1)}, u32[]{:S(2)}, u32[]{:S(2)}) collective-permute-start(bf16[70,16,128]{2,1,0:T(8,128)(2,1)S(1)} %collective-permute-done.12), channel_id=1, source_target_pairs={{0,96},{16,112},{32,0},{48,16},{64,32},{80,48},{96,64},{112,80},{1... | collective-permute-start | bytes 860168 | tf_op jit(solution)/shard_map/x/ppermute | solution.py:123
  31.4 1.2 collective-permute-start.14
  32.5 6.6 %collective-permute-done.9 = bf16[35,16,128]{2,1,0:T(8,128)(2,1)S(1)} collective-permute-done((bf16[35,16,128]{2,1,0:T(8,128)(2,1)S(1)}, bf16[35,16,128]{2,1,0:T(8,128)(2,1)S(1)}, u32[]{:S(2)}, u32[]{:S(2)}) %collective-permute-start.9) | collective-permute-done | bytes 143392 | tf_op jit(solution)/shard_map/x/ppermute | solution.py:123
  39.3 0.8 collective-permute-start.7
  40.2 2.8 %collective-permute-start.5 = (bf16[8,128,128]{2,1,0:T(8,128)(2,1)S(1)}, bf16[8,128,128]{2,1,0:T(8,128)(2,1)S(1)}, u32[]{:S(2)}, u32[]{:S(2)}) collective-permute-start(bf16[8,128,128]{2,1,0:T(8,128)(2,1)S(1)} %slice.211), channel_id=1, source_target_pairs={{0,1},{1,2},{2,3},{3,0},{4,5},{5,6},{6,7},{7,4},{8,9},{9,10},{10,1... | collective-permute-start | bytes 786440 | tf_op jit(solution)/shard_map/y/ppermute | solution.py:118
  43.0 4.0 %collective-permute-done.13 = bf16[70,16,128]{2,1,0:T(8,128)(2,1)S(1)} collective-permute-done((bf16[70,16,128]{2,1,0:T(8,128)(2,1)S(1)}, bf16[70,16,128]{2,1,0:T(8,128)(2,1)S(1)}, u32[]{:S(2)}, u32[]{:S(2)}) %collective-permute-start.13) | collective-permute-done | bytes 286752 | tf_op jit(solution)/shard_map/x/ppermute | solution.py:123
  47.4 3.2 %shard_map.77 = (bf16[8,70,16,128]{3,2,1,0:T(8,128)(2,1)S(1)}, bf16[8,70,16,128]{3,2,1,0:T(8,128)(2,1)S(1)}) custom-call(s32[140]{0:T(256)S(1)} %pad_add_fusion.pos_ref, s32[8]{0:T(128)S(1)} %fusion.28.chip_ref, bf16[65,128,128]{2,1,0:T(8,128)(2,1)S(1)} %constant_dynamic-update-slice_fusion.acts_ref, bf16[128,896]{1,0:T(8,128)(2,1)S(1)} %copy-done), custom_call_target="tpu_custom_call" | custom-call | flops 587202560 | bytes 6947408 | tf_op jit(solution)/shard_map/pallas_call | solution.py:96
  50.6 0.6 collective-permute-start.24
  51.2 0.5 collective-permute-done.16.w1_ref
  51.6 5.1 %shard_map.76 = (bf16[128,896]{1,0:T(8,128)(2,1)}, bf16[16,128,128]{2,1,0:T(8,128)(2,1)S(1)}, bf16[16,128,128]{2,1,0:T(8,128)(2,1)S(1)}, bf16[8,128,128]{2,1,0:T...) custom-call(s32[140]{0:T(256)S(1)} %pad_add_fusion.pos_ref, s32[8]{0:T(128)S(1)} %fusion.28.chip_ref, ...), custom_call_target="tpu_custom_call" | custom-call | flops 1174405120 | bytes 9273936 | tf_op jit(solution)/shard_map/pallas_call | solution.py:96
  56.8 2.4 %collective-permute-start.17 = (bf16[8,128,128]{2,1,0:T(8,128)(2,1)S(1)}, bf16[8,128,128]{2,1,0:T(8,128)(2,1)S(1)}, u32[]{:S(2)}, u32[]{:S(2)}) collective-permute-start(bf16[8,128,128]{2,1,0:T(8,128)(2,1)S(1)} %get-tuple-element.20), channel_id=1, source_target_pairs={{0,1},{1,2},{2,3},{3,0},{4,5},{5,6},{6,7},{7,4},{8,9},{9,10},{10,1... | collective-permute-start | bytes 786440 | tf_op jit(solution)/shard_map/y/ppermute | solution.py:118
  59.2 0.5 fusion.5
  59.8 3.3 %collective-permute-start.27 = (bf16[35,16,128]{2,1,0:T(8,128)(2,1)S(1)}, bf16[35,16,128]{2,1,0:T(8,128)(2,1)S(1)}, u32[]{:S(2)}, u32[]{:S(2)}) collective-permute-start(bf16[35,16,128]{2,1,0:T(8,128)(2,1)S(1)} %get-tuple-element.49), channel_id=1, source_target_pairs={{0,96},{16,112},{32,0},{48,16},{64,32},{80,48},{96,64},{112,80},{1... | collective-permute-start | bytes 430088 | tf_op jit(solution)/shard_map/x/ppermute | solution.py:123
  63.2 3.4 %collective-permute-done.27 = bf16[35,16,128]{2,1,0:T(8,128)(2,1)S(1)} collective-permute-done((bf16[35,16,128]{2,1,0:T(8,128)(2,1)S(1)}, bf16[35,16,128]{2,1,0:T(8,128)(2,1)S(1)}, u32[]{:S(2)}, u32[]{:S(2)}) %collective-permute-start.27) | collective-permute-done | bytes 143392 | tf_op jit(solution)/shard_map/x/ppermute | solution.py:123
  66.6 3.8 %collective-permute-start.28 = (bf16[70,16,128]{2,1,0:T(8,128)(2,1)S(1)}, bf16[70,16,128]{2,1,0:T(8,128)(2,1)S(1)}, u32[]{:S(2)}, u32[]{:S(2)}) collective-permute-start(bf16[70,16,128]{2,1,0:T(8,128)(2,1)S(1)} %pad_maximum_fusion.4), channel_id=1, source_target_pairs={{0,96},{16,112},{32,0},{48,16},{64,32},{80,48},{96,64},{112,80},{1... | collective-permute-start | bytes 860168 | tf_op jit(solution)/shard_map/x/ppermute | solution.py:123
  70.8 5.2 %collective-permute-done.28 = bf16[70,16,128]{2,1,0:T(8,128)(2,1)S(1)} collective-permute-done((bf16[70,16,128]{2,1,0:T(8,128)(2,1)S(1)}, bf16[70,16,128]{2,1,0:T(8,128)(2,1)S(1)}, u32[]{:S(2)}, u32[]{:S(2)}) %collective-permute-start.28) | collective-permute-done | bytes 286752 | tf_op jit(solution)/shard_map/x/ppermute | solution.py:123
  76.0 3.6 %collective-permute-done.26 = bf16[70,16,128]{2,1,0:T(8,128)(2,1)S(1)} collective-permute-done((bf16[70,16,128]{2,1,0:T(8,128)(2,1)S(1)}, bf16[70,16,128]{2,1,0:T(8,128)(2,1)S(1)}, u32[]{:S(2)}, u32[]{:S(2)}) %collective-permute-start.26) | collective-permute-done | bytes 286752 | tf_op jit(solution)/shard_map/x/ppermute | solution.py:123
  79.6 0.2 fusion.1
  79.8 0.2 collective-permute-start.31
  80.1 2.7 %collective-permute-start.18 = (bf16[16,128,128]{2,1,0:T(8,128)(2,1)S(1)}, bf16[16,128,128]{2,1,0:T(8,128)(2,1)S(1)}, u32[]{:S(2)}, u32[]{:S(2)}) collective-permute-start(bf16[16,128,128]{2,1,0:T(8,128)(2,1)S(1)} %pad_maximum_fusion.1), channel_id=1, source_target_pairs={{0,1},{1,2},{2,3},{3,0},{4,5},{5,6},{6,7},{7,4},{8,9},{9,10},{10,1... | collective-permute-start | bytes 1572872 | tf_op jit(solution)/shard_map/y/ppermute | solution.py:118
  82.8 10.4 %collective-permute-start.33 = (bf16[70,16,128]{2,1,0:T(8,128)(2,1)S(1)}, bf16[70,16,128]{2,1,0:T(8,128)(2,1)S(1)}, u32[]{:S(2)}, u32[]{:S(2)}) collective-permute-start(bf16[70,16,128]{2,1,0:T(8,128)(2,1)S(1)} %fusion.1), channel_id=1, source_target_pairs={{0,128},{16,144},{32,160},{48,176},{64,192},{80,208},{96,224},{112... | collective-permute-start | bytes 860168 | tf_op jit(solution)/shard_map/z_hi/ppermute | solution.py:128
  93.3 2.2 %collective-permute-start.29 = (bf16[35,16,128]{2,1,0:T(8,128)(2,1)S(1)}, bf16[35,16,128]{2,1,0:T(8,128)(2,1)S(1)}, u32[]{:S(2)}, u32[]{:S(2)}) collective-permute-start(bf16[35,16,128]{2,1,0:T(8,128)(2,1)S(1)} %get-tuple-element.46), channel_id=1, source_target_pairs={{0,32},{16,48},{32,64},{48,80},{64,96},{80,112},{96,0},{112,16},{1... | collective-permute-start | bytes 430088 | tf_op jit(solution)/shard_map/x/ppermute | solution.py:123
  95.6 1.4 %collective-permute-start.32 = (bf16[70,16,128]{2,1,0:T(8,128)(2,1)S(1)}, bf16[70,16,128]{2,1,0:T(8,128)(2,1)S(1)}, u32[]{:S(2)}, u32[]{:S(2)}) collective-permute-start(bf16[70,16,128]{2,1,0:T(8,128)(2,1)S(1)} %pad_maximum_fusion.6), channel_id=1, source_target_pairs={{0,96},{16,112},{32,0},{48,16},{64,32},{80,48},{96,64},{112,80},{1... | collective-permute-start | bytes 860168 | tf_op jit(solution)/shard_map/x/ppermute | solution.py:123
  97.0 2.9 %collective-permute-done.29 = bf16[35,16,128]{2,1,0:T(8,128)(2,1)S(1)} collective-permute-done((bf16[35,16,128]{2,1,0:T(8,128)(2,1)S(1)}, bf16[35,16,128]{2,1,0:T(8,128)(2,1)S(1)}, u32[]{:S(2)}, u32[]{:S(2)}) %collective-permute-start.29) | collective-permute-done | bytes 143392 | tf_op jit(solution)/shard_map/x/ppermute | solution.py:123
  100.0 2.0 %collective-permute-start.30 = (bf16[70,16,128]{2,1,0:T(8,128)(2,1)S(1)}, bf16[70,16,128]{2,1,0:T(8,128)(2,1)S(1)}, u32[]{:S(2)}, u32[]{:S(2)}) collective-permute-start(bf16[70,16,128]{2,1,0:T(8,128)(2,1)S(1)} %pad_maximum_fusion.5), channel_id=1, source_target_pairs={{0,32},{16,48},{32,64},{48,80},{64,96},{80,112},{96,0},{112,16},{1... | collective-permute-start | bytes 860168 | tf_op jit(solution)/shard_map/x/ppermute | solution.py:123
  102.0 0.2 fusion.33
  102.3 3.5 %collective-permute-start.23 = (bf16[4,128,128]{2,1,0:T(8,128)(2,1)S(1)}, bf16[4,128,128]{2,1,0:T(8,128)(2,1)S(1)}, u32[]{:S(2)}, u32[]{:S(2)}) collective-permute-start(bf16[4,128,128]{2,1,0:T(8,128)(2,1)S(1)} %get-tuple-element.44), channel_id=1, source_target_pairs={{0,4},{1,5},{2,6},{3,7},{4,8},{5,9},{6,10},{7,11},{8,12},{9,13},{1... | collective-permute-start | bytes 393224 | tf_op jit(solution)/shard_map/z_lo/ppermute | solution.py:113
  105.8 3.9 %collective-permute-start.22 = (bf16[4,128,128]{2,1,0:T(8,128)(2,1)S(1)}, bf16[4,128,128]{2,1,0:T(8,128)(2,1)S(1)}, u32[]{:S(2)}, u32[]{:S(2)}) collective-permute-start(bf16[4,128,128]{2,1,0:T(8,128)(2,1)S(1)} %get-tuple-element.45), channel_id=1, source_target_pairs={{0,8},{1,9},{2,10},{3,11},{4,12},{5,13},{6,14},{7,15},{8,0},{9,1},... | collective-permute-start | bytes 393224 | tf_op jit(solution)/shard_map/z_lo/ppermute | solution.py:113
  109.7 0.1 convert_add_fusion.2
  110.0 3.6 %collective-permute-done.23 = bf16[4,128,128]{2,1,0:T(8,128)(2,1)S(1)} collective-permute-done((bf16[4,128,128]{2,1,0:T(8,128)(2,1)S(1)}, bf16[4,128,128]{2,1,0:T(8,128)(2,1)S(1)}, u32[]{:S(2)}, u32[]{:S(2)}) %collective-permute-start.23) | collective-permute-done | bytes 131104 | tf_op jit(solution)/shard_map/z_lo/ppermute | solution.py:113
  113.6 2.1 %collective-permute-done.22 = bf16[4,128,128]{2,1,0:T(8,128)(2,1)S(1)} collective-permute-done((bf16[4,128,128]{2,1,0:T(8,128)(2,1)S(1)}, bf16[4,128,128]{2,1,0:T(8,128)(2,1)S(1)}, u32[]{:S(2)}, u32[]{:S(2)}) %collective-permute-start.22) | collective-permute-done | bytes 131104 | tf_op jit(solution)/shard_map/z_lo/ppermute | solution.py:113
  115.8 0.1 copy.10
  115.9 0.8 copy.11
  116.7 0.8 maximum_select_fusion
  (85 shorter events, 2.6 us)
Async XLA Ops:
  1.8 16.2 %collective-permute-start.2 = (bf16[4,128,128]{2,1,0:T(8,128)(2,1)S(1)}, bf16[4,128,128]{2,1,0:T(8,128)(2,1)S(1)}, u32[]{:S(2)}, u32[]{:S(2)}) collective-permute-start(bf16[4,128,128]{2,1,0:T(8,128)(2,1)S(1)} %bitcast.64), channel_id=1, source_target_pairs={{0,12},{1,13},{2,14},{3,15},{4,0},{5,1},{6,2},{7,3},{8,4},{9,5},{1... | collective-permute-start | bytes 393224 | tf_op jit(solution)/shard_map/z_lo/ppermute | solution.py:113
  6.5 11.5 %collective-permute-start.1 = (bf16[4,128,128]{2,1,0:T(8,128)(2,1)S(1)}, bf16[4,128,128]{2,1,0:T(8,128)(2,1)S(1)}, u32[]{:S(2)}, u32[]{:S(2)}) collective-permute-start(bf16[4,128,128]{2,1,0:T(8,128)(2,1)S(1)} %bitcast.65), channel_id=1, source_target_pairs={{0,8},{1,9},{2,10},{3,11},{4,12},{5,13},{6,14},{7,15},{8,0},{9,1},... | collective-permute-start | bytes 393224 | tf_op jit(solution)/shard_map/z_lo/ppermute | solution.py:113
  6.5 11.5 %collective-permute-start = (bf16[4,128,128]{2,1,0:T(8,128)(2,1)S(1)}, bf16[4,128,128]{2,1,0:T(8,128)(2,1)S(1)}, u32[]{:S(2)}, u32[]{:S(2)}) collective-permute-start(bf16[4,128,128]{2,1,0:T(8,128)(2,1)S(1)} %bitcast.66), channel_id=1, source_target_pairs={{0,4},{1,5},{2,6},{3,7},{4,8},{5,9},{6,10},{7,11},{8,12},{9,13},{1... | collective-permute-start | bytes 393224 | tf_op jit(solution)/shard_map/z_lo/ppermute | solution.py:113
  8.2 1.5 %collective-permute-start.3 = (bf16[7,10,8,128]{3,2,1,0:T(8,128)(2,1)S(1)}, bf16[7,10,8,128]{3,2,1,0:T(8,128)(2,1)S(1)}, u32[]{:S(2)}, u32[]{:S(2)}) collective-permute-start(bf16[7,10,8,128]{3,2,1,0:T(8,128)(2,1)S(1)} %get-tuple-element.51), channel_id=1, source_target_pairs={{0,16},{16,0},{32,48},{48,32},{64,80},{80,64},{96,112},{112,96},{1... | collective-permute-start | bytes 430088 | tf_op jit(solution)/shard_map/core/ppermute | solution.py:133
  9.7 18.4 %collective-permute-start.12 = (bf16[70,16,128]{2,1,0:T(8,128)(2,1)S(1)}, bf16[70,16,128]{2,1,0:T(8,128)(2,1)S(1)}, u32[]{:S(2)}, u32[]{:S(2)}) collective-permute-start(bf16[70,16,128]{2,1,0:T(8,128)(2,1)S(1)} %maximum_select_fusion.1), channel_id=1, source_target_pairs={{0,128},{16,144},{32,160},{48,176},{64,192},{80,208},{96,224},{112... | collective-permute-start | bytes 860168 | tf_op jit(solution)/shard_map/z_hi/ppermute | solution.py:128
  15.2 9.0 %collective-permute-start.10 = (bf16[70,16,128]{2,1,0:T(8,128)(2,1)S(1)}, bf16[70,16,128]{2,1,0:T(8,128)(2,1)S(1)}, u32[]{:S(2)}, u32[]{:S(2)}) collective-permute-start(bf16[70,16,128]{2,1,0:T(8,128)(2,1)S(1)} %maximum_select_fusion.1), channel_id=1, source_target_pairs={{0,96},{16,112},{32,0},{48,16},{64,32},{80,48},{96,64},{112,80},{1... | collective-permute-start | bytes 860168 | tf_op jit(solution)/shard_map/x/ppermute | solution.py:123
  18.0 10.0 %collective-permute-start.8 = (bf16[70,16,128]{2,1,0:T(8,128)(2,1)S(1)}, bf16[70,16,128]{2,1,0:T(8,128)(2,1)S(1)}, u32[]{:S(2)}, u32[]{:S(2)}) collective-permute-start(bf16[70,16,128]{2,1,0:T(8,128)(2,1)S(1)} %maximum_select_fusion.1), channel_id=1, source_target_pairs={{0,32},{16,48},{32,64},{48,80},{64,96},{80,112},{96,0},{112,16},{1... | collective-permute-start | bytes 860168 | tf_op jit(solution)/shard_map/x/ppermute | solution.py:123
  18.1 21.2 %collective-permute-start.6 = (bf16[16,128,128]{2,1,0:T(8,128)(2,1)S(1)}, bf16[16,128,128]{2,1,0:T(8,128)(2,1)S(1)}, u32[]{:S(2)}, u32[]{:S(2)}) collective-permute-start(bf16[16,128,128]{2,1,0:T(8,128)(2,1)S(1)} %pad_maximum_fusion), channel_id=1, source_target_pairs={{0,3},{1,0},{2,1},{3,2},{4,7},{5,4},{6,5},{7,6},{8,11},{9,8},{10,9... | collective-permute-start | bytes 1572872 | tf_op jit(solution)/shard_map/y/ppermute | solution.py:118
  18.9 21.2 %collective-permute-start.4 = (bf16[16,128,128]{2,1,0:T(8,128)(2,1)S(1)}, bf16[16,128,128]{2,1,0:T(8,128)(2,1)S(1)}, u32[]{:S(2)}, u32[]{:S(2)}) collective-permute-start(bf16[16,128,128]{2,1,0:T(8,128)(2,1)S(1)} %pad_maximum_fusion), channel_id=1, source_target_pairs={{0,1},{1,2},{2,3},{3,0},{4,5},{5,6},{6,7},{7,4},{8,9},{9,10},{10,1... | collective-permute-start | bytes 1572872 | tf_op jit(solution)/shard_map/y/ppermute | solution.py:118
  24.2 7.2 %collective-permute-start.11 = (bf16[35,16,128]{2,1,0:T(8,128)(2,1)S(1)}, bf16[35,16,128]{2,1,0:T(8,128)(2,1)S(1)}, u32[]{:S(2)}, u32[]{:S(2)}) collective-permute-start(bf16[35,16,128]{2,1,0:T(8,128)(2,1)S(1)} %slice.214), channel_id=1, source_target_pairs={{0,96},{16,112},{32,0},{48,16},{64,32},{80,48},{96,64},{112,80},{1... | collective-permute-start | bytes 430088 | tf_op jit(solution)/shard_map/x/ppermute | solution.py:123
  28.0 11.1 %collective-permute-start.9 = (bf16[35,16,128]{2,1,0:T(8,128)(2,1)S(1)}, bf16[35,16,128]{2,1,0:T(8,128)(2,1)S(1)}, u32[]{:S(2)}, u32[]{:S(2)}) collective-permute-start(bf16[35,16,128]{2,1,0:T(8,128)(2,1)S(1)} %slice.213), channel_id=1, source_target_pairs={{0,32},{16,48},{32,64},{48,80},{64,96},{80,112},{96,0},{112,16},{1... | collective-permute-start | bytes 430088 | tf_op jit(solution)/shard_map/x/ppermute | solution.py:123
  28.1 19.0 %collective-permute-start.15 = (bf16[70,16,128]{2,1,0:T(8,128)(2,1)S(1)}, bf16[70,16,128]{2,1,0:T(8,128)(2,1)S(1)}, u32[]{:S(2)}, u32[]{:S(2)}) collective-permute-start(bf16[70,16,128]{2,1,0:T(8,128)(2,1)S(1)} %collective-permute-done.12), channel_id=1, source_target_pairs={{0,96},{16,112},{32,0},{48,16},{64,32},{80,48},{96,64},{112,80},{1... | collective-permute-start | bytes 860168 | tf_op jit(solution)/shard_map/x/ppermute | solution.py:123
  31.4 15.6 %collective-permute-start.14 = (bf16[70,16,128]{2,1,0:T(8,128)(2,1)S(1)}, bf16[70,16,128]{2,1,0:T(8,128)(2,1)S(1)}, u32[]{:S(2)}, u32[]{:S(2)}) collective-permute-start(bf16[70,16,128]{2,1,0:T(8,128)(2,1)S(1)} %collective-permute-done.12), channel_id=1, source_target_pairs={{0,64},{16,80},{32,96},{48,112},{64,0},{80,16},{96,32},{112,48},{1... | collective-permute-start | bytes 860168 | tf_op jit(solution)/shard_map/x/ppermute | solution.py:123
  39.1 7.8 %collective-permute-start.13 = (bf16[70,16,128]{2,1,0:T(8,128)(2,1)S(1)}, bf16[70,16,128]{2,1,0:T(8,128)(2,1)S(1)}, u32[]{:S(2)}, u32[]{:S(2)}) collective-permute-start(bf16[70,16,128]{2,1,0:T(8,128)(2,1)S(1)} %collective-permute-done.12), channel_id=1, source_target_pairs={{0,32},{16,48},{32,64},{48,80},{64,96},{80,112},{96,0},{112,16},{1... | collective-permute-start | bytes 860168 | tf_op jit(solution)/shard_map/x/ppermute | solution.py:123
  39.3 8.0 %collective-permute-start.7 = (bf16[8,128,128]{2,1,0:T(8,128)(2,1)S(1)}, bf16[8,128,128]{2,1,0:T(8,128)(2,1)S(1)}, u32[]{:S(2)}, u32[]{:S(2)}) collective-permute-start(bf16[8,128,128]{2,1,0:T(8,128)(2,1)S(1)} %slice.212), channel_id=1, source_target_pairs={{0,3},{1,0},{2,1},{3,2},{4,7},{5,4},{6,5},{7,6},{8,11},{9,8},{10,9... | collective-permute-start | bytes 786440 | tf_op jit(solution)/shard_map/y/ppermute | solution.py:118
  40.1 7.3 %copy-start = (bf16[128,896]{1,0:T(8,128)(2,1)S(1)}, bf16[128,896]{1,0:T(8,128)(2,1)}, u32[]{:S(2)}) copy-start(bf16[128,896]{1,0:T(8,128)(2,1)} %up_ref.3) | copy-start | bytes 688132
  40.2 7.1 %collective-permute-start.5 = (bf16[8,128,128]{2,1,0:T(8,128)(2,1)S(1)}, bf16[8,128,128]{2,1,0:T(8,128)(2,1)S(1)}, u32[]{:S(2)}, u32[]{:S(2)}) collective-permute-start(bf16[8,128,128]{2,1,0:T(8,128)(2,1)S(1)} %slice.211), channel_id=1, source_target_pairs={{0,1},{1,2},{2,3},{3,0},{4,5},{5,6},{6,7},{7,4},{8,9},{9,10},{10,1... | collective-permute-start | bytes 786440 | tf_op jit(solution)/shard_map/y/ppermute | solution.py:118
  47.1 4.5 %collective-permute-start.16 = (bf16[8,70,16,128]{3,2,1,0:T(8,128)(2,1)S(1)}, bf16[8,70,16,128]{3,2,1,0:T(8,128)(2,1)S(1)}, u32[]{:S(2)}, u32[]{:S(2)}) collective-permute-start(bf16[8,70,16,128]{3,2,1,0:T(8,128)(2,1)S(1)} %bitcast_dynamic-update-slice_fusion.w0_ref), channel_id=1, source_target_pairs={{0,16},{16,0},{32,48},{48,32},{64,80},{80,64},{96,112},{112,96},{1... | collective-permute-start | bytes 6881288 | tf_op jit(solution)/shard_map/core/ppermute | solution.py:133
  50.6 8.6 %collective-permute-start.24 = (bf16[8,70,16,128]{3,2,1,0:T(8,128)(2,1)S(1)}, bf16[8,70,16,128]{3,2,1,0:T(8,128)(2,1)S(1)}, u32[]{:S(2)}, u32[]{:S(2)}) collective-permute-start(bf16[8,70,16,128]{3,2,1,0:T(8,128)(2,1)S(1)} %get-tuple-element.24), channel_id=1, source_target_pairs={{0,16},{16,0},{32,48},{48,32},{64,80},{80,64},{96,112},{112,96},{1... | collective-permute-start | bytes 6881288 | tf_op jit(solution)/shard_map/core/ppermute | solution.py:133
  56.8 23.2 %collective-permute-start.17 = (bf16[8,128,128]{2,1,0:T(8,128)(2,1)S(1)}, bf16[8,128,128]{2,1,0:T(8,128)(2,1)S(1)}, u32[]{:S(2)}, u32[]{:S(2)}) collective-permute-start(bf16[8,128,128]{2,1,0:T(8,128)(2,1)S(1)} %get-tuple-element.20), channel_id=1, source_target_pairs={{0,1},{1,2},{2,3},{3,0},{4,5},{5,6},{6,7},{7,4},{8,9},{9,10},{10,1... | collective-permute-start | bytes 786440 | tf_op jit(solution)/shard_map/y/ppermute | solution.py:118
  59.2 11.4 %collective-permute-start.19 = (bf16[8,128,128]{2,1,0:T(8,128)(2,1)S(1)}, bf16[8,128,128]{2,1,0:T(8,128)(2,1)S(1)}, u32[]{:S(2)}, u32[]{:S(2)}) collective-permute-start(bf16[8,128,128]{2,1,0:T(8,128)(2,1)S(1)} %get-tuple-element.22), channel_id=1, source_target_pairs={{0,3},{1,0},{2,1},{3,2},{4,7},{5,4},{6,5},{7,6},{8,11},{9,8},{10,9... | collective-permute-start | bytes 786440 | tf_op jit(solution)/shard_map/y/ppermute | solution.py:118
  59.8 10.6 %collective-permute-start.25 = (bf16[35,16,128]{2,1,0:T(8,128)(2,1)S(1)}, bf16[35,16,128]{2,1,0:T(8,128)(2,1)S(1)}, u32[]{:S(2)}, u32[]{:S(2)}) collective-permute-start(bf16[35,16,128]{2,1,0:T(8,128)(2,1)S(1)} %get-tuple-element.48), channel_id=1, source_target_pairs={{0,32},{16,48},{32,64},{48,80},{64,96},{80,112},{96,0},{112,16},{1... | collective-permute-start | bytes 430088 | tf_op jit(solution)/shard_map/x/ppermute | solution.py:123
  59.8 6.7 %collective-permute-start.27 = (bf16[35,16,128]{2,1,0:T(8,128)(2,1)S(1)}, bf16[35,16,128]{2,1,0:T(8,128)(2,1)S(1)}, u32[]{:S(2)}, u32[]{:S(2)}) collective-permute-start(bf16[35,16,128]{2,1,0:T(8,128)(2,1)S(1)} %get-tuple-element.49), channel_id=1, source_target_pairs={{0,96},{16,112},{32,0},{48,16},{64,32},{80,48},{96,64},{112,80},{1... | collective-permute-start | bytes 430088 | tf_op jit(solution)/shard_map/x/ppermute | solution.py:123
  66.6 9.4 %collective-permute-start.28 = (bf16[70,16,128]{2,1,0:T(8,128)(2,1)S(1)}, bf16[70,16,128]{2,1,0:T(8,128)(2,1)S(1)}, u32[]{:S(2)}, u32[]{:S(2)}) collective-permute-start(bf16[70,16,128]{2,1,0:T(8,128)(2,1)S(1)} %pad_maximum_fusion.4), channel_id=1, source_target_pairs={{0,96},{16,112},{32,0},{48,16},{64,32},{80,48},{96,64},{112,80},{1... | collective-permute-start | bytes 860168 | tf_op jit(solution)/shard_map/x/ppermute | solution.py:123
  70.5 9.1 %collective-permute-start.26 = (bf16[70,16,128]{2,1,0:T(8,128)(2,1)S(1)}, bf16[70,16,128]{2,1,0:T(8,128)(2,1)S(1)}, u32[]{:S(2)}, u32[]{:S(2)}) collective-permute-start(bf16[70,16,128]{2,1,0:T(8,128)(2,1)S(1)} %pad_maximum_fusion.3), channel_id=1, source_target_pairs={{0,32},{16,48},{32,64},{48,80},{64,96},{80,112},{96,0},{112,16},{1... | collective-permute-start | bytes 860168 | tf_op jit(solution)/shard_map/x/ppermute | solution.py:123
  70.7 31.3 %collective-permute-start.20 = (bf16[16,128,128]{2,1,0:T(8,128)(2,1)S(1)}, bf16[16,128,128]{2,1,0:T(8,128)(2,1)S(1)}, u32[]{:S(2)}, u32[]{:S(2)}) collective-permute-start(bf16[16,128,128]{2,1,0:T(8,128)(2,1)S(1)} %pad_maximum_fusion.2), channel_id=1, source_target_pairs={{0,3},{1,0},{2,1},{3,2},{4,7},{5,4},{6,5},{7,6},{8,11},{9,8},{10,9... | collective-permute-start | bytes 1572872 | tf_op jit(solution)/shard_map/y/ppermute | solution.py:118
  79.8 15.7 %collective-permute-start.31 = (bf16[35,16,128]{2,1,0:T(8,128)(2,1)S(1)}, bf16[35,16,128]{2,1,0:T(8,128)(2,1)S(1)}, u32[]{:S(2)}, u32[]{:S(2)}) collective-permute-start(bf16[35,16,128]{2,1,0:T(8,128)(2,1)S(1)} %get-tuple-element.47), channel_id=1, source_target_pairs={{0,96},{16,112},{32,0},{48,16},{64,32},{80,48},{96,64},{112,80},{1... | collective-permute-start | bytes 430088 | tf_op jit(solution)/shard_map/x/ppermute | solution.py:123
  80.1 21.9 %collective-permute-start.18 = (bf16[16,128,128]{2,1,0:T(8,128)(2,1)S(1)}, bf16[16,128,128]{2,1,0:T(8,128)(2,1)S(1)}, u32[]{:S(2)}, u32[]{:S(2)}) collective-permute-start(bf16[16,128,128]{2,1,0:T(8,128)(2,1)S(1)} %pad_maximum_fusion.1), channel_id=1, source_target_pairs={{0,1},{1,2},{2,3},{3,0},{4,5},{5,6},{6,7},{7,4},{8,9},{9,10},{10,1... | collective-permute-start | bytes 1572872 | tf_op jit(solution)/shard_map/y/ppermute | solution.py:118
  82.8 23.0 %collective-permute-start.33 = (bf16[70,16,128]{2,1,0:T(8,128)(2,1)S(1)}, bf16[70,16,128]{2,1,0:T(8,128)(2,1)S(1)}, u32[]{:S(2)}, u32[]{:S(2)}) collective-permute-start(bf16[70,16,128]{2,1,0:T(8,128)(2,1)S(1)} %fusion.1), channel_id=1, source_target_pairs={{0,128},{16,144},{32,160},{48,176},{64,192},{80,208},{96,224},{112... | collective-permute-start | bytes 860168 | tf_op jit(solution)/shard_map/z_hi/ppermute | solution.py:128
  93.3 6.6 %collective-permute-start.29 = (bf16[35,16,128]{2,1,0:T(8,128)(2,1)S(1)}, bf16[35,16,128]{2,1,0:T(8,128)(2,1)S(1)}, u32[]{:S(2)}, u32[]{:S(2)}) collective-permute-start(bf16[35,16,128]{2,1,0:T(8,128)(2,1)S(1)} %get-tuple-element.46), channel_id=1, source_target_pairs={{0,32},{16,48},{32,64},{48,80},{64,96},{80,112},{96,0},{112,16},{1... | collective-permute-start | bytes 430088 | tf_op jit(solution)/shard_map/x/ppermute | solution.py:123
  95.6 14.1 %collective-permute-start.32 = (bf16[70,16,128]{2,1,0:T(8,128)(2,1)S(1)}, bf16[70,16,128]{2,1,0:T(8,128)(2,1)S(1)}, u32[]{:S(2)}, u32[]{:S(2)}) collective-permute-start(bf16[70,16,128]{2,1,0:T(8,128)(2,1)S(1)} %pad_maximum_fusion.6), channel_id=1, source_target_pairs={{0,96},{16,112},{32,0},{48,16},{64,32},{80,48},{96,64},{112,80},{1... | collective-permute-start | bytes 860168 | tf_op jit(solution)/shard_map/x/ppermute | solution.py:123
  100.0 9.7 %collective-permute-start.30 = (bf16[70,16,128]{2,1,0:T(8,128)(2,1)S(1)}, bf16[70,16,128]{2,1,0:T(8,128)(2,1)S(1)}, u32[]{:S(2)}, u32[]{:S(2)}) collective-permute-start(bf16[70,16,128]{2,1,0:T(8,128)(2,1)S(1)} %pad_maximum_fusion.5), channel_id=1, source_target_pairs={{0,32},{16,48},{32,64},{48,80},{64,96},{80,112},{96,0},{112,16},{1... | collective-permute-start | bytes 860168 | tf_op jit(solution)/shard_map/x/ppermute | solution.py:123
  102.2 7.8 %collective-permute-start.21 = (bf16[4,128,128]{2,1,0:T(8,128)(2,1)S(1)}, bf16[4,128,128]{2,1,0:T(8,128)(2,1)S(1)}, u32[]{:S(2)}, u32[]{:S(2)}) collective-permute-start(bf16[4,128,128]{2,1,0:T(8,128)(2,1)S(1)} %get-tuple-element.43), channel_id=1, source_target_pairs={{0,12},{1,13},{2,14},{3,15},{4,0},{5,1},{6,2},{7,3},{8,4},{9,5},{1... | collective-permute-start | bytes 393224 | tf_op jit(solution)/shard_map/z_lo/ppermute | solution.py:113
  102.3 11.3 %collective-permute-start.23 = (bf16[4,128,128]{2,1,0:T(8,128)(2,1)S(1)}, bf16[4,128,128]{2,1,0:T(8,128)(2,1)S(1)}, u32[]{:S(2)}, u32[]{:S(2)}) collective-permute-start(bf16[4,128,128]{2,1,0:T(8,128)(2,1)S(1)} %get-tuple-element.44), channel_id=1, source_target_pairs={{0,4},{1,5},{2,6},{3,7},{4,8},{5,9},{6,10},{7,11},{8,12},{9,13},{1... | collective-permute-start | bytes 393224 | tf_op jit(solution)/shard_map/z_lo/ppermute | solution.py:113
  105.8 9.8 %collective-permute-start.22 = (bf16[4,128,128]{2,1,0:T(8,128)(2,1)S(1)}, bf16[4,128,128]{2,1,0:T(8,128)(2,1)S(1)}, u32[]{:S(2)}, u32[]{:S(2)}) collective-permute-start(bf16[4,128,128]{2,1,0:T(8,128)(2,1)S(1)} %get-tuple-element.45), channel_id=1, source_target_pairs={{0,8},{1,9},{2,10},{3,11},{4,12},{5,13},{6,14},{7,15},{8,0},{9,1},... | collective-permute-start | bytes 393224 | tf_op jit(solution)/shard_map/z_lo/ppermute | solution.py:113
  109.9 6.7 %collective-permute-start.34 = (f32[7,10,8,128]{3,2,1,0:T(8,128)S(1)}, f32[7,10,8,128]{3,2,1,0:T(8,128)S(1)}, u32[]{:S(2)}, u32[]{:S(2)}) collective-permute-start(f32[7,10,8,128]{3,2,1,0:T(8,128)S(1)} %get-tuple-element.42), channel_id=1, source_target_pairs={{0,16},{16,0},{32,48},{48,32},{64,80},{80,64},{96,112},{112,96},{1... | collective-permute-start | bytes 860168 | tf_op jit(solution)/shard_map/core/ppermute | solution.py:133

commit v4 on v3

--- a/solution.py
+++ b/solution.py
@@ -52,41 +52,50 @@
     lax.fori_loop(0, cols, column, 0)
 
 
-def project(cols, half, pos_ref, chip_ref, acts_ref, up_ref, w0_ref, w1_ref, hidden_ref, *rest):
+def pair(half, cols, c, h, k, pos_ref, chip_ref, w_ref):
+    slots = [c * half + k, c * half + k + 1]
+    rows = [pos_ref[h * cols * half + slot] for slot in slots]
+    weight = jnp.concatenate([w_ref[chip_ref[chip], slot] for slot in slots for chip in range(8)], axis=0)
+    return rows, weight
+
+
+def project_back(cols, half, pos_ref, chip_ref, up_ref, w0_ref, w1_ref, *rest):
     parts, total = rest[:-1], rest[-1]
     total[...] = jnp.zeros_like(total)
 
     def column(c, carry):
-        lanes = pl.ds(pl.multiple_of(c * BLK, BLK), BLK)
-        up = up_ref[:, lanes]
-        hidden = jnp.zeros((up.shape[0], BLK), jnp.float32)
+        up = up_ref[:, pl.ds(pl.multiple_of(c * BLK, BLK), BLK)]
         for h, w_ref in enumerate((w0_ref, w1_ref)):
             for k in range(0, half, 2):
-                rows = []
-                blocks = []
-                weights = []
-                for j in range(2):
-                    slot = c * half + k + j
-                    rows.append(pos_ref[h * cols * half + slot])
-                    blocks.append(acts_ref[rows[-1]])
-                    weights += [w_ref[chip_ref[chip], slot] for chip in range(8)]
-                weight = jnp.concatenate(weights, axis=0)
-                hidden += jnp.dot(
-                    jnp.concatenate(blocks, axis=1), weight, preferred_element_type=jnp.float32
-                )
+                rows, weight = pair(half, cols, c, h, k, pos_ref, chip_ref, w_ref)
                 back = lax.dot_general(
                     up, weight, (((1,), (1,)), ((), ())), preferred_element_type=jnp.float32
                 )
                 for j in range(2):
                     total[rows[j]] += back[:, j * BLK : (j + 1) * BLK]
-        hidden_ref[:, lanes] = hidden.astype(jnp.bfloat16)
         return carry
 
     lax.fori_loop(0, cols, column, 0)
     start = 0
     for part in parts:
-        part[...] = total[start : start + part.shape[0]].astype(jnp.bfloat16)
-        start += part.shape[0]
+        for piece in range(part.shape[0]):
+            for lane in range(0, part.shape[2], BLK):
+                part[piece, :, lane : lane + BLK] = total[start].astype(jnp.bfloat16)
+                start += 1
+
+
+def project(cols, half, pos_ref, chip_ref, acts_ref, w0_ref, w1_ref, hidden_ref):
+    def column(c, carry):
+        hidden = jnp.zeros((acts_ref.shape[1], BLK), jnp.float32)
+        for h, w_ref in enumerate((w0_ref, w1_ref)):
+            for k in range(0, half, 2):
+                rows, weight = pair(half, cols, c, h, k, pos_ref, chip_ref, w_ref)
+                blocks = jnp.concatenate([acts_ref[row] for row in rows], axis=1)
+                hidden += jnp.dot(blocks, weight, preferred_element_type=jnp.float32)
+        hidden_ref[:, pl.ds(pl.multiple_of(c * BLK, BLK), BLK)] = hidden.astype(jnp.bfloat16)
+        return carry
+
+    lax.fori_loop(0, cols, column, 0)
 
 
 def kernel_call(body, outs, scratch, flops, ins):
@@ -220,14 +229,14 @@
     )
     came = core_step(other)
 
-    part = jax.ShapeDtypeStruct((NZ * own_blocks, tokens, BLK), bf)
-    half_part = jax.ShapeDtypeStruct((NZ * own_blocks // 2, tokens, BLK), bf)
-    hidden_out, *parts = kernel_call(
-        functools.partial(project, cols, half),
-        [jax.ShapeDtypeStruct(grad_out.shape, bf), part, part, half_part, half_part, part],
+    part = jax.ShapeDtypeStruct((NZ, *acts.shape), bf)
+    half_part = jax.ShapeDtypeStruct((NZ // 2, *acts.shape), bf)
+    parts = kernel_call(
+        functools.partial(project_back, cols, half),
+        [part, part, half_part, half_part, part],
         [pltpu.VMEM((blocks + 1, tokens, BLK), jnp.float32)],
-        2 * flops,
-        (pos, chip, whole, grad_out, w8, w8_other),
+        flops,
+        (pos, chip, grad_out, w8, w8_other),
     )
 
     def over_x(zr, after=None):
@@ -246,10 +255,17 @@
     grad_values = ordered(keep, core_step(send), 1)
 
     rest = sum_passed(y_step, *parts)
-    total = rest[:own_blocks]
+    (hidden_out,) = kernel_call(
+        functools.partial(project, cols, half),
+        [jax.ShapeDtypeStruct(grad_out.shape, bf)],
+        [],
+        flops,
+        (pos, chip, tie(whole, away), w8, w8_other),
+    )
+    total = tie(rest[0], hidden_out)
     for q in range(1, NZ):
-        total += f32(z_step(rest[q * own_blocks : (q + 1) * own_blocks].astype(bf), -q))
-    grad_acts = total.transpose(1, 0, 2).reshape(tokens, own_blocks * BLK).astype(bf)
+        total += f32(z_step(rest[q].astype(bf), -q))
+    grad_acts = total.astype(bf)
     return hidden_out, grad_acts, grad_values
 
 

time: 118 us -> 112 us (0.949); the launches traced: 118 us -> 110 us
  waiting for transfers between devices: 34.8 us -> 25.2 us
  Pallas kernels: 8.23 us -> 10.4 us
    ppermute x15, waiting for transfers between devices: 28.4 us -> 20.3 us  [x_step(): return lax.ppermute(a, 'dp', x_pairs(s))]
    ppermute x6, waiting for transfers between devices: 5.66 us -> 0.02 us  [z_step(): return lax.ppermute(a, 'mp', z_pairs(q))]
    ppermute x2, waiting for transfers between devices: 0.01 us -> 4.19 us  [zh_step(): return lax.ppermute(a, 'dp', HALF_PAIRS)]
    ppermute x8, starting transfers between devices: 12.1 us -> 8.64 us  [y_step(): return lax.ppermute(a, 'mp', y_pairs(p))]
    ppermute x6, starting transfers between devices: 12.8 us -> 16.3 us  [z_step(): return lax.ppermute(a, 'mp', z_pairs(q))]
    pallas_call x2 -> x3, Pallas kernels: 8.23 us -> 10.4 us  [kernel_call(): pl.pallas_call(body, out_shape=outs, in_specs=specs, out_specs=[pl.BlockS...]
  transfers between devices with their start and end apart: 35 -> 35, of which waited for: 11 -> 10; matrix products, arithmetic and copies ran while one was open for 5% -> 5% of each run, Pallas kernels for 7% -> 9%
where the time goes in v4:
time: 112 us; the launch traced here: 110 us
  starting transfers between devices  65.9 us (59%)
  waiting for transfers between devices  25.2 us (22%)
  Pallas kernels  10.4 us (9%)
  other arithmetic  5.45 us (5%)
  local copies, waits for them, and re-layouts  2.04 us (2%)
    ppermute x15, starting transfers between devices, x_step(): return lax.ppermute(a, 'dp', x_pairs(s))  25.2 us
    ppermute x15, waiting for transfers between devices, x_step(): return lax.ppermute(a, 'dp', x_pairs(s))  20.3 us
    ppermute x6, starting transfers between devices, z_step(): return lax.ppermute(a, 'mp', z_pairs(q))  16.3 us
    ppermute x2, starting transfers between devices, zh_step(): return lax.ppermute(a, 'dp', HALF_PAIRS)  15 us
    pallas_call x3, Pallas kernels, kernel_call(): pl.pallas_call(body, out_shape=outs, in_specs=specs, out_specs=[pl.BlockS...  10.4 us
    ppermute x8, starting transfers between devices, y_step(): return lax.ppermute(a, 'mp', y_pairs(p))  8.64 us
    ppermute x2, waiting for transfers between devices, zh_step(): return lax.ppermute(a, 'dp', HALF_PAIRS)  4.19 us
  transfers between devices with their start and end apart: 35, of which 10 were waited for; matrix products, arithmetic and copies ran while one was open for 5% of the time, Pallas kernels for 9%

profile of v4, /device:TPU:24, one launch (start us, length us, event | category | flops | bytes accessed | tf_op | source)
XLA Modules:
  0.0 110.1 jit_solution(15435054386999364173)
XLA Ops:
  0.6 1.0 copy.8
  1.8 4.7 %collective-permute-start.2 = (bf16[4,128,128]{2,1,0:T(8,128)(2,1)S(1)}, bf16[4,128,128]{2,1,0:T(8,128)(2,1)S(1)}, u32[]{:S(2)}, u32[]{:S(2)}) collective-permute-start(bf16[4,128,128]{2,1,0:T(8,128)(2,1)S(1)} %bitcast.68), channel_id=1, source_target_pairs={{0,12},{1,13},{2,14},{3,15},{4,0},{5,1},{6,2},{7,3},{8,4},{9,5},{1... | collective-permute-start | bytes 393224 | tf_op jit(solution)/shard_map/z_lo/ppermute | solution.py:122
  6.5 0.7 collective-permute-start
  7.2 1.0 broadcast_select_fusion.1
  8.3 0.8 fusion.17
  9.4 0.2 collective-permute-done.3
  9.7 1.6 %collective-permute-start.14 = (bf16[70,16,128]{2,1,0:T(8,128)(2,1)S(1)}, bf16[70,16,128]{2,1,0:T(8,128)(2,1)S(1)}, u32[]{:S(2)}, u32[]{:S(2)}) collective-permute-start(bf16[70,16,128]{2,1,0:T(8,128)(2,1)S(1)} %maximum_select_fusion.1), channel_id=1, source_target_pairs={{0,32},{16,48},{32,64},{48,80},{64,96},{80,112},{96,0},{112,16},{1... | collective-permute-start | bytes 860168 | tf_op jit(solution)/shard_map/x/ppermute | solution.py:132
  11.3 1.7 %collective-permute-start.16 = (bf16[70,16,128]{2,1,0:T(8,128)(2,1)S(1)}, bf16[70,16,128]{2,1,0:T(8,128)(2,1)S(1)}, u32[]{:S(2)}, u32[]{:S(2)}) collective-permute-start(bf16[70,16,128]{2,1,0:T(8,128)(2,1)S(1)} %maximum_select_fusion.1), channel_id=1, source_target_pairs={{0,96},{16,112},{32,0},{48,16},{64,32},{80,48},{96,64},{112,80},{1... | collective-permute-start | bytes 860168 | tf_op jit(solution)/shard_map/x/ppermute | solution.py:132
  13.0 5.4 %collective-permute-start.18 = (bf16[70,16,128]{2,1,0:T(8,128)(2,1)S(1)}, bf16[70,16,128]{2,1,0:T(8,128)(2,1)S(1)}, u32[]{:S(2)}, u32[]{:S(2)}) collective-permute-start(bf16[70,16,128]{2,1,0:T(8,128)(2,1)S(1)} %maximum_select_fusion.1), channel_id=1, source_target_pairs={{0,128},{16,144},{32,160},{48,176},{64,192},{80,208},{96,224},{112... | collective-permute-start | bytes 860168 | tf_op jit(solution)/shard_map/z_hi/ppermute | solution.py:137
  18.5 0.3 collective-permute-start.4
  18.8 1.8 %collective-permute-start.6 = (bf16[16,128,128]{2,1,0:T(8,128)(2,1)S(1)}, bf16[16,128,128]{2,1,0:T(8,128)(2,1)S(1)}, u32[]{:S(2)}, u32[]{:S(2)}) collective-permute-start(bf16[16,128,128]{2,1,0:T(8,128)(2,1)S(1)} %pad_maximum_fusion), channel_id=1, source_target_pairs={{0,3},{1,0},{2,1},{3,2},{4,7},{5,4},{6,5},{7,6},{8,11},{9,8},{10,9... | collective-permute-start | bytes 1572872 | tf_op jit(solution)/shard_map/y/ppermute | solution.py:127
  20.8 2.3 %collective-permute-start.17 = (bf16[35,16,128]{2,1,0:T(8,128)(2,1)S(1)}, bf16[35,16,128]{2,1,0:T(8,128)(2,1)S(1)}, u32[]{:S(2)}, u32[]{:S(2)}) collective-permute-start(bf16[35,16,128]{2,1,0:T(8,128)(2,1)S(1)} %slice.224), channel_id=1, source_target_pairs={{0,96},{16,112},{32,0},{48,16},{64,32},{80,48},{96,64},{112,80},{1... | collective-permute-start | bytes 430088 | tf_op jit(solution)/shard_map/x/ppermute | solution.py:132
  23.2 4.2 %collective-permute-done.18 = bf16[70,16,128]{2,1,0:T(8,128)(2,1)S(1)} collective-permute-done((bf16[70,16,128]{2,1,0:T(8,128)(2,1)S(1)}, bf16[70,16,128]{2,1,0:T(8,128)(2,1)S(1)}, u32[]{:S(2)}, u32[]{:S(2)}) %collective-permute-start.18) | collective-permute-done | bytes 286752 | tf_op jit(solution)/shard_map/z_hi/ppermute | solution.py:137
  27.3 2.5 %collective-permute-start.19 = (bf16[70,16,128]{2,1,0:T(8,128)(2,1)S(1)}, bf16[70,16,128]{2,1,0:T(8,128)(2,1)S(1)}, u32[]{:S(2)}, u32[]{:S(2)}) collective-permute-start(bf16[70,16,128]{2,1,0:T(8,128)(2,1)S(1)} %collective-permute-done.18), channel_id=1, source_target_pairs={{0,32},{16,48},{32,64},{48,80},{64,96},{80,112},{96,0},{112,16},{1... | collective-permute-start | bytes 860168 | tf_op jit(solution)/shard_map/x/ppermute | solution.py:132
  29.9 2.8 %collective-permute-start.20 = (bf16[70,16,128]{2,1,0:T(8,128)(2,1)S(1)}, bf16[70,16,128]{2,1,0:T(8,128)(2,1)S(1)}, u32[]{:S(2)}, u32[]{:S(2)}) collective-permute-start(bf16[70,16,128]{2,1,0:T(8,128)(2,1)S(1)} %collective-permute-done.18), channel_id=1, source_target_pairs={{0,64},{16,80},{32,96},{48,112},{64,0},{80,16},{96,32},{112,48},{1... | collective-permute-start | bytes 860168 | tf_op jit(solution)/shard_map/x/ppermute | solution.py:132
  32.7 1.4 %collective-permute-start.21 = (bf16[70,16,128]{2,1,0:T(8,128)(2,1)S(1)}, bf16[70,16,128]{2,1,0:T(8,128)(2,1)S(1)}, u32[]{:S(2)}, u32[]{:S(2)}) collective-permute-start(bf16[70,16,128]{2,1,0:T(8,128)(2,1)S(1)} %collective-permute-done.18), channel_id=1, source_target_pairs={{0,96},{16,112},{32,0},{48,16},{64,32},{80,48},{96,64},{112,80},{1... | collective-permute-start | bytes 860168 | tf_op jit(solution)/shard_map/x/ppermute | solution.py:132
  34.3 0.3 collective-permute-start.5
  34.7 2.1 %collective-permute-start.7 = (bf16[8,128,128]{2,1,0:T(8,128)(2,1)S(1)}, bf16[8,128,128]{2,1,0:T(8,128)(2,1)S(1)}, u32[]{:S(2)}, u32[]{:S(2)}) collective-permute-start(bf16[8,128,128]{2,1,0:T(8,128)(2,1)S(1)} %slice.212), channel_id=1, source_target_pairs={{0,3},{1,0},{2,1},{3,2},{4,7},{5,4},{6,5},{7,6},{8,11},{9,8},{10,9... | collective-permute-start | bytes 786440 | tf_op jit(solution)/shard_map/y/ppermute | solution.py:127
  36.8 2.6 %collective-permute-done.19 = bf16[70,16,128]{2,1,0:T(8,128)(2,1)S(1)} collective-permute-done((bf16[70,16,128]{2,1,0:T(8,128)(2,1)S(1)}, bf16[70,16,128]{2,1,0:T(8,128)(2,1)S(1)}, u32[]{:S(2)}, u32[]{:S(2)}) %collective-permute-start.19) | collective-permute-done | bytes 286752 | tf_op jit(solution)/shard_map/x/ppermute | solution.py:132
  39.4 3.9 %collective-permute-done.20 = bf16[70,16,128]{2,1,0:T(8,128)(2,1)S(1)} collective-permute-done((bf16[70,16,128]{2,1,0:T(8,128)(2,1)S(1)}, bf16[70,16,128]{2,1,0:T(8,128)(2,1)S(1)}, u32[]{:S(2)}, u32[]{:S(2)}) %collective-permute-start.20) | collective-permute-done | bytes 286752 | tf_op jit(solution)/shard_map/x/ppermute | solution.py:132
  43.3 0.2 collective-permute-done.21
  43.9 3.2 %shard_map.76 = (bf16[8,70,16,128]{3,2,1,0:T(8,128)(2,1)S(1)}, bf16[8,70,16,128]{3,2,1,0:T(8,128)(2,1)S(1)}) custom-call(s32[140]{0:T(256)S(1)} %pad_add_fusion.pos_ref, s32[8]{0:T(128)S(1)} %fusion.24.chip_ref, bf16[65,128,128]{2,1,0:T(8,128)(2,1)S(1)} %constant_dynamic-update-slice_fusion.acts_ref, bf16[128,896]{1,0:T(8,128)(2,1)S(1)} %copy-done), custom_call_target="tpu_custom_call" | custom-call | flops 587202560 | bytes 6947408 | tf_op jit(solution)/shard_map/pallas_call | solution.py:105
  47.1 0.6 collective-permute-start.8
  47.7 0.5 collective-permute-done.22.w1_ref
  48.1 3.6 %shard_map.78 = (bf16[4,128,512]{2,1,0:T(8,128)(2,1)S(1)}, bf16[4,128,512]{2,1,0:T(8,128)(2,1)S(1)}, bf16[2,128,512]{2,1,0:T(8,128)(2,1)S(1)}, bf16[2,128,512]{2,1,0:T(8,128)(2,1)S(1)}, bf16[4,128,512]{2,1,0:T(8,128)(2,1)S(1)}) custom-call(s32[140]{0:T(256)S(1)} %pad_add_fusion.pos_ref, s32[8]{0:T(128)S(1)} %fusion.24.chip_ref, ...), custom_call_target="tpu_custom_call" | custom-call | flops 587202560 | bytes 6914640 | tf_op jit(solution)/shard_map/pallas_call | solution.py:105
  51.8 0.8 collective-permute-start.25
  52.6 2.6 %collective-permute-start.23 = (bf16[2,128,512]{2,1,0:T(8,128)(2,1)S(1)}, bf16[2,128,512]{2,1,0:T(8,128)(2,1)S(1)}, u32[]{:S(2)}, u32[]{:S(2)}) collective-permute-start(bf16[2,128,512]{2,1,0:T(8,128)(2,1)S(1)} %get-tuple-element.23), channel_id=1, source_target_pairs={{0,1},{1,2},{2,3},{3,0},{4,5},{5,6},{6,7},{7,4},{8,9},{9,10},{10,1... | collective-permute-start | bytes 786440 | tf_op jit(solution)/shard_map/y/ppermute | solution.py:127
  55.2 0.6 fusion.6
  55.8 2.7 %collective-permute-start.11 = (bf16[35,16,128]{2,1,0:T(8,128)(2,1)S(1)}, bf16[35,16,128]{2,1,0:T(8,128)(2,1)S(1)}, u32[]{:S(2)}, u32[]{:S(2)}) collective-permute-start(bf16[35,16,128]{2,1,0:T(8,128)(2,1)S(1)} %get-tuple-element.48), channel_id=1, source_target_pairs={{0,96},{16,112},{32,0},{48,16},{64,32},{80,48},{96,64},{112,80},{1... | collective-permute-start | bytes 430088 | tf_op jit(solution)/shard_map/x/ppermute | solution.py:132
  58.6 2.6 %collective-permute-done.11 = bf16[35,16,128]{2,1,0:T(8,128)(2,1)S(1)} collective-permute-done((bf16[35,16,128]{2,1,0:T(8,128)(2,1)S(1)}, bf16[35,16,128]{2,1,0:T(8,128)(2,1)S(1)}, u32[]{:S(2)}, u32[]{:S(2)}) %collective-permute-start.11) | collective-permute-done | bytes 143392 | tf_op jit(solution)/shard_map/x/ppermute | solution.py:132
  61.3 3.8 %collective-permute-start.12 = (bf16[70,16,128]{2,1,0:T(8,128)(2,1)S(1)}, bf16[70,16,128]{2,1,0:T(8,128)(2,1)S(1)}, u32[]{:S(2)}, u32[]{:S(2)}) collective-permute-start(bf16[70,16,128]{2,1,0:T(8,128)(2,1)S(1)} %pad_maximum_fusion.4), channel_id=1, source_target_pairs={{0,96},{16,112},{32,0},{48,16},{64,32},{80,48},{96,64},{112,80},{1... | collective-permute-start | bytes 860168 | tf_op jit(solution)/shard_map/x/ppermute | solution.py:132
  65.5 4.5 %collective-permute-done.12 = bf16[70,16,128]{2,1,0:T(8,128)(2,1)S(1)} collective-permute-done((bf16[70,16,128]{2,1,0:T(8,128)(2,1)S(1)}, bf16[70,16,128]{2,1,0:T(8,128)(2,1)S(1)}, u32[]{:S(2)}, u32[]{:S(2)}) %collective-permute-start.12) | collective-permute-done | bytes 286752 | tf_op jit(solution)/shard_map/x/ppermute | solution.py:132
  70.0 3.6 %collective-permute-done.10 = bf16[70,16,128]{2,1,0:T(8,128)(2,1)S(1)} collective-permute-done((bf16[70,16,128]{2,1,0:T(8,128)(2,1)S(1)}, bf16[70,16,128]{2,1,0:T(8,128)(2,1)S(1)}, u32[]{:S(2)}, u32[]{:S(2)}) %collective-permute-start.10) | collective-permute-done | bytes 286752 | tf_op jit(solution)/shard_map/x/ppermute | solution.py:132
  73.6 0.2 fusion.1
  73.8 0.2 collective-permute-start.32
  74.1 0.7 collective-permute-start.24
  74.8 9.6 %collective-permute-start.13 = (bf16[70,16,128]{2,1,0:T(8,128)(2,1)S(1)}, bf16[70,16,128]{2,1,0:T(8,128)(2,1)S(1)}, u32[]{:S(2)}, u32[]{:S(2)}) collective-permute-start(bf16[70,16,128]{2,1,0:T(8,128)(2,1)S(1)} %fusion.1), channel_id=1, source_target_pairs={{0,128},{16,144},{32,160},{48,176},{64,192},{80,208},{96,224},{112... | collective-permute-start | bytes 860168 | tf_op jit(solution)/shard_map/z_hi/ppermute | solution.py:137
  84.4 2.2 %collective-permute-start.30 = (bf16[35,16,128]{2,1,0:T(8,128)(2,1)S(1)}, bf16[35,16,128]{2,1,0:T(8,128)(2,1)S(1)}, u32[]{:S(2)}, u32[]{:S(2)}) collective-permute-start(bf16[35,16,128]{2,1,0:T(8,128)(2,1)S(1)} %get-tuple-element.45), channel_id=1, source_target_pairs={{0,32},{16,48},{32,64},{48,80},{64,96},{80,112},{96,0},{112,16},{1... | collective-permute-start | bytes 430088 | tf_op jit(solution)/shard_map/x/ppermute | solution.py:132
  86.7 1.4 %collective-permute-start.33 = (bf16[70,16,128]{2,1,0:T(8,128)(2,1)S(1)}, bf16[70,16,128]{2,1,0:T(8,128)(2,1)S(1)}, u32[]{:S(2)}, u32[]{:S(2)}) collective-permute-start(bf16[70,16,128]{2,1,0:T(8,128)(2,1)S(1)} %pad_maximum_fusion.6), channel_id=1, source_target_pairs={{0,96},{16,112},{32,0},{48,16},{64,32},{80,48},{96,64},{112,80},{1... | collective-permute-start | bytes 860168 | tf_op jit(solution)/shard_map/x/ppermute | solution.py:132
  88.1 2.9 %collective-permute-done.30 = bf16[35,16,128]{2,1,0:T(8,128)(2,1)S(1)} collective-permute-done((bf16[35,16,128]{2,1,0:T(8,128)(2,1)S(1)}, bf16[35,16,128]{2,1,0:T(8,128)(2,1)S(1)}, u32[]{:S(2)}, u32[]{:S(2)}) %collective-permute-start.30) | collective-permute-done | bytes 143392 | tf_op jit(solution)/shard_map/x/ppermute | solution.py:132
  91.1 2.3 %collective-permute-start.31 = (bf16[70,16,128]{2,1,0:T(8,128)(2,1)S(1)}, bf16[70,16,128]{2,1,0:T(8,128)(2,1)S(1)}, u32[]{:S(2)}, u32[]{:S(2)}) collective-permute-start(bf16[70,16,128]{2,1,0:T(8,128)(2,1)S(1)} %pad_maximum_fusion.5), channel_id=1, source_target_pairs={{0,32},{16,48},{32,64},{48,80},{64,96},{80,112},{96,0},{112,16},{1... | collective-permute-start | bytes 860168 | tf_op jit(solution)/shard_map/x/ppermute | solution.py:132
  93.4 0.2 fusion.29
  93.7 6.7 %collective-permute-start.29 = (bf16[128,512]{1,0:T(8,128)(2,1)S(1)}, bf16[128,512]{1,0:T(8,128)(2,1)S(1)}, u32[]{:S(2)}, u32[]{:S(2)}) collective-permute-start(bf16[128,512]{1,0:T(8,128)(2,1)S(1)} %get-tuple-element.43), channel_id=1, source_target_pairs={{0,4},{1,5},{2,6},{3,7},{4,8},{5,9},{6,10},{7,11},{8,12},{9,13},{1... | collective-permute-start | bytes 393224 | tf_op jit(solution)/shard_map/z_lo/ppermute | solution.py:122
  100.4 1.3 %collective-permute-start.28 = (bf16[128,512]{1,0:T(8,128)(2,1)S(1)}, bf16[128,512]{1,0:T(8,128)(2,1)S(1)}, u32[]{:S(2)}, u32[]{:S(2)}) collective-permute-start(bf16[128,512]{1,0:T(8,128)(2,1)S(1)} %get-tuple-element.44), channel_id=1, source_target_pairs={{0,8},{1,9},{2,10},{3,11},{4,12},{5,13},{6,14},{7,15},{8,0},{9,1},... | collective-permute-start | bytes 393224 | tf_op jit(solution)/shard_map/z_lo/ppermute | solution.py:122
  101.7 2.9 %collective-permute-start.27 = (bf16[128,512]{1,0:T(8,128)(2,1)S(1)}, bf16[128,512]{1,0:T(8,128)(2,1)S(1)}, u32[]{:S(2)}, u32[]{:S(2)}) collective-permute-start(bf16[128,512]{1,0:T(8,128)(2,1)S(1)} %get-tuple-element.42), channel_id=1, source_target_pairs={{0,12},{1,13},{2,14},{3,15},{4,0},{5,1},{6,2},{7,3},{8,4},{9,5},{1... | collective-permute-start | bytes 393224 | tf_op jit(solution)/shard_map/z_lo/ppermute | solution.py:122
  104.9 3.5 %shard_map.77 = bf16[128,896]{1,0:T(8,128)(2,1)} custom-call(s32[140]{0:T(256)S(1)} %pad_add_fusion.pos_ref, s32[8]{0:T(128)S(1)} %fusion.24.chip_ref, bf16[65,128,128]{2,1,0:T(8,128)(2,1)S(1)} %constant_dynamic-update-slice_fusion.acts_ref, bf16[8,70,16,128]{3,2,1,0:T(8,128)(2,1)S(1)} %bitcast_dynamic-update-slice_fusion.w0_ref, ...), custom_call_target="tpu_custom_call" | custom-call | flops 587202560 | bytes 6947408 | tf_op jit(solution)/shard_map/pallas_call | solution.py:105
  108.5 0.7 add_convert_fusion.12
  109.2 0.8 maximum_select_fusion
  (85 shorter events, 2.9 us)
Async XLA Ops:
  1.8 11.2 %collective-permute-start.2 = (bf16[4,128,128]{2,1,0:T(8,128)(2,1)S(1)}, bf16[4,128,128]{2,1,0:T(8,128)(2,1)S(1)}, u32[]{:S(2)}, u32[]{:S(2)}) collective-permute-start(bf16[4,128,128]{2,1,0:T(8,128)(2,1)S(1)} %bitcast.68), channel_id=1, source_target_pairs={{0,12},{1,13},{2,14},{3,15},{4,0},{5,1},{6,2},{7,3},{8,4},{9,5},{1... | collective-permute-start | bytes 393224 | tf_op jit(solution)/shard_map/z_lo/ppermute | solution.py:122
  6.5 11.9 %collective-permute-start.1 = (bf16[4,128,128]{2,1,0:T(8,128)(2,1)S(1)}, bf16[4,128,128]{2,1,0:T(8,128)(2,1)S(1)}, u32[]{:S(2)}, u32[]{:S(2)}) collective-permute-start(bf16[4,128,128]{2,1,0:T(8,128)(2,1)S(1)} %bitcast.69), channel_id=1, source_target_pairs={{0,8},{1,9},{2,10},{3,11},{4,12},{5,13},{6,14},{7,15},{8,0},{9,1},... | collective-permute-start | bytes 393224 | tf_op jit(solution)/shard_map/z_lo/ppermute | solution.py:122
  6.5 11.9 %collective-permute-start = (bf16[4,128,128]{2,1,0:T(8,128)(2,1)S(1)}, bf16[4,128,128]{2,1,0:T(8,128)(2,1)S(1)}, u32[]{:S(2)}, u32[]{:S(2)}) collective-permute-start(bf16[4,128,128]{2,1,0:T(8,128)(2,1)S(1)} %bitcast.70), channel_id=1, source_target_pairs={{0,4},{1,5},{2,6},{3,7},{4,8},{5,9},{6,10},{7,11},{8,12},{9,13},{1... | collective-permute-start | bytes 393224 | tf_op jit(solution)/shard_map/z_lo/ppermute | solution.py:122
  8.2 1.5 %collective-permute-start.3 = (bf16[7,10,8,128]{3,2,1,0:T(8,128)(2,1)S(1)}, bf16[7,10,8,128]{3,2,1,0:T(8,128)(2,1)S(1)}, u32[]{:S(2)}, u32[]{:S(2)}) collective-permute-start(bf16[7,10,8,128]{3,2,1,0:T(8,128)(2,1)S(1)} %get-tuple-element.50), channel_id=1, source_target_pairs={{0,16},{16,0},{32,48},{48,32},{64,80},{80,64},{96,112},{112,96},{1... | collective-permute-start | bytes 430088 | tf_op jit(solution)/shard_map/core/ppermute | solution.py:142
  9.7 13.3 %collective-permute-start.14 = (bf16[70,16,128]{2,1,0:T(8,128)(2,1)S(1)}, bf16[70,16,128]{2,1,0:T(8,128)(2,1)S(1)}, u32[]{:S(2)}, u32[]{:S(2)}) collective-permute-start(bf16[70,16,128]{2,1,0:T(8,128)(2,1)S(1)} %maximum_select_fusion.1), channel_id=1, source_target_pairs={{0,32},{16,48},{32,64},{48,80},{64,96},{80,112},{96,0},{112,16},{1... | collective-permute-start | bytes 860168 | tf_op jit(solution)/shard_map/x/ppermute | solution.py:132
  11.3 9.5 %collective-permute-start.16 = (bf16[70,16,128]{2,1,0:T(8,128)(2,1)S(1)}, bf16[70,16,128]{2,1,0:T(8,128)(2,1)S(1)}, u32[]{:S(2)}, u32[]{:S(2)}) collective-permute-start(bf16[70,16,128]{2,1,0:T(8,128)(2,1)S(1)} %maximum_select_fusion.1), channel_id=1, source_target_pairs={{0,96},{16,112},{32,0},{48,16},{64,32},{80,48},{96,64},{112,80},{1... | collective-permute-start | bytes 860168 | tf_op jit(solution)/shard_map/x/ppermute | solution.py:132
  13.0 14.3 %collective-permute-start.18 = (bf16[70,16,128]{2,1,0:T(8,128)(2,1)S(1)}, bf16[70,16,128]{2,1,0:T(8,128)(2,1)S(1)}, u32[]{:S(2)}, u32[]{:S(2)}) collective-permute-start(bf16[70,16,128]{2,1,0:T(8,128)(2,1)S(1)} %maximum_select_fusion.1), channel_id=1, source_target_pairs={{0,128},{16,144},{32,160},{48,176},{64,192},{80,208},{96,224},{112... | collective-permute-start | bytes 860168 | tf_op jit(solution)/shard_map/z_hi/ppermute | solution.py:137
  18.5 15.8 %collective-permute-start.4 = (bf16[16,128,128]{2,1,0:T(8,128)(2,1)S(1)}, bf16[16,128,128]{2,1,0:T(8,128)(2,1)S(1)}, u32[]{:S(2)}, u32[]{:S(2)}) collective-permute-start(bf16[16,128,128]{2,1,0:T(8,128)(2,1)S(1)} %pad_maximum_fusion), channel_id=1, source_target_pairs={{0,1},{1,2},{2,3},{3,0},{4,5},{5,6},{6,7},{7,4},{8,9},{9,10},{10,1... | collective-permute-start | bytes 1572872 | tf_op jit(solution)/shard_map/y/ppermute | solution.py:127
  18.8 15.8 %collective-permute-start.6 = (bf16[16,128,128]{2,1,0:T(8,128)(2,1)S(1)}, bf16[16,128,128]{2,1,0:T(8,128)(2,1)S(1)}, u32[]{:S(2)}, u32[]{:S(2)}) collective-permute-start(bf16[16,128,128]{2,1,0:T(8,128)(2,1)S(1)} %pad_maximum_fusion), channel_id=1, source_target_pairs={{0,3},{1,0},{2,1},{3,2},{4,7},{5,4},{6,5},{7,6},{8,11},{9,8},{10,9... | collective-permute-start | bytes 1572872 | tf_op jit(solution)/shard_map/y/ppermute | solution.py:127
  20.8 9.1 %collective-permute-start.17 = (bf16[35,16,128]{2,1,0:T(8,128)(2,1)S(1)}, bf16[35,16,128]{2,1,0:T(8,128)(2,1)S(1)}, u32[]{:S(2)}, u32[]{:S(2)}) collective-permute-start(bf16[35,16,128]{2,1,0:T(8,128)(2,1)S(1)} %slice.224), channel_id=1, source_target_pairs={{0,96},{16,112},{32,0},{48,16},{64,32},{80,48},{96,64},{112,80},{1... | collective-permute-start | bytes 430088 | tf_op jit(solution)/shard_map/x/ppermute | solution.py:132
  23.1 9.6 %collective-permute-start.15 = (bf16[35,16,128]{2,1,0:T(8,128)(2,1)S(1)}, bf16[35,16,128]{2,1,0:T(8,128)(2,1)S(1)}, u32[]{:S(2)}, u32[]{:S(2)}) collective-permute-start(bf16[35,16,128]{2,1,0:T(8,128)(2,1)S(1)} %slice.223), channel_id=1, source_target_pairs={{0,32},{16,48},{32,64},{48,80},{64,96},{80,112},{96,0},{112,16},{1... | collective-permute-start | bytes 430088 | tf_op jit(solution)/shard_map/x/ppermute | solution.py:132
  27.3 12.0 %collective-permute-start.19 = (bf16[70,16,128]{2,1,0:T(8,128)(2,1)S(1)}, bf16[70,16,128]{2,1,0:T(8,128)(2,1)S(1)}, u32[]{:S(2)}, u32[]{:S(2)}) collective-permute-start(bf16[70,16,128]{2,1,0:T(8,128)(2,1)S(1)} %collective-permute-done.18), channel_id=1, source_target_pairs={{0,32},{16,48},{32,64},{48,80},{64,96},{80,112},{96,0},{112,16},{1... | collective-permute-start | bytes 860168 | tf_op jit(solution)/shard_map/x/ppermute | solution.py:132
  29.9 13.4 %collective-permute-start.20 = (bf16[70,16,128]{2,1,0:T(8,128)(2,1)S(1)}, bf16[70,16,128]{2,1,0:T(8,128)(2,1)S(1)}, u32[]{:S(2)}, u32[]{:S(2)}) collective-permute-start(bf16[70,16,128]{2,1,0:T(8,128)(2,1)S(1)} %collective-permute-done.18), channel_id=1, source_target_pairs={{0,64},{16,80},{32,96},{48,112},{64,0},{80,16},{96,32},{112,48},{1... | collective-permute-start | bytes 860168 | tf_op jit(solution)/shard_map/x/ppermute | solution.py:132
  32.7 10.9 %collective-permute-start.21 = (bf16[70,16,128]{2,1,0:T(8,128)(2,1)S(1)}, bf16[70,16,128]{2,1,0:T(8,128)(2,1)S(1)}, u32[]{:S(2)}, u32[]{:S(2)}) collective-permute-start(bf16[70,16,128]{2,1,0:T(8,128)(2,1)S(1)} %collective-permute-done.18), channel_id=1, source_target_pairs={{0,96},{16,112},{32,0},{48,16},{64,32},{80,48},{96,64},{112,80},{1... | collective-permute-start | bytes 860168 | tf_op jit(solution)/shard_map/x/ppermute | solution.py:132
  34.3 9.4 %collective-permute-start.5 = (bf16[8,128,128]{2,1,0:T(8,128)(2,1)S(1)}, bf16[8,128,128]{2,1,0:T(8,128)(2,1)S(1)}, u32[]{:S(2)}, u32[]{:S(2)}) collective-permute-start(bf16[8,128,128]{2,1,0:T(8,128)(2,1)S(1)} %slice.211), channel_id=1, source_target_pairs={{0,1},{1,2},{2,3},{3,0},{4,5},{5,6},{6,7},{7,4},{8,9},{9,10},{10,1... | collective-permute-start | bytes 786440 | tf_op jit(solution)/shard_map/y/ppermute | solution.py:127
  34.6 9.3 %copy-start = (bf16[128,896]{1,0:T(8,128)(2,1)S(1)}, bf16[128,896]{1,0:T(8,128)(2,1)}, u32[]{:S(2)}) copy-start(bf16[128,896]{1,0:T(8,128)(2,1)} %up_ref.3) | copy-start | bytes 688132
  34.7 9.1 %collective-permute-start.7 = (bf16[8,128,128]{2,1,0:T(8,128)(2,1)S(1)}, bf16[8,128,128]{2,1,0:T(8,128)(2,1)S(1)}, u32[]{:S(2)}, u32[]{:S(2)}) collective-permute-start(bf16[8,128,128]{2,1,0:T(8,128)(2,1)S(1)} %slice.212), channel_id=1, source_target_pairs={{0,3},{1,0},{2,1},{3,2},{4,7},{5,4},{6,5},{7,6},{8,11},{9,8},{10,9... | collective-permute-start | bytes 786440 | tf_op jit(solution)/shard_map/y/ppermute | solution.py:127
  43.6 4.5 %collective-permute-start.22 = (bf16[8,70,16,128]{3,2,1,0:T(8,128)(2,1)S(1)}, bf16[8,70,16,128]{3,2,1,0:T(8,128)(2,1)S(1)}, u32[]{:S(2)}, u32[]{:S(2)}) collective-permute-start(bf16[8,70,16,128]{3,2,1,0:T(8,128)(2,1)S(1)} %bitcast_dynamic-update-slice_fusion.w0_ref), channel_id=1, source_target_pairs={{0,16},{16,0},{32,48},{48,32},{64,80},{80,64},{96,112},{112,96},{1... | collective-permute-start | bytes 6881288 | tf_op jit(solution)/shard_map/core/ppermute | solution.py:142
  47.1 8.1 %collective-permute-start.8 = (bf16[8,70,16,128]{3,2,1,0:T(8,128)(2,1)S(1)}, bf16[8,70,16,128]{3,2,1,0:T(8,128)(2,1)S(1)}, u32[]{:S(2)}, u32[]{:S(2)}) collective-permute-start(bf16[8,70,16,128]{3,2,1,0:T(8,128)(2,1)S(1)} %get-tuple-element.19), channel_id=1, source_target_pairs={{0,16},{16,0},{32,48},{48,32},{64,80},{80,64},{96,112},{112,96},{1... | collective-permute-start | bytes 6881288 | tf_op jit(solution)/shard_map/core/ppermute | solution.py:142
  51.8 13.5 %collective-permute-start.25 = (bf16[2,128,512]{2,1,0:T(8,128)(2,1)S(1)}, bf16[2,128,512]{2,1,0:T(8,128)(2,1)S(1)}, u32[]{:S(2)}, u32[]{:S(2)}) collective-permute-start(bf16[2,128,512]{2,1,0:T(8,128)(2,1)S(1)} %get-tuple-element.25), channel_id=1, source_target_pairs={{0,3},{1,0},{2,1},{3,2},{4,7},{5,4},{6,5},{7,6},{8,11},{9,8},{10,9... | collective-permute-start | bytes 786440 | tf_op jit(solution)/shard_map/y/ppermute | solution.py:127
  52.6 21.4 %collective-permute-start.23 = (bf16[2,128,512]{2,1,0:T(8,128)(2,1)S(1)}, bf16[2,128,512]{2,1,0:T(8,128)(2,1)S(1)}, u32[]{:S(2)}, u32[]{:S(2)}) collective-permute-start(bf16[2,128,512]{2,1,0:T(8,128)(2,1)S(1)} %get-tuple-element.23), channel_id=1, source_target_pairs={{0,1},{1,2},{2,3},{3,0},{4,5},{5,6},{6,7},{7,4},{8,9},{9,10},{10,1... | collective-permute-start | bytes 786440 | tf_op jit(solution)/shard_map/y/ppermute | solution.py:127
  55.8 5.4 %collective-permute-start.11 = (bf16[35,16,128]{2,1,0:T(8,128)(2,1)S(1)}, bf16[35,16,128]{2,1,0:T(8,128)(2,1)S(1)}, u32[]{:S(2)}, u32[]{:S(2)}) collective-permute-start(bf16[35,16,128]{2,1,0:T(8,128)(2,1)S(1)} %get-tuple-element.48), channel_id=1, source_target_pairs={{0,96},{16,112},{32,0},{48,16},{64,32},{80,48},{96,64},{112,80},{1... | collective-permute-start | bytes 430088 | tf_op jit(solution)/shard_map/x/ppermute | solution.py:132
  58.5 6.6 %collective-permute-start.9 = (bf16[35,16,128]{2,1,0:T(8,128)(2,1)S(1)}, bf16[35,16,128]{2,1,0:T(8,128)(2,1)S(1)}, u32[]{:S(2)}, u32[]{:S(2)}) collective-permute-start(bf16[35,16,128]{2,1,0:T(8,128)(2,1)S(1)} %get-tuple-element.47), channel_id=1, source_target_pairs={{0,32},{16,48},{32,64},{48,80},{64,96},{80,112},{96,0},{112,16},{1... | collective-permute-start | bytes 430088 | tf_op jit(solution)/shard_map/x/ppermute | solution.py:132
  61.3 8.7 %collective-permute-start.12 = (bf16[70,16,128]{2,1,0:T(8,128)(2,1)S(1)}, bf16[70,16,128]{2,1,0:T(8,128)(2,1)S(1)}, u32[]{:S(2)}, u32[]{:S(2)}) collective-permute-start(bf16[70,16,128]{2,1,0:T(8,128)(2,1)S(1)} %pad_maximum_fusion.4), channel_id=1, source_target_pairs={{0,96},{16,112},{32,0},{48,16},{64,32},{80,48},{96,64},{112,80},{1... | collective-permute-start | bytes 860168 | tf_op jit(solution)/shard_map/x/ppermute | solution.py:132
  65.2 8.4 %collective-permute-start.10 = (bf16[70,16,128]{2,1,0:T(8,128)(2,1)S(1)}, bf16[70,16,128]{2,1,0:T(8,128)(2,1)S(1)}, u32[]{:S(2)}, u32[]{:S(2)}) collective-permute-start(bf16[70,16,128]{2,1,0:T(8,128)(2,1)S(1)} %pad_maximum_fusion.3), channel_id=1, source_target_pairs={{0,32},{16,48},{32,64},{48,80},{64,96},{80,112},{96,0},{112,16},{1... | collective-permute-start | bytes 860168 | tf_op jit(solution)/shard_map/x/ppermute | solution.py:132
  65.4 28.0 %collective-permute-start.26 = (bf16[4,128,512]{2,1,0:T(8,128)(2,1)S(1)}, bf16[4,128,512]{2,1,0:T(8,128)(2,1)S(1)}, u32[]{:S(2)}, u32[]{:S(2)}) collective-permute-start(bf16[4,128,512]{2,1,0:T(8,128)(2,1)S(1)} %pad_maximum_fusion.2), channel_id=1, source_target_pairs={{0,3},{1,0},{2,1},{3,2},{4,7},{5,4},{6,5},{7,6},{8,11},{9,8},{10,9... | collective-permute-start | bytes 1572872 | tf_op jit(solution)/shard_map/y/ppermute | solution.py:127
  73.8 12.8 %collective-permute-start.32 = (bf16[35,16,128]{2,1,0:T(8,128)(2,1)S(1)}, bf16[35,16,128]{2,1,0:T(8,128)(2,1)S(1)}, u32[]{:S(2)}, u32[]{:S(2)}) collective-permute-start(bf16[35,16,128]{2,1,0:T(8,128)(2,1)S(1)} %get-tuple-element.46), channel_id=1, source_target_pairs={{0,96},{16,112},{32,0},{48,16},{64,32},{80,48},{96,64},{112,80},{1... | collective-permute-start | bytes 430088 | tf_op jit(solution)/shard_map/x/ppermute | solution.py:132
  74.1 19.3 %collective-permute-start.24 = (bf16[4,128,512]{2,1,0:T(8,128)(2,1)S(1)}, bf16[4,128,512]{2,1,0:T(8,128)(2,1)S(1)}, u32[]{:S(2)}, u32[]{:S(2)}) collective-permute-start(bf16[4,128,512]{2,1,0:T(8,128)(2,1)S(1)} %pad_maximum_fusion.1), channel_id=1, source_target_pairs={{0,1},{1,2},{2,3},{3,0},{4,5},{5,6},{6,7},{7,4},{8,9},{9,10},{10,1... | collective-permute-start | bytes 1572872 | tf_op jit(solution)/shard_map/y/ppermute | solution.py:127
  74.8 26.9 %collective-permute-start.13 = (bf16[70,16,128]{2,1,0:T(8,128)(2,1)S(1)}, bf16[70,16,128]{2,1,0:T(8,128)(2,1)S(1)}, u32[]{:S(2)}, u32[]{:S(2)}) collective-permute-start(bf16[70,16,128]{2,1,0:T(8,128)(2,1)S(1)} %fusion.1), channel_id=1, source_target_pairs={{0,128},{16,144},{32,160},{48,176},{64,192},{80,208},{96,224},{112... | collective-permute-start | bytes 860168 | tf_op jit(solution)/shard_map/z_hi/ppermute | solution.py:137
  84.4 6.6 %collective-permute-start.30 = (bf16[35,16,128]{2,1,0:T(8,128)(2,1)S(1)}, bf16[35,16,128]{2,1,0:T(8,128)(2,1)S(1)}, u32[]{:S(2)}, u32[]{:S(2)}) collective-permute-start(bf16[35,16,128]{2,1,0:T(8,128)(2,1)S(1)} %get-tuple-element.45), channel_id=1, source_target_pairs={{0,32},{16,48},{32,64},{48,80},{64,96},{80,112},{96,0},{112,16},{1... | collective-permute-start | bytes 430088 | tf_op jit(solution)/shard_map/x/ppermute | solution.py:132
  86.7 17.9 %collective-permute-start.33 = (bf16[70,16,128]{2,1,0:T(8,128)(2,1)S(1)}, bf16[70,16,128]{2,1,0:T(8,128)(2,1)S(1)}, u32[]{:S(2)}, u32[]{:S(2)}) collective-permute-start(bf16[70,16,128]{2,1,0:T(8,128)(2,1)S(1)} %pad_maximum_fusion.6), channel_id=1, source_target_pairs={{0,96},{16,112},{32,0},{48,16},{64,32},{80,48},{96,64},{112,80},{1... | collective-permute-start | bytes 860168 | tf_op jit(solution)/shard_map/x/ppermute | solution.py:132
  91.1 13.5 %collective-permute-start.31 = (bf16[70,16,128]{2,1,0:T(8,128)(2,1)S(1)}, bf16[70,16,128]{2,1,0:T(8,128)(2,1)S(1)}, u32[]{:S(2)}, u32[]{:S(2)}) collective-permute-start(bf16[70,16,128]{2,1,0:T(8,128)(2,1)S(1)} %pad_maximum_fusion.5), channel_id=1, source_target_pairs={{0,32},{16,48},{32,64},{48,80},{64,96},{80,112},{96,0},{112,16},{1... | collective-permute-start | bytes 860168 | tf_op jit(solution)/shard_map/x/ppermute | solution.py:132
  93.7 14.8 %collective-permute-start.29 = (bf16[128,512]{1,0:T(8,128)(2,1)S(1)}, bf16[128,512]{1,0:T(8,128)(2,1)S(1)}, u32[]{:S(2)}, u32[]{:S(2)}) collective-permute-start(bf16[128,512]{1,0:T(8,128)(2,1)S(1)} %get-tuple-element.43), channel_id=1, source_target_pairs={{0,4},{1,5},{2,6},{3,7},{4,8},{5,9},{6,10},{7,11},{8,12},{9,13},{1... | collective-permute-start | bytes 393224 | tf_op jit(solution)/shard_map/z_lo/ppermute | solution.py:122
  100.4 8.1 %collective-permute-start.28 = (bf16[128,512]{1,0:T(8,128)(2,1)S(1)}, bf16[128,512]{1,0:T(8,128)(2,1)S(1)}, u32[]{:S(2)}, u32[]{:S(2)}) collective-permute-start(bf16[128,512]{1,0:T(8,128)(2,1)S(1)} %get-tuple-element.44), channel_id=1, source_target_pairs={{0,8},{1,9},{2,10},{3,11},{4,12},{5,13},{6,14},{7,15},{8,0},{9,1},... | collective-permute-start | bytes 393224 | tf_op jit(solution)/shard_map/z_lo/ppermute | solution.py:122
  101.7 6.8 %collective-permute-start.27 = (bf16[128,512]{1,0:T(8,128)(2,1)S(1)}, bf16[128,512]{1,0:T(8,128)(2,1)S(1)}, u32[]{:S(2)}, u32[]{:S(2)}) collective-permute-start(bf16[128,512]{1,0:T(8,128)(2,1)S(1)} %get-tuple-element.42), channel_id=1, source_target_pairs={{0,12},{1,13},{2,14},{3,15},{4,0},{5,1},{6,2},{7,3},{8,4},{9,5},{1... | collective-permute-start | bytes 393224 | tf_op jit(solution)/shard_map/z_lo/ppermute | solution.py:122
  104.8 4.4 %collective-permute-start.34 = (f32[7,10,8,128]{3,2,1,0:T(8,128)S(1)}, f32[7,10,8,128]{3,2,1,0:T(8,128)S(1)}, u32[]{:S(2)}, u32[]{:S(2)}) collective-permute-start(f32[7,10,8,128]{3,2,1,0:T(8,128)S(1)} %get-tuple-element.41), channel_id=1, source_target_pairs={{0,16},{16,0},{32,48},{48,32},{64,80},{80,64},{96,112},{112,96},{1... | collective-permute-start | bytes 860168 | tf_op jit(solution)/shard_map/core/ppermute | solution.py:142

commit v5 on v4

--- a/solution.py
+++ b/solution.py
@@ -202,8 +202,12 @@
     chips = jnp.arange(8, dtype=jnp.int32)
     chip = (zh + chips // NX) % 2 * NX + (x - chips % NX) % NX
 
-    mine, other = halves(values)
-    rows16 = ordered(mine, core_step(other), 2).reshape(cols * half, 16, BLK)
+    came = core_step(values)
+    rows16 = jnp.where(
+        first,
+        jnp.concatenate([values[:, :half], came[:, :half]], axis=2),
+        jnp.concatenate([came[:, half:], values[:, half:]], axis=2),
+    ).reshape(cols * half, 16, BLK)
 
     own = acts.reshape(tokens, own_blocks, BLK).transpose(1, 0, 2)
     along_z = jnp.concatenate([own] + [z_step(own, q) for q in range(1, NZ)])

time: 112 us -> 112 us (level)
  transfers between devices with their start and end apart: 35 -> 35, of which waited for: 10 -> 9; matrix products, arithmetic and copies ran while one was open for 5% -> 5% of each run, Pallas kernels for 9% -> 9%
where the time goes in v5:
time: 112 us; the launch traced here: 110 us
  starting transfers between devices  66 us (59%)
  waiting for transfers between devices  25.1 us (22%)
  Pallas kernels  10.4 us (9%)
  other arithmetic  4.48 us (4%)
  local copies, waits for them, and re-layouts  3.07 us (3%)
    ppermute x15, starting transfers between devices, x_step(): return lax.ppermute(a, 'dp', x_pairs(s))  25.4 us
    ppermute x15, waiting for transfers between devices, x_step(): return lax.ppermute(a, 'dp', x_pairs(s))  20.4 us
    ppermute x6, starting transfers between devices, z_step(): return lax.ppermute(a, 'mp', z_pairs(q))  16.3 us
    ppermute x2, starting transfers between devices, zh_step(): return lax.ppermute(a, 'dp', HALF_PAIRS)  14.9 us
    pallas_call x3, Pallas kernels, kernel_call(): pl.pallas_call(body, out_shape=outs, in_specs=specs, out_specs=[pl.BlockS...  10.4 us
    ppermute x8, starting transfers between devices, y_step(): return lax.ppermute(a, 'mp', y_pairs(p))  8.64 us
    ppermute x2, waiting for transfers between devices, zh_step(): return lax.ppermute(a, 'dp', HALF_PAIRS)  4.23 us
  transfers between devices with their start and end apart: 35, of which 9 were waited for; matrix products, arithmetic and copies ran while one was open for 5% of the time, Pallas kernels for 9%

profile of v5, /device:TPU:24, one launch (start us, length us, event | category | flops | bytes accessed | tf_op | source)
XLA Modules:
  0.0 110.2 jit_solution(40024407489664242)
XLA Ops:
  0.6 1.0 copy.8
  1.8 4.7 %collective-permute-start.2 = (bf16[4,128,128]{2,1,0:T(8,128)(2,1)S(1)}, bf16[4,128,128]{2,1,0:T(8,128)(2,1)S(1)}, u32[]{:S(2)}, u32[]{:S(2)}) collective-permute-start(bf16[4,128,128]{2,1,0:T(8,128)(2,1)S(1)} %bitcast.76), channel_id=1, source_target_pairs={{0,12},{1,13},{2,14},{3,15},{4,0},{5,1},{6,2},{7,3},{8,4},{9,5},{1... | collective-permute-start | bytes 393224 | tf_op jit(solution)/shard_map/z_lo/ppermute | solution.py:122
  6.5 0.7 collective-permute-start
  7.2 0.8 fusion.17
  8.3 1.0 fusion.32
  9.4 1.6 %collective-permute-start.14 = (bf16[70,16,128]{2,1,0:T(8,128)(2,1)S(1)}, bf16[70,16,128]{2,1,0:T(8,128)(2,1)S(1)}, u32[]{:S(2)}, u32[]{:S(2)}) collective-permute-start(bf16[70,16,128]{2,1,0:T(8,128)(2,1)S(1)} %maximum_select_fusion.1), channel_id=1, source_target_pairs={{0,32},{16,48},{32,64},{48,80},{64,96},{80,112},{96,0},{112,16},{1... | collective-permute-start | bytes 860168 | tf_op jit(solution)/shard_map/x/ppermute | solution.py:132
  11.0 1.7 %collective-permute-start.16 = (bf16[70,16,128]{2,1,0:T(8,128)(2,1)S(1)}, bf16[70,16,128]{2,1,0:T(8,128)(2,1)S(1)}, u32[]{:S(2)}, u32[]{:S(2)}) collective-permute-start(bf16[70,16,128]{2,1,0:T(8,128)(2,1)S(1)} %maximum_select_fusion.1), channel_id=1, source_target_pairs={{0,96},{16,112},{32,0},{48,16},{64,32},{80,48},{96,64},{112,80},{1... | collective-permute-start | bytes 860168 | tf_op jit(solution)/shard_map/x/ppermute | solution.py:132
  12.7 5.4 %collective-permute-start.18 = (bf16[70,16,128]{2,1,0:T(8,128)(2,1)S(1)}, bf16[70,16,128]{2,1,0:T(8,128)(2,1)S(1)}, u32[]{:S(2)}, u32[]{:S(2)}) collective-permute-start(bf16[70,16,128]{2,1,0:T(8,128)(2,1)S(1)} %maximum_select_fusion.1), channel_id=1, source_target_pairs={{0,128},{16,144},{32,160},{48,176},{64,192},{80,208},{96,224},{112... | collective-permute-start | bytes 860168 | tf_op jit(solution)/shard_map/z_hi/ppermute | solution.py:137
  18.2 0.3 collective-permute-start.4
  18.5 1.8 %collective-permute-start.6 = (bf16[16,128,128]{2,1,0:T(8,128)(2,1)S(1)}, bf16[16,128,128]{2,1,0:T(8,128)(2,1)S(1)}, u32[]{:S(2)}, u32[]{:S(2)}) collective-permute-start(bf16[16,128,128]{2,1,0:T(8,128)(2,1)S(1)} %pad_maximum_fusion), channel_id=1, source_target_pairs={{0,3},{1,0},{2,1},{3,2},{4,7},{5,4},{6,5},{7,6},{8,11},{9,8},{10,9... | collective-permute-start | bytes 1572872 | tf_op jit(solution)/shard_map/y/ppermute | solution.py:127
  20.5 2.5 %collective-permute-start.17 = (bf16[35,16,128]{2,1,0:T(8,128)(2,1)S(1)}, bf16[35,16,128]{2,1,0:T(8,128)(2,1)S(1)}, u32[]{:S(2)}, u32[]{:S(2)}) collective-permute-start(bf16[35,16,128]{2,1,0:T(8,128)(2,1)S(1)} %slice.232), channel_id=1, source_target_pairs={{0,96},{16,112},{32,0},{48,16},{64,32},{80,48},{96,64},{112,80},{1... | collective-permute-start | bytes 430088 | tf_op jit(solution)/shard_map/x/ppermute | solution.py:132
  23.1 4.2 %collective-permute-done.18 = bf16[70,16,128]{2,1,0:T(8,128)(2,1)S(1)} collective-permute-done((bf16[70,16,128]{2,1,0:T(8,128)(2,1)S(1)}, bf16[70,16,128]{2,1,0:T(8,128)(2,1)S(1)}, u32[]{:S(2)}, u32[]{:S(2)}) %collective-permute-start.18) | collective-permute-done | bytes 286752 | tf_op jit(solution)/shard_map/z_hi/ppermute | solution.py:137
  27.3 2.5 %collective-permute-start.19 = (bf16[70,16,128]{2,1,0:T(8,128)(2,1)S(1)}, bf16[70,16,128]{2,1,0:T(8,128)(2,1)S(1)}, u32[]{:S(2)}, u32[]{:S(2)}) collective-permute-start(bf16[70,16,128]{2,1,0:T(8,128)(2,1)S(1)} %collective-permute-done.18), channel_id=1, source_target_pairs={{0,32},{16,48},{32,64},{48,80},{64,96},{80,112},{96,0},{112,16},{1... | collective-permute-start | bytes 860168 | tf_op jit(solution)/shard_map/x/ppermute | solution.py:132
  29.9 2.8 %collective-permute-start.20 = (bf16[70,16,128]{2,1,0:T(8,128)(2,1)S(1)}, bf16[70,16,128]{2,1,0:T(8,128)(2,1)S(1)}, u32[]{:S(2)}, u32[]{:S(2)}) collective-permute-start(bf16[70,16,128]{2,1,0:T(8,128)(2,1)S(1)} %collective-permute-done.18), channel_id=1, source_target_pairs={{0,64},{16,80},{32,96},{48,112},{64,0},{80,16},{96,32},{112,48},{1... | collective-permute-start | bytes 860168 | tf_op jit(solution)/shard_map/x/ppermute | solution.py:132
  32.7 1.4 %collective-permute-start.21 = (bf16[70,16,128]{2,1,0:T(8,128)(2,1)S(1)}, bf16[70,16,128]{2,1,0:T(8,128)(2,1)S(1)}, u32[]{:S(2)}, u32[]{:S(2)}) collective-permute-start(bf16[70,16,128]{2,1,0:T(8,128)(2,1)S(1)} %collective-permute-done.18), channel_id=1, source_target_pairs={{0,96},{16,112},{32,0},{48,16},{64,32},{80,48},{96,64},{112,80},{1... | collective-permute-start | bytes 860168 | tf_op jit(solution)/shard_map/x/ppermute | solution.py:132
  34.3 0.3 collective-permute-start.5
  34.7 2.1 %collective-permute-start.7 = (bf16[8,128,128]{2,1,0:T(8,128)(2,1)S(1)}, bf16[8,128,128]{2,1,0:T(8,128)(2,1)S(1)}, u32[]{:S(2)}, u32[]{:S(2)}) collective-permute-start(bf16[8,128,128]{2,1,0:T(8,128)(2,1)S(1)} %slice.220), channel_id=1, source_target_pairs={{0,3},{1,0},{2,1},{3,2},{4,7},{5,4},{6,5},{7,6},{8,11},{9,8},{10,9... | collective-permute-start | bytes 786440 | tf_op jit(solution)/shard_map/y/ppermute | solution.py:127
  36.8 2.7 %collective-permute-done.19 = bf16[70,16,128]{2,1,0:T(8,128)(2,1)S(1)} collective-permute-done((bf16[70,16,128]{2,1,0:T(8,128)(2,1)S(1)}, bf16[70,16,128]{2,1,0:T(8,128)(2,1)S(1)}, u32[]{:S(2)}, u32[]{:S(2)}) %collective-permute-start.19) | collective-permute-done | bytes 286752 | tf_op jit(solution)/shard_map/x/ppermute | solution.py:132
  39.5 3.7 %collective-permute-done.20 = bf16[70,16,128]{2,1,0:T(8,128)(2,1)S(1)} collective-permute-done((bf16[70,16,128]{2,1,0:T(8,128)(2,1)S(1)}, bf16[70,16,128]{2,1,0:T(8,128)(2,1)S(1)}, u32[]{:S(2)}, u32[]{:S(2)}) %collective-permute-start.20) | collective-permute-done | bytes 286752 | tf_op jit(solution)/shard_map/x/ppermute | solution.py:132
  43.3 0.3 collective-permute-done.21
  44.0 3.2 %shard_map.76 = (bf16[8,70,16,128]{3,2,1,0:T(8,128)(2,1)S(1)}, bf16[8,70,16,128]{3,2,1,0:T(8,128)(2,1)S(1)}) custom-call(s32[140]{0:T(256)S(1)} %pad_add_fusion.pos_ref, s32[8]{0:T(128)S(1)} %fusion.24.chip_ref, bf16[65,128,128]{2,1,0:T(8,128)(2,1)S(1)} %constant_dynamic-update-slice_fusion.acts_ref, bf16[128,896]{1,0:T(8,128)(2,1)S(1)} %copy-done), custom_call_target="tpu_custom_call" | custom-call | flops 587202560 | bytes 6947408 | tf_op jit(solution)/shard_map/pallas_call | solution.py:105
  47.2 0.6 collective-permute-start.8
  47.7 0.5 collective-permute-done.22.w1_ref
  48.2 3.6 %shard_map.78 = (bf16[4,128,512]{2,1,0:T(8,128)(2,1)S(1)}, bf16[4,128,512]{2,1,0:T(8,128)(2,1)S(1)}, bf16[2,128,512]{2,1,0:T(8,128)(2,1)S(1)}, bf16[2,128,512]{2,1,0:T(8,128)(2,1)S(1)}, bf16[4,128,512]{2,1,0:T(8,128)(2,1)S(1)}) custom-call(s32[140]{0:T(256)S(1)} %pad_add_fusion.pos_ref, s32[8]{0:T(128)S(1)} %fusion.24.chip_ref, ...), custom_call_target="tpu_custom_call" | custom-call | flops 587202560 | bytes 6914640 | tf_op jit(solution)/shard_map/pallas_call | solution.py:105
  51.8 0.8 collective-permute-start.25
  52.7 2.6 %collective-permute-start.23 = (bf16[2,128,512]{2,1,0:T(8,128)(2,1)S(1)}, bf16[2,128,512]{2,1,0:T(8,128)(2,1)S(1)}, u32[]{:S(2)}, u32[]{:S(2)}) collective-permute-start(bf16[2,128,512]{2,1,0:T(8,128)(2,1)S(1)} %get-tuple-element.23), channel_id=1, source_target_pairs={{0,1},{1,2},{2,3},{3,0},{4,5},{5,6},{6,7},{7,4},{8,9},{9,10},{10,1... | collective-permute-start | bytes 786440 | tf_op jit(solution)/shard_map/y/ppermute | solution.py:127
  55.3 0.6 fusion.6
  55.9 2.7 %collective-permute-start.11 = (bf16[35,16,128]{2,1,0:T(8,128)(2,1)S(1)}, bf16[35,16,128]{2,1,0:T(8,128)(2,1)S(1)}, u32[]{:S(2)}, u32[]{:S(2)}) collective-permute-start(bf16[35,16,128]{2,1,0:T(8,128)(2,1)S(1)} %get-tuple-element.48), channel_id=1, source_target_pairs={{0,96},{16,112},{32,0},{48,16},{64,32},{80,48},{96,64},{112,80},{1... | collective-permute-start | bytes 430088 | tf_op jit(solution)/shard_map/x/ppermute | solution.py:132
  58.7 2.6 %collective-permute-done.11 = bf16[35,16,128]{2,1,0:T(8,128)(2,1)S(1)} collective-permute-done((bf16[35,16,128]{2,1,0:T(8,128)(2,1)S(1)}, bf16[35,16,128]{2,1,0:T(8,128)(2,1)S(1)}, u32[]{:S(2)}, u32[]{:S(2)}) %collective-permute-start.11) | collective-permute-done | bytes 143392 | tf_op jit(solution)/shard_map/x/ppermute | solution.py:132
  61.4 3.8 %collective-permute-start.12 = (bf16[70,16,128]{2,1,0:T(8,128)(2,1)S(1)}, bf16[70,16,128]{2,1,0:T(8,128)(2,1)S(1)}, u32[]{:S(2)}, u32[]{:S(2)}) collective-permute-start(bf16[70,16,128]{2,1,0:T(8,128)(2,1)S(1)} %pad_maximum_fusion.4), channel_id=1, source_target_pairs={{0,96},{16,112},{32,0},{48,16},{64,32},{80,48},{96,64},{112,80},{1... | collective-permute-start | bytes 860168 | tf_op jit(solution)/shard_map/x/ppermute | solution.py:132
  65.6 4.5 %collective-permute-done.12 = bf16[70,16,128]{2,1,0:T(8,128)(2,1)S(1)} collective-permute-done((bf16[70,16,128]{2,1,0:T(8,128)(2,1)S(1)}, bf16[70,16,128]{2,1,0:T(8,128)(2,1)S(1)}, u32[]{:S(2)}, u32[]{:S(2)}) %collective-permute-start.12) | collective-permute-done | bytes 286752 | tf_op jit(solution)/shard_map/x/ppermute | solution.py:132
  70.1 3.6 %collective-permute-done.10 = bf16[70,16,128]{2,1,0:T(8,128)(2,1)S(1)} collective-permute-done((bf16[70,16,128]{2,1,0:T(8,128)(2,1)S(1)}, bf16[70,16,128]{2,1,0:T(8,128)(2,1)S(1)}, u32[]{:S(2)}, u32[]{:S(2)}) %collective-permute-start.10) | collective-permute-done | bytes 286752 | tf_op jit(solution)/shard_map/x/ppermute | solution.py:132
  73.6 0.2 fusion.1
  73.9 0.2 collective-permute-start.32
  74.2 0.7 collective-permute-start.24
  74.9 9.5 %collective-permute-start.13 = (bf16[70,16,128]{2,1,0:T(8,128)(2,1)S(1)}, bf16[70,16,128]{2,1,0:T(8,128)(2,1)S(1)}, u32[]{:S(2)}, u32[]{:S(2)}) collective-permute-start(bf16[70,16,128]{2,1,0:T(8,128)(2,1)S(1)} %fusion.1), channel_id=1, source_target_pairs={{0,128},{16,144},{32,160},{48,176},{64,192},{80,208},{96,224},{112... | collective-permute-start | bytes 860168 | tf_op jit(solution)/shard_map/z_hi/ppermute | solution.py:137
  84.4 2.2 %collective-permute-start.30 = (bf16[35,16,128]{2,1,0:T(8,128)(2,1)S(1)}, bf16[35,16,128]{2,1,0:T(8,128)(2,1)S(1)}, u32[]{:S(2)}, u32[]{:S(2)}) collective-permute-start(bf16[35,16,128]{2,1,0:T(8,128)(2,1)S(1)} %get-tuple-element.45), channel_id=1, source_target_pairs={{0,32},{16,48},{32,64},{48,80},{64,96},{80,112},{96,0},{112,16},{1... | collective-permute-start | bytes 430088 | tf_op jit(solution)/shard_map/x/ppermute | solution.py:132
  86.7 1.4 %collective-permute-start.33 = (bf16[70,16,128]{2,1,0:T(8,128)(2,1)S(1)}, bf16[70,16,128]{2,1,0:T(8,128)(2,1)S(1)}, u32[]{:S(2)}, u32[]{:S(2)}) collective-permute-start(bf16[70,16,128]{2,1,0:T(8,128)(2,1)S(1)} %pad_maximum_fusion.6), channel_id=1, source_target_pairs={{0,96},{16,112},{32,0},{48,16},{64,32},{80,48},{96,64},{112,80},{1... | collective-permute-start | bytes 860168 | tf_op jit(solution)/shard_map/x/ppermute | solution.py:132
  88.1 2.9 %collective-permute-done.30 = bf16[35,16,128]{2,1,0:T(8,128)(2,1)S(1)} collective-permute-done((bf16[35,16,128]{2,1,0:T(8,128)(2,1)S(1)}, bf16[35,16,128]{2,1,0:T(8,128)(2,1)S(1)}, u32[]{:S(2)}, u32[]{:S(2)}) %collective-permute-start.30) | collective-permute-done | bytes 143392 | tf_op jit(solution)/shard_map/x/ppermute | solution.py:132
  91.1 2.3 %collective-permute-start.31 = (bf16[70,16,128]{2,1,0:T(8,128)(2,1)S(1)}, bf16[70,16,128]{2,1,0:T(8,128)(2,1)S(1)}, u32[]{:S(2)}, u32[]{:S(2)}) collective-permute-start(bf16[70,16,128]{2,1,0:T(8,128)(2,1)S(1)} %pad_maximum_fusion.5), channel_id=1, source_target_pairs={{0,32},{16,48},{32,64},{48,80},{64,96},{80,112},{96,0},{112,16},{1... | collective-permute-start | bytes 860168 | tf_op jit(solution)/shard_map/x/ppermute | solution.py:132
  93.4 0.2 fusion.29
  93.7 6.7 %collective-permute-start.29 = (bf16[128,512]{1,0:T(8,128)(2,1)S(1)}, bf16[128,512]{1,0:T(8,128)(2,1)S(1)}, u32[]{:S(2)}, u32[]{:S(2)}) collective-permute-start(bf16[128,512]{1,0:T(8,128)(2,1)S(1)} %get-tuple-element.43), channel_id=1, source_target_pairs={{0,4},{1,5},{2,6},{3,7},{4,8},{5,9},{6,10},{7,11},{8,12},{9,13},{1... | collective-permute-start | bytes 393224 | tf_op jit(solution)/shard_map/z_lo/ppermute | solution.py:122
  100.4 1.3 %collective-permute-start.28 = (bf16[128,512]{1,0:T(8,128)(2,1)S(1)}, bf16[128,512]{1,0:T(8,128)(2,1)S(1)}, u32[]{:S(2)}, u32[]{:S(2)}) collective-permute-start(bf16[128,512]{1,0:T(8,128)(2,1)S(1)} %get-tuple-element.44), channel_id=1, source_target_pairs={{0,8},{1,9},{2,10},{3,11},{4,12},{5,13},{6,14},{7,15},{8,0},{9,1},... | collective-permute-start | bytes 393224 | tf_op jit(solution)/shard_map/z_lo/ppermute | solution.py:122
  101.8 2.9 %collective-permute-start.27 = (bf16[128,512]{1,0:T(8,128)(2,1)S(1)}, bf16[128,512]{1,0:T(8,128)(2,1)S(1)}, u32[]{:S(2)}, u32[]{:S(2)}) collective-permute-start(bf16[128,512]{1,0:T(8,128)(2,1)S(1)} %get-tuple-element.42), channel_id=1, source_target_pairs={{0,12},{1,13},{2,14},{3,15},{4,0},{5,1},{6,2},{7,3},{8,4},{9,5},{1... | collective-permute-start | bytes 393224 | tf_op jit(solution)/shard_map/z_lo/ppermute | solution.py:122
  104.7 0.1 convert_add_fusion.2
  105.0 3.6 %shard_map.77 = bf16[128,896]{1,0:T(8,128)(2,1)} custom-call(s32[140]{0:T(256)S(1)} %pad_add_fusion.pos_ref, s32[8]{0:T(128)S(1)} %fusion.24.chip_ref, bf16[65,128,128]{2,1,0:T(8,128)(2,1)S(1)} %constant_dynamic-update-slice_fusion.acts_ref, bf16[8,70,16,128]{3,2,1,0:T(8,128)(2,1)S(1)} %bitcast_dynamic-update-slice_fusion.w0_ref, ...), custom_call_target="tpu_custom_call" | custom-call | flops 587202560 | bytes 6947408 | tf_op jit(solution)/shard_map/pallas_call | solution.py:105
  108.6 0.7 add_convert_fusion.12
  109.3 0.8 maximum_select_fusion
  (86 shorter events, 2.7 us)
Async XLA Ops:
  1.8 10.9 %collective-permute-start.2 = (bf16[4,128,128]{2,1,0:T(8,128)(2,1)S(1)}, bf16[4,128,128]{2,1,0:T(8,128)(2,1)S(1)}, u32[]{:S(2)}, u32[]{:S(2)}) collective-permute-start(bf16[4,128,128]{2,1,0:T(8,128)(2,1)S(1)} %bitcast.76), channel_id=1, source_target_pairs={{0,12},{1,13},{2,14},{3,15},{4,0},{5,1},{6,2},{7,3},{8,4},{9,5},{1... | collective-permute-start | bytes 393224 | tf_op jit(solution)/shard_map/z_lo/ppermute | solution.py:122
  6.5 11.6 %collective-permute-start.1 = (bf16[4,128,128]{2,1,0:T(8,128)(2,1)S(1)}, bf16[4,128,128]{2,1,0:T(8,128)(2,1)S(1)}, u32[]{:S(2)}, u32[]{:S(2)}) collective-permute-start(bf16[4,128,128]{2,1,0:T(8,128)(2,1)S(1)} %bitcast.77), channel_id=1, source_target_pairs={{0,8},{1,9},{2,10},{3,11},{4,12},{5,13},{6,14},{7,15},{8,0},{9,1},... | collective-permute-start | bytes 393224 | tf_op jit(solution)/shard_map/z_lo/ppermute | solution.py:122
  6.5 11.6 %collective-permute-start = (bf16[4,128,128]{2,1,0:T(8,128)(2,1)S(1)}, bf16[4,128,128]{2,1,0:T(8,128)(2,1)S(1)}, u32[]{:S(2)}, u32[]{:S(2)}) collective-permute-start(bf16[4,128,128]{2,1,0:T(8,128)(2,1)S(1)} %bitcast.78), channel_id=1, source_target_pairs={{0,4},{1,5},{2,6},{3,7},{4,8},{5,9},{6,10},{7,11},{8,12},{9,13},{1... | collective-permute-start | bytes 393224 | tf_op jit(solution)/shard_map/z_lo/ppermute | solution.py:122
  7.2 2.1 %collective-permute-start.3 = (bf16[7,20,8,128]{3,2,1,0:T(8,128)(2,1)}, bf16[7,20,8,128]{3,2,1,0:T(8,128)(2,1)S(1)}, u32[]{:S(2)}, u32[]{:S(2)}) collective-permute-start(bf16[7,20,8,128]{3,2,1,0:T(8,128)(2,1)} %param.7), channel_id=1, source_target_pairs={{0,16},{16,0},{32,48},{48,32},{64,80},{80,64},{96,112},{112,96},{1... | collective-permute-start | bytes 860168 | tf_op jit(solution)/shard_map/core/ppermute | solution.py:142
  9.4 13.6 %collective-permute-start.14 = (bf16[70,16,128]{2,1,0:T(8,128)(2,1)S(1)}, bf16[70,16,128]{2,1,0:T(8,128)(2,1)S(1)}, u32[]{:S(2)}, u32[]{:S(2)}) collective-permute-start(bf16[70,16,128]{2,1,0:T(8,128)(2,1)S(1)} %maximum_select_fusion.1), channel_id=1, source_target_pairs={{0,32},{16,48},{32,64},{48,80},{64,96},{80,112},{96,0},{112,16},{1... | collective-permute-start | bytes 860168 | tf_op jit(solution)/shard_map/x/ppermute | solution.py:132
  11.0 9.5 %collective-permute-start.16 = (bf16[70,16,128]{2,1,0:T(8,128)(2,1)S(1)}, bf16[70,16,128]{2,1,0:T(8,128)(2,1)S(1)}, u32[]{:S(2)}, u32[]{:S(2)}) collective-permute-start(bf16[70,16,128]{2,1,0:T(8,128)(2,1)S(1)} %maximum_select_fusion.1), channel_id=1, source_target_pairs={{0,96},{16,112},{32,0},{48,16},{64,32},{80,48},{96,64},{112,80},{1... | collective-permute-start | bytes 860168 | tf_op jit(solution)/shard_map/x/ppermute | solution.py:132
  12.7 14.6 %collective-permute-start.18 = (bf16[70,16,128]{2,1,0:T(8,128)(2,1)S(1)}, bf16[70,16,128]{2,1,0:T(8,128)(2,1)S(1)}, u32[]{:S(2)}, u32[]{:S(2)}) collective-permute-start(bf16[70,16,128]{2,1,0:T(8,128)(2,1)S(1)} %maximum_select_fusion.1), channel_id=1, source_target_pairs={{0,128},{16,144},{32,160},{48,176},{64,192},{80,208},{96,224},{112... | collective-permute-start | bytes 860168 | tf_op jit(solution)/shard_map/z_hi/ppermute | solution.py:137
  18.2 16.1 %collective-permute-start.4 = (bf16[16,128,128]{2,1,0:T(8,128)(2,1)S(1)}, bf16[16,128,128]{2,1,0:T(8,128)(2,1)S(1)}, u32[]{:S(2)}, u32[]{:S(2)}) collective-permute-start(bf16[16,128,128]{2,1,0:T(8,128)(2,1)S(1)} %pad_maximum_fusion), channel_id=1, source_target_pairs={{0,1},{1,2},{2,3},{3,0},{4,5},{5,6},{6,7},{7,4},{8,9},{9,10},{10,1... | collective-permute-start | bytes 1572872 | tf_op jit(solution)/shard_map/y/ppermute | solution.py:127
  18.5 16.1 %collective-permute-start.6 = (bf16[16,128,128]{2,1,0:T(8,128)(2,1)S(1)}, bf16[16,128,128]{2,1,0:T(8,128)(2,1)S(1)}, u32[]{:S(2)}, u32[]{:S(2)}) collective-permute-start(bf16[16,128,128]{2,1,0:T(8,128)(2,1)S(1)} %pad_maximum_fusion), channel_id=1, source_target_pairs={{0,3},{1,0},{2,1},{3,2},{4,7},{5,4},{6,5},{7,6},{8,11},{9,8},{10,9... | collective-permute-start | bytes 1572872 | tf_op jit(solution)/shard_map/y/ppermute | solution.py:127
  20.5 9.4 %collective-permute-start.17 = (bf16[35,16,128]{2,1,0:T(8,128)(2,1)S(1)}, bf16[35,16,128]{2,1,0:T(8,128)(2,1)S(1)}, u32[]{:S(2)}, u32[]{:S(2)}) collective-permute-start(bf16[35,16,128]{2,1,0:T(8,128)(2,1)S(1)} %slice.232), channel_id=1, source_target_pairs={{0,96},{16,112},{32,0},{48,16},{64,32},{80,48},{96,64},{112,80},{1... | collective-permute-start | bytes 430088 | tf_op jit(solution)/shard_map/x/ppermute | solution.py:132
  23.0 9.7 %collective-permute-start.15 = (bf16[35,16,128]{2,1,0:T(8,128)(2,1)S(1)}, bf16[35,16,128]{2,1,0:T(8,128)(2,1)S(1)}, u32[]{:S(2)}, u32[]{:S(2)}) collective-permute-start(bf16[35,16,128]{2,1,0:T(8,128)(2,1)S(1)} %slice.231), channel_id=1, source_target_pairs={{0,32},{16,48},{32,64},{48,80},{64,96},{80,112},{96,0},{112,16},{1... | collective-permute-start | bytes 430088 | tf_op jit(solution)/shard_map/x/ppermute | solution.py:132
  27.3 12.2 %collective-permute-start.19 = (bf16[70,16,128]{2,1,0:T(8,128)(2,1)S(1)}, bf16[70,16,128]{2,1,0:T(8,128)(2,1)S(1)}, u32[]{:S(2)}, u32[]{:S(2)}) collective-permute-start(bf16[70,16,128]{2,1,0:T(8,128)(2,1)S(1)} %collective-permute-done.18), channel_id=1, source_target_pairs={{0,32},{16,48},{32,64},{48,80},{64,96},{80,112},{96,0},{112,16},{1... | collective-permute-start | bytes 860168 | tf_op jit(solution)/shard_map/x/ppermute | solution.py:132
  29.9 13.4 %collective-permute-start.20 = (bf16[70,16,128]{2,1,0:T(8,128)(2,1)S(1)}, bf16[70,16,128]{2,1,0:T(8,128)(2,1)S(1)}, u32[]{:S(2)}, u32[]{:S(2)}) collective-permute-start(bf16[70,16,128]{2,1,0:T(8,128)(2,1)S(1)} %collective-permute-done.18), channel_id=1, source_target_pairs={{0,64},{16,80},{32,96},{48,112},{64,0},{80,16},{96,32},{112,48},{1... | collective-permute-start | bytes 860168 | tf_op jit(solution)/shard_map/x/ppermute | solution.py:132
  32.7 10.9 %collective-permute-start.21 = (bf16[70,16,128]{2,1,0:T(8,128)(2,1)S(1)}, bf16[70,16,128]{2,1,0:T(8,128)(2,1)S(1)}, u32[]{:S(2)}, u32[]{:S(2)}) collective-permute-start(bf16[70,16,128]{2,1,0:T(8,128)(2,1)S(1)} %collective-permute-done.18), channel_id=1, source_target_pairs={{0,96},{16,112},{32,0},{48,16},{64,32},{80,48},{96,64},{112,80},{1... | collective-permute-start | bytes 860168 | tf_op jit(solution)/shard_map/x/ppermute | solution.py:132
  34.3 9.4 %collective-permute-start.5 = (bf16[8,128,128]{2,1,0:T(8,128)(2,1)S(1)}, bf16[8,128,128]{2,1,0:T(8,128)(2,1)S(1)}, u32[]{:S(2)}, u32[]{:S(2)}) collective-permute-start(bf16[8,128,128]{2,1,0:T(8,128)(2,1)S(1)} %slice.219), channel_id=1, source_target_pairs={{0,1},{1,2},{2,3},{3,0},{4,5},{5,6},{6,7},{7,4},{8,9},{9,10},{10,1... | collective-permute-start | bytes 786440 | tf_op jit(solution)/shard_map/y/ppermute | solution.py:127
  34.7 9.3 %copy-start = (bf16[128,896]{1,0:T(8,128)(2,1)S(1)}, bf16[128,896]{1,0:T(8,128)(2,1)}, u32[]{:S(2)}) copy-start(bf16[128,896]{1,0:T(8,128)(2,1)} %up_ref.3) | copy-start | bytes 688132
  34.7 9.2 %collective-permute-start.7 = (bf16[8,128,128]{2,1,0:T(8,128)(2,1)S(1)}, bf16[8,128,128]{2,1,0:T(8,128)(2,1)S(1)}, u32[]{:S(2)}, u32[]{:S(2)}) collective-permute-start(bf16[8,128,128]{2,1,0:T(8,128)(2,1)S(1)} %slice.220), channel_id=1, source_target_pairs={{0,3},{1,0},{2,1},{3,2},{4,7},{5,4},{6,5},{7,6},{8,11},{9,8},{10,9... | collective-permute-start | bytes 786440 | tf_op jit(solution)/shard_map/y/ppermute | solution.py:127
  43.7 4.5 %collective-permute-start.22 = (bf16[8,70,16,128]{3,2,1,0:T(8,128)(2,1)S(1)}, bf16[8,70,16,128]{3,2,1,0:T(8,128)(2,1)S(1)}, u32[]{:S(2)}, u32[]{:S(2)}) collective-permute-start(bf16[8,70,16,128]{3,2,1,0:T(8,128)(2,1)S(1)} %bitcast_dynamic-update-slice_fusion.w0_ref), channel_id=1, source_target_pairs={{0,16},{16,0},{32,48},{48,32},{64,80},{80,64},{96,112},{112,96},{1... | collective-permute-start | bytes 6881288 | tf_op jit(solution)/shard_map/core/ppermute | solution.py:142
  47.2 8.1 %collective-permute-start.8 = (bf16[8,70,16,128]{3,2,1,0:T(8,128)(2,1)S(1)}, bf16[8,70,16,128]{3,2,1,0:T(8,128)(2,1)S(1)}, u32[]{:S(2)}, u32[]{:S(2)}) collective-permute-start(bf16[8,70,16,128]{3,2,1,0:T(8,128)(2,1)S(1)} %get-tuple-element.19), channel_id=1, source_target_pairs={{0,16},{16,0},{32,48},{48,32},{64,80},{80,64},{96,112},{112,96},{1... | collective-permute-start | bytes 6881288 | tf_op jit(solution)/shard_map/core/ppermute | solution.py:142
  51.8 13.5 %collective-permute-start.25 = (bf16[2,128,512]{2,1,0:T(8,128)(2,1)S(1)}, bf16[2,128,512]{2,1,0:T(8,128)(2,1)S(1)}, u32[]{:S(2)}, u32[]{:S(2)}) collective-permute-start(bf16[2,128,512]{2,1,0:T(8,128)(2,1)S(1)} %get-tuple-element.25), channel_id=1, source_target_pairs={{0,3},{1,0},{2,1},{3,2},{4,7},{5,4},{6,5},{7,6},{8,11},{9,8},{10,9... | collective-permute-start | bytes 786440 | tf_op jit(solution)/shard_map/y/ppermute | solution.py:127
  52.7 21.3 %collective-permute-start.23 = (bf16[2,128,512]{2,1,0:T(8,128)(2,1)S(1)}, bf16[2,128,512]{2,1,0:T(8,128)(2,1)S(1)}, u32[]{:S(2)}, u32[]{:S(2)}) collective-permute-start(bf16[2,128,512]{2,1,0:T(8,128)(2,1)S(1)} %get-tuple-element.23), channel_id=1, source_target_pairs={{0,1},{1,2},{2,3},{3,0},{4,5},{5,6},{6,7},{7,4},{8,9},{9,10},{10,1... | collective-permute-start | bytes 786440 | tf_op jit(solution)/shard_map/y/ppermute | solution.py:127
  55.9 5.4 %collective-permute-start.11 = (bf16[35,16,128]{2,1,0:T(8,128)(2,1)S(1)}, bf16[35,16,128]{2,1,0:T(8,128)(2,1)S(1)}, u32[]{:S(2)}, u32[]{:S(2)}) collective-permute-start(bf16[35,16,128]{2,1,0:T(8,128)(2,1)S(1)} %get-tuple-element.48), channel_id=1, source_target_pairs={{0,96},{16,112},{32,0},{48,16},{64,32},{80,48},{96,64},{112,80},{1... | collective-permute-start | bytes 430088 | tf_op jit(solution)/shard_map/x/ppermute | solution.py:132
  58.6 6.6 %collective-permute-start.9 = (bf16[35,16,128]{2,1,0:T(8,128)(2,1)S(1)}, bf16[35,16,128]{2,1,0:T(8,128)(2,1)S(1)}, u32[]{:S(2)}, u32[]{:S(2)}) collective-permute-start(bf16[35,16,128]{2,1,0:T(8,128)(2,1)S(1)} %get-tuple-element.47), channel_id=1, source_target_pairs={{0,32},{16,48},{32,64},{48,80},{64,96},{80,112},{96,0},{112,16},{1... | collective-permute-start | bytes 430088 | tf_op jit(solution)/shard_map/x/ppermute | solution.py:132
  61.4 8.7 %collective-permute-start.12 = (bf16[70,16,128]{2,1,0:T(8,128)(2,1)S(1)}, bf16[70,16,128]{2,1,0:T(8,128)(2,1)S(1)}, u32[]{:S(2)}, u32[]{:S(2)}) collective-permute-start(bf16[70,16,128]{2,1,0:T(8,128)(2,1)S(1)} %pad_maximum_fusion.4), channel_id=1, source_target_pairs={{0,96},{16,112},{32,0},{48,16},{64,32},{80,48},{96,64},{112,80},{1... | collective-permute-start | bytes 860168 | tf_op jit(solution)/shard_map/x/ppermute | solution.py:132
  65.3 8.4 %collective-permute-start.10 = (bf16[70,16,128]{2,1,0:T(8,128)(2,1)S(1)}, bf16[70,16,128]{2,1,0:T(8,128)(2,1)S(1)}, u32[]{:S(2)}, u32[]{:S(2)}) collective-permute-start(bf16[70,16,128]{2,1,0:T(8,128)(2,1)S(1)} %pad_maximum_fusion.3), channel_id=1, source_target_pairs={{0,32},{16,48},{32,64},{48,80},{64,96},{80,112},{96,0},{112,16},{1... | collective-permute-start | bytes 860168 | tf_op jit(solution)/shard_map/x/ppermute | solution.py:132
  65.5 28.0 %collective-permute-start.26 = (bf16[4,128,512]{2,1,0:T(8,128)(2,1)S(1)}, bf16[4,128,512]{2,1,0:T(8,128)(2,1)S(1)}, u32[]{:S(2)}, u32[]{:S(2)}) collective-permute-start(bf16[4,128,512]{2,1,0:T(8,128)(2,1)S(1)} %pad_maximum_fusion.2), channel_id=1, source_target_pairs={{0,3},{1,0},{2,1},{3,2},{4,7},{5,4},{6,5},{7,6},{8,11},{9,8},{10,9... | collective-permute-start | bytes 1572872 | tf_op jit(solution)/shard_map/y/ppermute | solution.py:127
  73.9 12.8 %collective-permute-start.32 = (bf16[35,16,128]{2,1,0:T(8,128)(2,1)S(1)}, bf16[35,16,128]{2,1,0:T(8,128)(2,1)S(1)}, u32[]{:S(2)}, u32[]{:S(2)}) collective-permute-start(bf16[35,16,128]{2,1,0:T(8,128)(2,1)S(1)} %get-tuple-element.46), channel_id=1, source_target_pairs={{0,96},{16,112},{32,0},{48,16},{64,32},{80,48},{96,64},{112,80},{1... | collective-permute-start | bytes 430088 | tf_op jit(solution)/shard_map/x/ppermute | solution.py:132
  74.2 19.3 %collective-permute-start.24 = (bf16[4,128,512]{2,1,0:T(8,128)(2,1)S(1)}, bf16[4,128,512]{2,1,0:T(8,128)(2,1)S(1)}, u32[]{:S(2)}, u32[]{:S(2)}) collective-permute-start(bf16[4,128,512]{2,1,0:T(8,128)(2,1)S(1)} %pad_maximum_fusion.1), channel_id=1, source_target_pairs={{0,1},{1,2},{2,3},{3,0},{4,5},{5,6},{6,7},{7,4},{8,9},{9,10},{10,1... | collective-permute-start | bytes 1572872 | tf_op jit(solution)/shard_map/y/ppermute | solution.py:127
  74.9 26.9 %collective-permute-start.13 = (bf16[70,16,128]{2,1,0:T(8,128)(2,1)S(1)}, bf16[70,16,128]{2,1,0:T(8,128)(2,1)S(1)}, u32[]{:S(2)}, u32[]{:S(2)}) collective-permute-start(bf16[70,16,128]{2,1,0:T(8,128)(2,1)S(1)} %fusion.1), channel_id=1, source_target_pairs={{0,128},{16,144},{32,160},{48,176},{64,192},{80,208},{96,224},{112... | collective-permute-start | bytes 860168 | tf_op jit(solution)/shard_map/z_hi/ppermute | solution.py:137
  84.4 6.6 %collective-permute-start.30 = (bf16[35,16,128]{2,1,0:T(8,128)(2,1)S(1)}, bf16[35,16,128]{2,1,0:T(8,128)(2,1)S(1)}, u32[]{:S(2)}, u32[]{:S(2)}) collective-permute-start(bf16[35,16,128]{2,1,0:T(8,128)(2,1)S(1)} %get-tuple-element.45), channel_id=1, source_target_pairs={{0,32},{16,48},{32,64},{48,80},{64,96},{80,112},{96,0},{112,16},{1... | collective-permute-start | bytes 430088 | tf_op jit(solution)/shard_map/x/ppermute | solution.py:132
  86.7 18.0 %collective-permute-start.33 = (bf16[70,16,128]{2,1,0:T(8,128)(2,1)S(1)}, bf16[70,16,128]{2,1,0:T(8,128)(2,1)S(1)}, u32[]{:S(2)}, u32[]{:S(2)}) collective-permute-start(bf16[70,16,128]{2,1,0:T(8,128)(2,1)S(1)} %pad_maximum_fusion.6), channel_id=1, source_target_pairs={{0,96},{16,112},{32,0},{48,16},{64,32},{80,48},{96,64},{112,80},{1... | collective-permute-start | bytes 860168 | tf_op jit(solution)/shard_map/x/ppermute | solution.py:132
  91.1 13.6 %collective-permute-start.31 = (bf16[70,16,128]{2,1,0:T(8,128)(2,1)S(1)}, bf16[70,16,128]{2,1,0:T(8,128)(2,1)S(1)}, u32[]{:S(2)}, u32[]{:S(2)}) collective-permute-start(bf16[70,16,128]{2,1,0:T(8,128)(2,1)S(1)} %pad_maximum_fusion.5), channel_id=1, source_target_pairs={{0,32},{16,48},{32,64},{48,80},{64,96},{80,112},{96,0},{112,16},{1... | collective-permute-start | bytes 860168 | tf_op jit(solution)/shard_map/x/ppermute | solution.py:132
  93.7 14.9 %collective-permute-start.29 = (bf16[128,512]{1,0:T(8,128)(2,1)S(1)}, bf16[128,512]{1,0:T(8,128)(2,1)S(1)}, u32[]{:S(2)}, u32[]{:S(2)}) collective-permute-start(bf16[128,512]{1,0:T(8,128)(2,1)S(1)} %get-tuple-element.43), channel_id=1, source_target_pairs={{0,4},{1,5},{2,6},{3,7},{4,8},{5,9},{6,10},{7,11},{8,12},{9,13},{1... | collective-permute-start | bytes 393224 | tf_op jit(solution)/shard_map/z_lo/ppermute | solution.py:122
  100.4 8.1 %collective-permute-start.28 = (bf16[128,512]{1,0:T(8,128)(2,1)S(1)}, bf16[128,512]{1,0:T(8,128)(2,1)S(1)}, u32[]{:S(2)}, u32[]{:S(2)}) collective-permute-start(bf16[128,512]{1,0:T(8,128)(2,1)S(1)} %get-tuple-element.44), channel_id=1, source_target_pairs={{0,8},{1,9},{2,10},{3,11},{4,12},{5,13},{6,14},{7,15},{8,0},{9,1},... | collective-permute-start | bytes 393224 | tf_op jit(solution)/shard_map/z_lo/ppermute | solution.py:122
  101.8 6.8 %collective-permute-start.27 = (bf16[128,512]{1,0:T(8,128)(2,1)S(1)}, bf16[128,512]{1,0:T(8,128)(2,1)S(1)}, u32[]{:S(2)}, u32[]{:S(2)}) collective-permute-start(bf16[128,512]{1,0:T(8,128)(2,1)S(1)} %get-tuple-element.42), channel_id=1, source_target_pairs={{0,12},{1,13},{2,14},{3,15},{4,0},{5,1},{6,2},{7,3},{8,4},{9,5},{1... | collective-permute-start | bytes 393224 | tf_op jit(solution)/shard_map/z_lo/ppermute | solution.py:122
  104.9 4.4 %collective-permute-start.34 = (f32[7,10,8,128]{3,2,1,0:T(8,128)S(1)}, f32[7,10,8,128]{3,2,1,0:T(8,128)S(1)}, u32[]{:S(2)}, u32[]{:S(2)}) collective-permute-start(f32[7,10,8,128]{3,2,1,0:T(8,128)S(1)} %get-tuple-element.41), channel_id=1, source_target_pairs={{0,16},{16,0},{32,48},{48,32},{64,80},{80,64},{96,112},{112,96},{1... | collective-permute-start | bytes 860168 | tf_op jit(solution)/shard_map/core/ppermute | solution.py:142
